TPU v7x, 32 devices: a whole 2x2x4 slice. The times are simulated.
32 devices in a mesh: dp: 16 (over z, y, x), tensor: 2 (over core).
Axes of the slice: x: 2, y: 2, z: 4, core: 2. Of those that a mesh axis runs over, the one named last changes fastest.
Arguments:
- input_rows: bfloat16 [32768, 768], P(('dp', 'tensor')), may hold values from -6 to 6
- first_values: bfloat16 [32768, 384], P('dp', 'tensor'), may hold values from -6 to 6
- doc_split: int32 [16], P('dp'), may hold values from 1024 to 2048, as said below
- gain_norm1: bfloat16 [768], replicated, may hold values from 0.5 to 1.5
- bias_norm1: bfloat16 [768], replicated, may hold values from -2 to 2
- w_query: bfloat16 [768, 768], P(None, 'tensor'), may hold values from -0.21875 to 0.21875
- bias_query: bfloat16 [768], P('tensor'), may hold values from -3 to 3
- w_key: bfloat16 [768, 768], P(None, 'tensor'), may hold values from -0.21875 to 0.21875
- w_value: bfloat16 [768, 384], P(None, 'tensor'), may hold values from -0.21875 to 0.21875
- bias_value: bfloat16 [384], P('tensor'), may hold values from -3 to 3
- w_out: bfloat16 [768, 768], P('tensor'), may hold values from -0.875 to 0.875
- bias_attn_out: bfloat16 [768], replicated, may hold values from -2 to 2
- gain_norm2: bfloat16 [768], replicated, may hold values from 0.5 to 1.5
- bias_norm2: bfloat16 [768], replicated, may hold values from -2 to 2
- w_up: bfloat16 [768, 3072], P(None, 'tensor'), may hold values from -0.21875 to 0.21875
- bias_up: bfloat16 [3072], P('tensor'), may hold values from -3 to 3
- w_down: bfloat16 [3072, 768], P('tensor'), may hold values from -0.109375 to 0.109375
- bias_down: bfloat16 [768], replicated, may hold values from -2 to 2
- cotangent: bfloat16 [32768, 768], P(('dp', 'tensor')), may hold values from -6 to 6
Outputs:
- output: bfloat16 [32768, 768], P(('dp', 'tensor'))
- grad_input: float32 [32768, 768], P(('dp', 'tensor'))
- grad_first_values: float32 [32768, 384], P('dp', 'tensor')
- grad_gain_norm1: float32 [768], replicated
- grad_bias_norm1: float32 [768], replicated
- grad_w_query: float32 [768, 768], P(None, 'tensor')
- grad_bias_query: float32 [768], P('tensor')
- grad_w_key: float32 [768, 768], P(None, 'tensor')
- grad_w_value: float32 [768, 384], P(None, 'tensor')
- grad_bias_value: float32 [384], P('tensor')
- grad_w_out: float32 [768, 768], P('tensor')
- grad_bias_attn_out: float32 [768], replicated
- grad_gain_norm2: float32 [768], replicated
- grad_bias_norm2: float32 [768], replicated
- grad_w_up: float32 [768, 3072], P(None, 'tensor')
- grad_bias_up: float32 [3072], P('tensor')
- grad_w_down: float32 [3072, 768], P('tensor')
- grad_bias_down: float32 [768], replicated
Inputs may be any that keep to these rules, and one draw needn't show every extreme that they name: `doc_split`: each entry is 1024 (the group holds two documents of 1024 tokens) or 2 * 1024 (one document of 2048 tokens); both occur in every draw.
All inputs are finite; a program needn't handle non-finite values.
Results may differ from a plain program's by a relative error of at most 0.012.
Values may be sent and summed in bfloat16 or wider, within the bound.
A program may use at most 256 MiB of HBM per device.

v0:
```python
from functools import partial

import jax
import jax.numpy as jnp
from jax import lax
from jax.sharding import PartitionSpec as P

HEAD_DIM = 64


norm_eps = 1e-05
masked_fill = -1000000000.0


def normalize(rows_in, norm_gain, norm_shift):
    center = jnp.mean(rows_in, axis=1, keepdims=True)
    centered = rows_in - center
    inverse = lax.rsqrt(jnp.mean(centered * centered, axis=1, keepdims=True) + norm_eps)
    normed = centered * inverse
    return (normed * norm_gain + norm_shift, normed, inverse)


def normalize_back(grad_rows, normed, inverse, norm_gain):
    scaled = grad_rows * norm_gain
    return inverse * (
        scaled
        - jnp.mean(scaled, axis=1, keepdims=True)
        - normed * jnp.mean(scaled * normed, axis=1, keepdims=True)
    )


def contract_rows(left_array, right_array):
    return lax.dot_general(
        left_array, right_array, (((0,), (0,)), ((), ())), preferred_element_type=jnp.float32
    )


def contract_cols(left_array, right_array):
    return lax.dot_general(
        left_array, right_array, (((1,), (1,)), ((), ())), preferred_element_type=jnp.float32
    )


def masked_scores(query_block, key_block, row_start, col_start):
    scores = jnp.einsum(
        "qhd,khd->hqk", query_block, key_block, preferred_element_type=jnp.float32
    ) * query_block.shape[2] ** (-0.5)
    row_ids = row_start + lax.broadcasted_iota(jnp.int32, scores.shape, 1)
    col_ids = col_start + lax.broadcasted_iota(jnp.int32, scores.shape, 2)
    return jnp.where(col_ids <= row_ids, scores, masked_fill)


def block_forward(query_block, key_block, value_block, row_start, col_start):
    scores = masked_scores(query_block, key_block, row_start, col_start)
    top_score = jnp.max(scores, axis=2, keepdims=True)
    weights_exp = jnp.exp(scores - top_score)
    denominator = jnp.sum(weights_exp, axis=2, keepdims=True)
    probabilities = (weights_exp / denominator).astype(jnp.bfloat16)
    attended = jnp.einsum(
        "hqk,khd->qhd", probabilities, value_block, preferred_element_type=jnp.float32
    )
    return (attended.astype(jnp.bfloat16), (top_score + jnp.log(denominator))[:, :, 0])


def block_backward(
    query_block, key_block, value_block, grad_block, lse_block, row_start, col_start
):
    scores = masked_scores(query_block, key_block, row_start, col_start)
    probabilities = jnp.exp(scores - lse_block[:, :, None])
    grad_probs = jnp.einsum(
        "qhd,khd->hqk", grad_block, value_block, preferred_element_type=jnp.float32
    )
    inner_sum = jnp.sum(probabilities * grad_probs, axis=2, keepdims=True)
    grad_scores = (probabilities * (grad_probs - inner_sum)).astype(jnp.bfloat16)
    key_scale = query_block.shape[2] ** (-0.5)
    grad_query = (
        jnp.einsum("hqk,khd->qhd", grad_scores, key_block, preferred_element_type=jnp.float32)
        * key_scale
    )
    grad_key = (
        jnp.einsum("hqk,qhd->khd", grad_scores, query_block, preferred_element_type=jnp.float32)
        * key_scale
    )
    grad_value = jnp.einsum(
        "hqk,qhd->khd",
        probabilities.astype(jnp.bfloat16),
        grad_block,
        preferred_element_type=jnp.float32,
    )
    return (grad_query, grad_key, grad_value)


def far_backward(query_block, key_block, value_block, grad_block, lse_block, row_start, half_rows):
    grad_query, grad_key, grad_value = block_backward(
        query_block,
        key_block[half_rows:],
        value_block[half_rows:],
        grad_block,
        lse_block,
        row_start,
        half_rows,
    )
    zero_rows = jnp.zeros((half_rows,) + grad_key.shape[1:], jnp.float32)
    return (
        grad_query,
        jnp.concatenate([zero_rows, grad_key]),
        jnp.concatenate([zero_rows, grad_value]),
    )


def attention_forward(queries, key_rows, values, two_docs):
    row_total = queries.shape[0]
    half_rows = row_total // 2
    block_rows = min(512, half_rows)
    out_parts = []
    lse_parts = []
    for row_start in range(0, row_total, block_rows):
        row_stop = row_start + block_rows
        query_block = queries[row_start:row_stop]
        near_call = partial(
            block_forward, query_block, key_rows[:row_stop], values[:row_stop], row_start, 0
        )
        if row_start >= half_rows:
            far_call = partial(
                block_forward,
                query_block,
                key_rows[half_rows:row_stop],
                values[half_rows:row_stop],
                row_start,
                half_rows,
            )
            attended, lse_block = lax.cond(two_docs, far_call, near_call)
        else:
            attended, lse_block = near_call()
        out_parts.append(attended)
        lse_parts.append(lse_block)
    return (jnp.concatenate(out_parts, axis=0), jnp.concatenate(lse_parts, axis=1))


def attention_backward(queries, key_rows, values, grad_out, lse_all, two_docs):
    row_total = queries.shape[0]
    half_rows = row_total // 2
    block_rows = min(512, half_rows)
    grad_keys = jnp.zeros(key_rows.shape, jnp.float32)
    grad_values = jnp.zeros(values.shape, jnp.float32)
    query_parts = []
    for row_start in range(0, row_total, block_rows):
        row_stop = row_start + block_rows
        query_block = queries[row_start:row_stop]
        grad_block = grad_out[row_start:row_stop]
        lse_block = lse_all[:, row_start:row_stop]
        near_call = partial(
            block_backward,
            query_block,
            key_rows[:row_stop],
            values[:row_stop],
            grad_block,
            lse_block,
            row_start,
            0,
        )
        if row_start >= half_rows:
            far_call = partial(
                far_backward,
                query_block,
                key_rows[:row_stop],
                values[:row_stop],
                grad_block,
                lse_block,
                row_start,
                half_rows,
            )
            grad_query, grad_key, grad_value = lax.cond(two_docs, far_call, near_call)
        else:
            grad_query, grad_key, grad_value = near_call()
        query_parts.append(grad_query)
        grad_keys = grad_keys.at[:row_stop].add(grad_key)
        grad_values = grad_values.at[:row_stop].add(grad_value)
    return (jnp.concatenate(query_parts, axis=0), grad_keys, grad_values)


def on_device(
    input_rows,
    first_values,
    doc_split,
    gain_norm1,
    bias_norm1,
    w_query,
    bias_query,
    w_key,
    w_value,
    bias_value,
    w_out,
    bias_attn_out,
    gain_norm2,
    bias_norm2,
    w_up,
    bias_up,
    w_down,
    bias_down,
    cotangent,
):
    residual_in = input_rows.astype(jnp.float32)
    ln_one, normed_one, inverse_one = normalize(residual_in, gain_norm1, bias_norm1)
    ln_one_low = ln_one.astype(jnp.bfloat16)
    ln_one_all = lax.all_gather(ln_one_low, "tensor", axis=0, tiled=True)
    group_rows = ln_one_all.shape[0]
    two_docs = doc_split[0] < group_rows
    head_shape = (group_rows, -1, HEAD_DIM)
    queries = (
        jnp.dot(ln_one_all, w_query, preferred_element_type=jnp.float32) + bias_query
    ).astype(jnp.bfloat16)
    key_rows = jnp.dot(ln_one_all, w_key, preferred_element_type=jnp.float32).astype(jnp.bfloat16)
    fresh_values = (
        jnp.dot(ln_one_all, w_value, preferred_element_type=jnp.float32) + bias_value
    ).astype(jnp.bfloat16)
    values = jnp.concatenate([fresh_values, first_values], axis=1)
    queries, key_rows, values = (
        queries.reshape(head_shape),
        key_rows.reshape(head_shape),
        values.reshape(head_shape),
    )
    attended, lse_all = attention_forward(queries, key_rows, values, two_docs)
    attended_flat = attended.reshape(group_rows, -1)
    attn_terms = jnp.dot(attended_flat, w_out, preferred_element_type=jnp.float32)
    middle = (
        residual_in
        + lax.psum_scatter(attn_terms, "tensor", scatter_dimension=0, tiled=True)
        + bias_attn_out
    )
    ln_two, normed_two, inverse_two = normalize(middle, gain_norm2, bias_norm2)
    ln_two_low = ln_two.astype(jnp.bfloat16)
    ln_two_all = lax.all_gather(ln_two_low, "tensor", axis=0, tiled=True)
    hidden = jnp.dot(ln_two_all, w_up, preferred_element_type=jnp.float32) + bias_up
    hidden, activated = (hidden, jax.nn.gelu(hidden, approximate=True).astype(jnp.bfloat16))
    mlp_terms = jnp.dot(activated, w_down, preferred_element_type=jnp.float32)
    output = (
        middle
        + lax.psum_scatter(
            mlp_terms.astype(jnp.bfloat16), "tensor", scatter_dimension=0, tiled=True
        ).astype(jnp.float32)
        + bias_down
    ).astype(jnp.bfloat16)
    cot_rows = cotangent.astype(jnp.float32)
    grad_mlp_all = lax.all_gather(cotangent, "tensor", axis=0, tiled=True)
    grad_w_down = contract_rows(activated, grad_mlp_all)
    grad_act = contract_cols(grad_mlp_all, w_down)
    gelu_back = jax.vjp(partial(jax.nn.gelu, approximate=True), hidden)[1]
    grad_hidden = gelu_back(grad_act)[0].astype(jnp.bfloat16)
    grad_w_up = contract_rows(ln_two_all, grad_hidden)
    grad_bias_up = jnp.sum(grad_hidden, axis=0, dtype=jnp.float32)
    grad_ln_two = lax.psum_scatter(
        contract_cols(grad_hidden, w_up), "tensor", scatter_dimension=0, tiled=True
    )
    grad_middle = cot_rows + normalize_back(grad_ln_two, normed_two, inverse_two, gain_norm2)
    grad_attn_low = grad_middle.astype(jnp.bfloat16)
    grad_attn_all = lax.all_gather(grad_attn_low, "tensor", axis=0, tiled=True)
    grad_w_out = contract_rows(attended_flat, grad_attn_all)
    grad_attended = contract_cols(grad_attn_all, w_out).astype(jnp.bfloat16).reshape(head_shape)
    grad_query, grad_keys, grad_values = attention_backward(
        queries, key_rows, values, grad_attended, lse_all, two_docs
    )
    fresh_heads = w_value.shape[1] // HEAD_DIM
    grad_query_low = grad_query.reshape(group_rows, -1).astype(jnp.bfloat16)
    grad_key_low = grad_keys.reshape(group_rows, -1).astype(jnp.bfloat16)
    grad_fresh_low = grad_values[:, :fresh_heads].reshape(group_rows, -1).astype(jnp.bfloat16)
    grad_first_values = grad_values[:, fresh_heads:].reshape(group_rows, -1)
    grad_w_query = contract_rows(ln_one_all, grad_query_low)
    grad_bias_query = jnp.sum(grad_query_low, axis=0, dtype=jnp.float32)
    grad_w_key = contract_rows(ln_one_all, grad_key_low)
    grad_w_value = contract_rows(ln_one_all, grad_fresh_low)
    grad_bias_value = jnp.sum(grad_fresh_low, axis=0, dtype=jnp.float32)
    grad_ln_terms = (
        contract_cols(grad_query_low, w_query)
        + contract_cols(grad_key_low, w_key)
        + contract_cols(grad_fresh_low, w_value)
    )
    grad_ln_one = lax.psum_scatter(grad_ln_terms, "tensor", scatter_dimension=0, tiled=True)
    grad_input = grad_middle + normalize_back(grad_ln_one, normed_one, inverse_one, gain_norm1)
    (
        grad_w_down,
        grad_w_up,
        grad_bias_up,
        grad_w_out,
        grad_w_query,
        grad_bias_query,
        grad_w_key,
        grad_w_value,
        grad_bias_value,
    ) = lax.psum(
        (
            grad_w_down,
            grad_w_up,
            grad_bias_up,
            grad_w_out,
            grad_w_query,
            grad_bias_query,
            grad_w_key,
            grad_w_value,
            grad_bias_value,
        ),
        "dp",
    )
    gain_one_grad, shift_one_grad, attn_bias_grad, gain_two_grad, shift_two_grad, down_bias_grad = (
        lax.psum(
            (
                jnp.sum(grad_ln_one * normed_one, axis=0),
                jnp.sum(grad_ln_one, axis=0),
                jnp.sum(grad_attn_low, axis=0, dtype=jnp.float32),
                jnp.sum(grad_ln_two * normed_two, axis=0),
                jnp.sum(grad_ln_two, axis=0),
                jnp.sum(cot_rows, axis=0),
            ),
            ("dp", "tensor"),
        )
    )
    return (
        output,
        grad_input,
        grad_first_values,
        gain_one_grad,
        shift_one_grad,
        grad_w_query,
        grad_bias_query,
        grad_w_key,
        grad_w_value,
        grad_bias_value,
        grad_w_out,
        attn_bias_grad,
        gain_two_grad,
        shift_two_grad,
        grad_w_up,
        grad_bias_up,
        grad_w_down,
        down_bias_grad,
    )


def solution(mesh):
    placed = (
        P(("dp", "tensor"), None),
        P("dp", "tensor"),
        P("dp"),
        P(),
        P(),
        P(None, "tensor"),
        P("tensor"),
        P(None, "tensor"),
        P(None, "tensor"),
        P("tensor"),
        P("tensor", None),
        P(),
        P(),
        P(),
        P(None, "tensor"),
        P("tensor"),
        P("tensor", None),
        P(),
        P(("dp", "tensor"), None),
    )
    return jax.shard_map(
        on_device,
        mesh=mesh,
        in_specs=placed,
        out_specs=(
            P(("dp", "tensor"), None),
            P(("dp", "tensor"), None),
            P("dp", "tensor"),
            P(),
            P(),
            P(None, "tensor"),
            P("tensor"),
            P(None, "tensor"),
            P(None, "tensor"),
            P("tensor"),
            P("tensor", None),
            P(),
            P(),
            P(),
            P(None, "tensor"),
            P("tensor"),
            P("tensor", None),
            P(),
        ),
        check_vma=False,
    )
```

profile of v0, /device:TPU:0, one launch (start us, length us, event | category | flops | bytes accessed | tf_op | source)
XLA Modules:
  0.0 897.2 jit_solution(7069621855671684989)
XLA Ops:
  13.2 3.2 fusion.84
  17.7 13.7 %all-gather.5.cloned.1.call-done = bf16[2048,768]{1,0:T(8,128)(2,1)} async-done(((bf16[1024,768]{1,0:T(8,128)(2,1)}), bf16[2048,768]{1,0:T(8,128)(2,1)}) %all-gather.5.cloned.1.call-update) | async-done | bytes 3145744 | tf_op jit(solution)/shard_map/all_gather | solution.py:206
  31.4 3.1 fusion.96
  44.3 12.2 %conditional.9 = (f32[6,512]{1,0:T(8,128)S(1)}, bf16[512,6,64]{0,2,1:T(8,128)(2,1)S(1)}) conditional(s32[]{:T(128)} %bitcast.28, (bf16[512,6,64]{0,2,1:T(8,128)(2,1)}, bf16[2048,6,64]{0,2,1:T(8,128)(2,1)S(1)}, bf16[2048,6,64]{0,2,1:T(8,128)(2,1)S(1)}) %tuple.178, (bf16[2048,384]{0,1:T(8,128)(2,1)S(1)}, bf16[512,6,64]{0,2,1:T(8,128)(2,1)}, ...), branch_computations={%region_12.15_spmd, %region_15.18_spmd} | conditional | flops 1705178624 | bytes 79536144
  44.6 3.8 fusion.22
  48.4 3.4 fusion.21
  51.9 4.5 fusion.25
  57.2 8.1 conditional.8
  77.3 3.3 fusion.111
  82.1 4.5 fusion.124
  87.4 47.6 %reduce-scatter.5.cloned.1.call-done = f32[1024,768]{1,0:T(8,128)} async-done(((f32[2048,768]{1,0:T(8,128)}), f32[1024,768]{1,0:T(8,128)}) %reduce-scatter.5.cloned.1.call-update) | async-done | bytes 3145744 | tf_op jit(solution)/shard_map/reduce_scatter | solution.py:228
  143.3 11.3 %all-gather.7.cloned.1.call-done = bf16[2048,768]{1,0:T(8,128)(2,1)} async-done(((bf16[1024,768]{1,0:T(8,128)(2,1)}), bf16[2048,768]{1,0:T(8,128)(2,1)}) %all-gather.7.cloned.1.call-update) | async-done | bytes 3145744 | tf_op jit(solution)/shard_map/all_gather | solution.py:233
  154.6 13.6 %multiply_convert_fusion.5 = (bf16[2048,1536]{1,0:T(8,128)(2,1)}, f32[2048,1536]{1,0:T(8,128)}) fusion(f32[1536]{0:T(1024)} %convert_element_type.219, bf16[2048,768]{1,0:T(8,128)(2,1)} %all-gather.7.cloned.1.call-done, bf16[768,1536]{1,0:T(8,128)(2,1)S(1)} %copy-done), kind=kOutput, calls=%fused_computation.117 | convolution fusion | flops 4863295488 | bytes 24385536 | tf_op jit(solution)/shard_map/dot_general | solution.py:234
  169.4 17.4 %convert_reduce_fusion = (f32[1536]{0:T(1024)}, bf16[2048,1536]{1,0:T(8,128)(2,1)S(1)}) fusion(f32[2048,1536]{1,0:T(8,128)} %get-tuple-element.336, f32[1536]{0:T(1024)} %convert_element_type.219, bf16[2048,768]{1,0:T(8,128)(2,1)} %all-gather.9.cloned.1.call-done, bf16[1536,768]{1,0:T(8,128)(2,1)} %param.63), kind=kOutput, calls=%fused_computation.113 | convolution fusion | flops 4904188416 | bytes 24391680 | tf_op jit(solution)/shard_map/dot_general | solution.py:39
  189.5 6.9 fusion.125
  196.7 9.0 %convolution_convert_fusion = bf16[2048,768]{1,0:T(8,128)(2,1)} fusion(bf16[2048,1536]{1,0:T(8,128)(2,1)} %get-tuple-element.335, bf16[1536,768]{1,0:T(8,128)(2,1)} %param.63), kind=kOutput, calls=%fused_computation.148 | convolution fusion | flops 4833411072 | bytes 11796480 | tf_op jit(solution)/shard_map/dot_general | solution.py:236
  205.8 6.5 reduce-scatter.9.cloned.1.call-done
  212.3 4.2 multiply_reduce_fusion.6
  216.5 10.6 %reduce-scatter.7.cloned.1.call-done = bf16[1024,768]{1,0:T(8,128)(2,1)} async-done(((bf16[2048,768]{1,0:T(8,128)(2,1)}), bf16[1024,768]{1,0:T(8,128)(2,1)}) %reduce-scatter.7.cloned.1.call-update) | async-done | bytes 1572880 | tf_op jit(solution)/shard_map/reduce_scatter | solution.py:239
  227.1 6.5 convert_reduce_fusion.3
  234.3 12.7 %all-gather.11.cloned.1.call-done = bf16[2048,768]{1,0:T(8,128)(2,1)} async-done(((bf16[1024,768]{1,0:T(8,128)(2,1)}), bf16[2048,768]{1,0:T(8,128)(2,1)}) %all-gather.11.cloned.1.call-update) | async-done | bytes 3145744 | tf_op jit(solution)/shard_map/all_gather | solution.py:257
  247.0 3.5 convolution_convert_fusion.1
  250.7 4.0 fusion.103
  254.8 4.0 multiply_reduce_fusion.5
  258.8 6.4 multiply_convert_fusion.6
  265.2 3.4 fusion.108
  268.6 3.8 fusion.106
  272.9 6.8 multiply_reduce_fusion.4
  284.1 16.0 %conditional.20 = (bf16[512,6,64]{0,2,1:T(8,128)(2,1)S(1)}, f32[1536,6,64]{0,2,1:T(8,128)S(1)}, f32[1536,6,64]{0,2,1:T(8,128)S(1)}) conditional(s32[]{:T(128)} %bitcast.28, (bf16[512,6,64]{0,2,1:T(8,128)(2,1)S(1)}, bf16[1536,6,64]{0,2,1:T(8,128)(2,1)}, f32[6,512]{1,0:T(8,128)S(1)}, bf16[512,6,64]{0,2,1:T(8,128)(2,1)S(1)}, ...), branch_computations={%region_27.29_spmd, %region_29.31_spmd} | conditional | flops 3068065280 | bytes 265068640 | solution.py:173
  290.3 3.6 multiply_reduce_fusion.1
  300.1 4.3 fusion.97
  304.4 35.5 %conditional.21 = (bf16[512,6,64]{0,2,1:T(8,128)(2,1)S(1)}, f32[2048,6,64]{0,2,1:T(8,128)S(1)}, f32[2048,6,64]{0,2,1:T(8,128)}) conditional(s32[]{:T(128)} %bitcast.28, (bf16[512,6,64]{0,2,1:T(8,128)(2,1)}, bf16[2048,6,64]{0,2,1:T(8,128)(2,1)S(1)}, f32[6,512]{1,0:T(8,128)S(1)}, bf16[512,6,64]{0,2,1:T(8,128)(2,1)S(1)}, ...), branch_computations={%region_31.33_spmd, %region_33.35_spmd} | conditional | flops 4090623488 | bytes 201760800 | solution.py:173
  310.4 3.0 fusion.58
  313.4 8.1 multiply_reduce_fusion.3
  321.5 5.5 multiply_convert_fusion.3
  327.0 5.8 fusion.54
  340.0 4.7 add.327
  349.7 6.3 multiply_convert_fusion.4
  365.5 4.8 add_add_fusion
  370.6 9.8 %fusion.131 = f32[768,1536]{1,0:T(8,128)} fusion(bf16[2048,768]{1,0:T(8,128)(2,1)} %all-gather.7.cloned.1.call-done, bf16[2048,1536]{1,0:T(8,128)(2,1)} %copy-done.87), kind=kOutput, calls=%fused_computation.235 | convolution fusion | flops 4831838208 | bytes 14155776 | tf_op jit(solution)/shard_map/dot_general | solution.py:33
  380.3 8.9 fusion.132
  393.2 2.9 fusion.128
  396.1 2.9 fusion.129
  399.6 167.5 %all-reduce.7 = (f32[384]{0:T(512)}, f32[192]{0:T(256)}, f32[1536]{0:T(1024)}) all-reduce(f32[384]{0:T(512)S(1)} %reduce_sum.280, f32[192]{0:T(256)S(1)} %reduce_sum.282, f32[1536]{0:T(1024)S(1)} %copy-done.78), channel_id=1, replica_groups=mesh['dp'=16,'tensor'=2] {'dp'}, use_global_device_ids=true, to_apply=%region_44.45 | all-reduce | flops 2112 | bytes 16896 | tf_op jit(solution)/shard_map/psum | solution.py:290
  567.2 3.1 fusion.89
  570.3 40.5 %all-reduce.6 = (f32[768]{0:T(1024)}, f32[768]{0:T(1024)}, f32[768]{0:T(1024)}, f32[768]{0:T(1024)}, f32[768]{0:T(1024)}, /*index=5*/f32[768]{0:T(1024)}) all-reduce(f32[768]{0:T(1024)S(1)} %get-tuple-element.274, f32[768]{0:T(1024)S(1)} %get-tuple-element.279, ...), channel_id=1, replica_groups=mesh['dp'=16,'tensor'=2] {'dp','tensor'}, use_global_device_ids=true, to_apply=%region_39.40 | all-reduce | flops 4608 | bytes 36864 | tf_op jit(solution)/shard_map/psum | solution.py:305
  610.9 4.6 fusion.88
  615.4 262.4 %all-reduce.11.cloned.1.call-done = (f32[768,384]{1,0:T(8,128)}, f32[768,384]{1,0:T(8,128)}, f32[768,192]{0,1:T(8,128)}, f32[384,768]{1,0:T(8,128)}, f32[768,1536]{1,0:T(8,128)}, /*index=5*/f32[1536,768]{1,0:T(8,128)}) async-done(((f32[768,384]{1,0:T(8,128)}, f32[768,384]{1,0:T(8,128)}, f32[768,192]{0,1:T(8,128)}, f32[384,768]{1,0:T(8,128)}, f32[768,1536]{1,0:T(8,128)}, /*index=5*/f32[1536,768]{1,0:T(8,128)}), ...) | async-done | bytes 13565968 | tf_op jit(solution)/shard_map/psum | solution.py:290
  (302 shorter events, 102.2 us)
Async XLA Ops:
  7.2 147.4 %copy-start = (bf16[768,1536]{1,0:T(8,128)(2,1)S(1)}, bf16[768,1536]{1,0:T(8,128)(2,1)}, u32[]{:S(2)}) copy-start(bf16[768,1536]{1,0:T(8,128)(2,1)} %param.61) | copy-start | bytes 7077892
  7.2 9.9 %copy-start.86 = (bf16[192]{0:T(256)(128)(2,1)S(1)}, bf16[192]{0:T(256)(128)(2,1)}, u32[]{:S(2)}) copy-start(bf16[192]{0:T(256)(128)(2,1)} %param.56) | copy-start | bytes 1156
  7.2 9.9 %copy-start.83 = (bf16[384]{0:T(512)(128)(2,1)S(1)}, bf16[384]{0:T(512)(128)(2,1)}, u32[]{:S(2)}) copy-start(bf16[384]{0:T(512)(128)(2,1)} %param.53) | copy-start | bytes 2308
  7.2 24.1 %copy-start.49 = (bf16[768,192]{0,1:T(8,128)(2,1)S(1)}, bf16[768,192]{0,1:T(8,128)(2,1)}, u32[]{:S(2)}) copy-start(bf16[768,192]{0,1:T(8,128)(2,1)} %param.55) | copy-start | bytes 884740
  7.2 24.1 %all-gather.5.cloned.1.call-start = ((), (), s32[]{:S(2)}) async-start(), calls=%async_computation.4 | async-start | bytes 4718592 | tf_op jit(solution)/shard_map/all_gather | solution.py:206
  12.5 21.9 %copy-start.13 = (bf16[2048,192]{0,1:T(8,128)(2,1)S(1)}, bf16[2048,192]{0,1:T(8,128)(2,1)}, u32[]{:S(2)}) copy-start(bf16[2048,192]{0,1:T(8,128)(2,1)} %param.48) | copy-start | bytes 2359300
  16.4 118.6 %reduce-scatter.5.cloned.1.call-start = ((), (), s32[]{:S(2)}) async-start(), calls=%async_computation.5 | async-start | bytes 9437184 | tf_op jit(solution)/shard_map/reduce_scatter | solution.py:228
  37.5 6.8 copy-start.12
  44.2 21.1 %copy-start.36 = (bf16[512,384]{0,1:T(8,128)(2,1)}, bf16[512,384]{0,1:T(8,128)(2,1)S(1)}, u32[]{:S(2)}) copy-start(bf16[512,384]{0,1:T(8,128)(2,1)S(1)} %get-tuple-element.327) | copy-start | bytes 1179652
  44.2 25.9 %copy-start.32 = (bf16[512,384]{0,1:T(8,128)(2,1)}, bf16[512,384]{0,1:T(8,128)(2,1)S(1)}, u32[]{:S(2)}) copy-start(bf16[512,384]{0,1:T(8,128)(2,1)S(1)} %get-tuple-element.330) | copy-start | bytes 1179652
  86.6 68.0 %all-gather.7.cloned.1.call-start = ((), (), s32[]{:S(2)}) async-start(), calls=%async_computation.6 | async-start | bytes 4718592 | tf_op jit(solution)/shard_map/all_gather | solution.py:233
  141.2 28.2 %all-gather.9.cloned.1.call-start = ((), (), s32[]{:S(2)}) async-start(), calls=%async_computation.8 | async-start | bytes 4718592 | tf_op jit(solution)/shard_map/all_gather | solution.py:245
  141.8 70.5 %reduce-scatter.9.cloned.1.call-start = ((), (), s32[]{:S(2)}) async-start(), calls=%async_computation.9 | async-start | bytes 9437184 | tf_op jit(solution)/shard_map/reduce_scatter | solution.py:252
  196.5 30.6 %reduce-scatter.7.cloned.1.call-start = ((), (), s32[]{:S(2)}) async-start(), calls=%async_computation.7 | async-start | bytes 4718592 | tf_op jit(solution)/shard_map/reduce_scatter | solution.py:239
  196.7 9.1 %copy-start.81 = (bf16[768]{0:T(1024)(128)(2,1)S(1)}, bf16[768]{0:T(1024)(128)(2,1)}, u32[]{:S(2)}) copy-start(bf16[768]{0:T(1024)(128)(2,1)} %param.64) | copy-start | bytes 4612
  205.7 21.3 %copy-start.24 = (bf16[1024,768]{1,0:T(8,128)(2,1)S(1)}, bf16[1024,768]{1,0:T(8,128)(2,1)}, u32[]{:S(2)}) copy-start(bf16[1024,768]{1,0:T(8,128)(2,1)} %param.65) | copy-start | bytes 4718596
  205.7 41.3 %all-gather.11.cloned.1.call-start = ((), (), s32[]{:S(2)}) async-start(), calls=%async_computation.10 | async-start | bytes 4718592 | tf_op jit(solution)/shard_map/all_gather | solution.py:257
  227.1 6.6 copy-start.69
  227.1 7.2 copy-start.71
  227.1 7.2 copy-start.73
  227.1 20.0 %copy-start.42 = (bf16[384,768]{1,0:T(8,128)(2,1)S(1)}, bf16[384,768]{1,0:T(8,128)(2,1)}, u32[]{:S(2)}) copy-start(bf16[384,768]{1,0:T(8,128)(2,1)} %param.57) | copy-start | bytes 1769476
  233.6 333.6 %reduce-scatter.11.cloned.1.call-start = ((), (), s32[]{:S(2)}) async-start(), calls=%async_computation.11 | async-start | bytes 9437184 | tf_op jit(solution)/shard_map/reduce_scatter | solution.py:278
  234.3 45.4 %copy-start.51 = (f32[6,512]{1,0:T(8,128)}, f32[6,512]{1,0:T(8,128)S(1)}, u32[]{:S(2)}) copy-start(f32[6,512]{1,0:T(8,128)S(1)} %log_add_fusion.4) | copy-start | bytes 36868
  247.0 7.7 slice-start.6
  258.8 9.9 %copy-start.37 = (bf16[512,384]{0,1:T(8,128)(2,1)S(1)}, bf16[512,384]{0,1:T(8,128)(2,1)}, u32[]{:S(2)}) copy-start(bf16[512,384]{0,1:T(8,128)(2,1)} %copy-done.36) | copy-start | bytes 1179652
  258.8 14.1 %slice-start = ((s8[12582912]{0:T(1024)(128)(4,1)}), s8[4194304]{0:T(1024)(128)(4,1)S(1)}, s32[]{:S(2)}) async-start(s8[12582912]{0:T(1024)(128)(4,1)} %bitcast.176), calls=%async_computation.13 | async-start | bytes 8388608
  258.8 14.1 %slice-start.1 = ((s8[12582912]{0:T(1024)(128)(4,1)}), s8[4194304]{0:T(1024)(128)(4,1)S(1)}, s32[]{:S(2)}) async-start(s8[12582912]{0:T(1024)(128)(4,1)} %bitcast.176), calls=%async_computation.14 | async-start | bytes 8388608
  265.2 7.7 slice-start.2
  272.9 6.9 copy-start.18
  272.9 6.8 copy-start.56
  284.1 16.0 %copy-start.11 = (bf16[2048,384]{0,1:T(8,128)(2,1)S(1)}, bf16[2048,384]{0,1:T(8,128)(2,1)}, u32[]{:S(2)}) copy-start(bf16[2048,384]{0,1:T(8,128)(2,1)} %copy-done.10) | copy-start | bytes 4718596
  284.1 16.0 %copy-start.58 = (f32[6,512]{1,0:T(8,128)S(1)}, f32[6,512]{1,0:T(8,128)}, u32[]{:S(2)}) copy-start(f32[6,512]{1,0:T(8,128)} %copy-done.57) | copy-start | bytes 36868
  340.0 9.7 %slice-start.3 = ((s8[12582912]{0:T(1024)(128)(4,1)}), s8[4194304]{0:T(1024)(128)(4,1)S(1)}, s32[]{:S(2)}) async-start(s8[12582912]{0:T(1024)(128)(4,1)} %bitcast.178), calls=%async_computation.16 | async-start | bytes 8388608
  370.3 507.6 %all-reduce.11.cloned.1.call-start = ((), (), s32[]{:S(2)}) async-start(), calls=%async_computation.12 | async-start | bytes 27131904 | tf_op jit(solution)/shard_map/psum | solution.py:290
  370.5 9.8 %copy-start.84 = (bf16[2048,768]{1,0:T(8,128)(2,1)S(1)}, bf16[2048,768]{1,0:T(8,128)(2,1)}, u32[]{:S(2)}) copy-start(bf16[2048,768]{1,0:T(8,128)(2,1)} %all-gather.9.cloned.1.call-done) | copy-start | bytes 9437188
  380.3 8.9 copy-start.30
  380.3 10.5 %copy-start.21 = (bf16[2048,6,64]{0,2,1:T(8,128)(2,1)S(1)}, bf16[2048,6,64]{0,2,1:T(8,128)(2,1)}, u32[]{:S(2)}) copy-start(bf16[2048,6,64]{0,2,1:T(8,128)(2,1)} %copy-done.20) | copy-start | bytes 4718596
  380.3 10.5 %copy-start.85 = (bf16[2048,768]{1,0:T(8,128)(2,1)S(1)}, bf16[2048,768]{1,0:T(8,128)(2,1)}, u32[]{:S(2)}) copy-start(bf16[2048,768]{1,0:T(8,128)(2,1)} %all-gather.11.cloned.1.call-done) | copy-start | bytes 9437188
  398.9 168.2 %copy-start.6 = (bf16[1024,768]{1,0:T(8,128)(2,1)S(1)}, bf16[1024,768]{1,0:T(8,128)(2,1)}, u32[]{:S(2)}) copy-start(bf16[1024,768]{1,0:T(8,128)(2,1)} %param.47) | copy-start | bytes 4718596
  398.9 168.2 %copy-start.60 = (f32[1024]{0:T(1024)S(1)}, f32[1024]{0:T(1024)}, u32[]{:S(2)}) copy-start(f32[1024]{0:T(1024)} %copy-done.59) | copy-start | bytes 12292
  398.9 168.2 %copy-start.62 = (f32[768]{0:T(1024)S(1)}, f32[768]{0:T(1024)}, u32[]{:S(2)}) copy-start(f32[768]{0:T(1024)} %copy-done.61) | copy-start | bytes 9220
  398.9 168.2 %copy-start.64 = (f32[1024]{0:T(1024)S(1)}, f32[1024]{0:T(1024)}, u32[]{:S(2)}) copy-start(f32[1024]{0:T(1024)} %copy-done.63) | copy-start | bytes 12292
  399.0 171.3 %copy-start.74 = (f32[768]{0:T(1024)S(1)}, f32[768]{0:T(1024)}, u32[]{:S(2)}) copy-start(f32[768]{0:T(1024)} %get-tuple-element.272) | copy-start | bytes 9220
  399.0 171.3 %copy-start.75 = (f32[768]{0:T(1024)S(1)}, f32[768]{0:T(1024)}, u32[]{:S(2)}) copy-start(f32[768]{0:T(1024)} %get-tuple-element.278) | copy-start | bytes 9220
  399.0 171.3 %copy-start.76 = (f32[768]{0:T(1024)S(1)}, f32[768]{0:T(1024)}, u32[]{:S(2)}) copy-start(f32[768]{0:T(1024)} %get-tuple-element.299) | copy-start | bytes 9220
  399.0 171.3 %copy-start.77 = (f32[768]{0:T(1024)S(1)}, f32[768]{0:T(1024)}, u32[]{:S(2)}) copy-start(f32[768]{0:T(1024)} %get-tuple-element.322) | copy-start | bytes 9220
  877.9 6.9 copy-start.40
  877.9 8.0 copy-start.25
  (56 other events, 187.7 us)
Sparse Core Ops, SparseCore 0:
  16.5 14.8 all-gather.4
  86.7 48.1 reduce-scatter.4
  141.3 13.2 all-gather.6
  156.1 13.2 all-gather.8
  196.6 15.6 reduce-scatter.8
  215.0 12.0 reduce-scatter.6
  233.7 13.2 all-gather.10
  370.4 104.0 reduce-scatter.10
  482.7 395.1 all-reduce.10
where the time goes:
time: 904 us; the launch traced here: 897 us
  waiting for transfers between devices  367 us (41%)
  blocking collectives  208 us (23%)
  matrix products  176 us (19%)
  other arithmetic  78.7 us (9%)
  local copies, waits for them, and re-layouts  38.2 us (4%)
  between operations  15.8 us (2%)
  loops' own time  13 us (1%)
    psum x1, waiting for transfers between devices, on_device(): lax.psum((grad_w_down, grad_w_up, grad_bias_up, grad_w_out, grad_w_query,...  262 us
    psum x1, blocking collectives, on_device(): lax.psum((grad_w_down, grad_w_up, grad_bias_up, grad_w_out, grad_w_query,...  168 us
    reduce_scatter x1, waiting for transfers between devices, on_device(): lax.psum_scatter(attn_terms, 'tensor', scatter_dimension=0, tiled=True)  47.6 us
    psum x1, blocking collectives, on_device(): lax.psum((jnp.sum(grad_ln_one * normed_one, axis=0), jnp.sum(grad_ln_one,...  40.5 us
    dot_general x6, matrix products, contract_cols(): lax.dot_general(left_array, right_array, (((1,), (1,)), ((), ())), prefer...  35.4 us
    dot_general x6, matrix products, contract_rows(): lax.dot_general(left_array, right_array, (((0,), (0,)), ((), ())), prefer...  28.3 us
    unnamed x196, local copies, waits for them, and re-layouts  26.3 us
    dot_general x6, matrix products, masked_scores(): jnp.einsum('qhd,khd->hqk', query_block, key_block, preferred_element_type...  21.9 us
  transfers between devices with their start and end apart: 9, of which 8 were waited for; matrix products, arithmetic and copies ran while one was open for 7% of the time, Pallas kernels for 0%

commit v1 on v0

v1 whole, which is shorter than its diff:
```python
import functools

import jax
import jax.numpy as jnp
from jax import lax
from jax.experimental import pallas as pl
from jax.experimental.pallas import tpu as pltpu
from jax.sharding import PartitionSpec as P

HEAD_DIM = 64
NORM_EPS = 1e-05
GELU_ROOT = 0.7978845608028654
GELU_CUBE = 0.044715
NN = (((1,), (0,)), ((), ()))
NT = (((1,), (1,)), ((), ()))
TN = (((0,), (0,)), ((), ()))
F32 = jnp.float32
BF16 = jnp.bfloat16
VMEM_LIMIT = 60 << 20


def dot(left, right, dims=NN):
    return lax.dot_general(left, right, dims, preferred_element_type=F32)


def whole(array):
    return pl.BlockSpec(array.shape, lambda *_, nd=array.ndim: (0,) * nd)


def whole_shape(shape):
    return pl.BlockSpec(shape, lambda *_, nd=len(shape): (0,) * nd)


def row_normalize(rows):
    centered = rows - jnp.mean(rows, axis=1, keepdims=True)
    inverse = lax.rsqrt(jnp.mean(centered * centered, axis=1, keepdims=True) + NORM_EPS)
    return centered * inverse, inverse


def row_normalize_back(scaled, normed, inverse):
    return inverse * (
        scaled
        - jnp.mean(scaled, axis=1, keepdims=True)
        - normed * jnp.mean(scaled * normed, axis=1, keepdims=True)
    )


def project_kernel(place, x_own, x_other, first, gain, bias, wq, bq, wk, wv, bv, ln, qt, k, kt, v, vt):
    step = pl.program_id(0)
    rows = jnp.where(step == 0, x_own[...], x_other[...]).astype(F32)
    normed, _ = row_normalize(rows)
    low = (normed * gain[...].astype(F32) + bias[...].astype(F32)).astype(BF16)
    ln[...] = low
    scale = HEAD_DIM ** (-0.5)
    queries = (dot(low, wq[...]) + bq[...].astype(F32)).astype(BF16).astype(F32) * scale
    qt[...] = queries.astype(BF16).T
    keys = dot(low, wk[...]).astype(BF16)
    k[...] = keys
    kt[...] = keys.T
    fresh = (dot(low, wv[...]) + bv[...].astype(F32)).astype(BF16)
    values = jnp.concatenate([fresh, first[...]], axis=1)
    v[...] = values
    vt[...] = values.T


def project(place, x_own, x_other, first, gain, bias, wq, bq, wk, wv, bv):
    rows, width = x_own.shape
    heads = wq.shape[1]

    def spot(j, place):
        return jnp.where(j == 0, place[0], 1 - place[0])

    shapes = (
        ((2 * rows, width), (rows, width), lambda j, p: (spot(j, p), 0)),
        ((heads, 2 * rows), (heads, rows), lambda j, p: (0, spot(j, p))),
        ((2 * rows, heads), (rows, heads), lambda j, p: (spot(j, p), 0)),
        ((heads, 2 * rows), (heads, rows), lambda j, p: (0, spot(j, p))),
        ((2 * rows, heads), (rows, heads), lambda j, p: (spot(j, p), 0)),
        ((heads, 2 * rows), (heads, rows), lambda j, p: (0, spot(j, p))),
    )
    operands = (x_own, x_other, first, gain, bias, wq, bq, wk, wv, bv)
    specs = [whole(a) for a in operands]
    specs[2] = pl.BlockSpec((rows, first.shape[1]), lambda j, p: (spot(j, p), 0))
    return pl.pallas_call(
        project_kernel,
        out_shape=[jax.ShapeDtypeStruct(s, BF16) for s, _, _ in shapes],
        grid_spec=pltpu.PrefetchScalarGridSpec(
            num_scalar_prefetch=1,
            grid=(2,),
            in_specs=specs,
            out_specs=[pl.BlockSpec(b, m) for _, b, m in shapes],
        ),
        compiler_params=pltpu.CompilerParams(vmem_limit_bytes=VMEM_LIMIT),
        name="project",
    )(place, *operands)


def causal(size):
    keys = lax.broadcasted_iota(jnp.int32, (size, size), 0)
    return keys <= lax.broadcasted_iota(jnp.int32, (size, size), 1)


def query_blocks(tokens, block, two_docs, body):
    half = tokens // 2
    for start in range(0, tokens, block):
        if start < half:
            body(start, 0)
        else:

            @pl.when(two_docs)
            def _():
                body(start, half)

            @pl.when(jnp.logical_not(two_docs))
            def _():
                body(start, 0)


def attend_kernel(block, split, qt, k, vt, attended, lse, sums):
    width, tokens = qt.shape
    two_docs = split[0] < tokens
    ones = (lax.broadcasted_iota(jnp.int32, (16, tokens), 0) == 0).astype(BF16)
    sums[0, HEAD_DIM:, :] = ones
    sums[1, HEAD_DIM:, :] = ones

    def pair_step(pair, _):
        col = pl.multiple_of(pair * 2 * HEAD_DIM, 2 * HEAD_DIM)
        sums[0, :HEAD_DIM, :] = vt[pl.ds(col, HEAD_DIM), :]
        sums[1, :HEAD_DIM, :] = vt[pl.ds(col + HEAD_DIM, HEAD_DIM), :]
        owner = lax.broadcasted_iota(jnp.int32, (2 * HEAD_DIM, block), 0) // HEAD_DIM

        def body(start, low):
            stop = start + block
            inner = start - low
            queries = qt[pl.ds(col, 2 * HEAD_DIM), start:stop]
            keys = k[low:stop, pl.ds(col, 2 * HEAD_DIM)]
            scores = [
                dot(keys, jnp.where(owner == j, queries, jnp.zeros_like(queries))) for j in range(2)
            ]
            for j in range(2):
                edge = jnp.where(causal(block), scores[j][inner:], -1e30)
                top = jnp.max(edge, axis=0, keepdims=True)
                if inner:
                    near = scores[j][:inner]
                    top = jnp.maximum(top, jnp.max(near, axis=0, keepdims=True))
                    weights = jnp.concatenate(
                        [jnp.exp(near - top).astype(BF16), jnp.exp(edge - top).astype(BF16)], axis=0
                    )
                else:
                    weights = jnp.exp(edge - top).astype(BF16)
                total = dot(sums[j, :, low:stop], weights)
                denominator = total[HEAD_DIM : HEAD_DIM + 1]
                attended[pl.ds(col + HEAD_DIM * j, HEAD_DIM), start:stop] = (
                    total[:HEAD_DIM] * (1.0 / denominator)
                ).astype(BF16)
                lse[pl.ds(pair * 2 + j, 1), :, start:stop] = (top + jnp.log(denominator))[None]

        query_blocks(tokens, block, two_docs, body)
        return 0

    lax.fori_loop(0, width // (2 * HEAD_DIM), pair_step, 0)


def attend(split, qt, k, vt, block=512):
    width, tokens = qt.shape
    vmem = pl.BlockSpec(memory_space=pltpu.VMEM)
    return pl.pallas_call(
        functools.partial(attend_kernel, block),
        out_shape=(
            jax.ShapeDtypeStruct((width, tokens), BF16),
            jax.ShapeDtypeStruct((width // HEAD_DIM, 1, tokens), F32),
        ),
        in_specs=[pl.BlockSpec(memory_space=pltpu.SMEM), vmem, vmem, vmem],
        out_specs=(vmem, vmem),
        scratch_shapes=[pltpu.VMEM((2, HEAD_DIM + 16, tokens), BF16)],
        compiler_params=pltpu.CompilerParams(vmem_limit_bytes=VMEM_LIMIT),
        name="attend",
    )(split, qt, k, vt)


def extra_rows(row):
    high = row.astype(BF16).astype(F32)
    middle = (row - high).astype(BF16).astype(F32)
    low = row - high - middle
    index = lax.broadcasted_iota(jnp.int32, (HEAD_DIM, row.shape[1]), 0)
    rest = jnp.where(index == 2, low, 0.0)
    return jnp.where(index == 0, high, jnp.where(index == 1, middle, rest)).astype(BF16)


def attend_back_kernel(
    block, split, place, qt, k, kt, v, do_own, do_other, attended, lse,
    dqt, dkt, dvt, grads, q_aug, d_aug, k_aug, v_aug, dk_sum, dv_sum,
):
    width, tokens = qt.shape
    half = tokens // 2
    two_docs = split[0] < tokens
    own = pl.multiple_of(place[0] * half, half)
    other = pl.multiple_of((1 - place[0]) * half, half)
    grads[:, pl.ds(own, half)] = do_own[...]
    grads[:, pl.ds(other, half)] = do_other[...]

    def pair_step(pair, _):
        col = pl.multiple_of(pair * 2 * HEAD_DIM, 2 * HEAD_DIM)
        lane = lax.broadcasted_iota(jnp.int32, (tokens, 2 * HEAD_DIM), 1)
        ones = jnp.where(lax.rem(lane, HEAD_DIM) < 3, 1.0, 0.0).astype(BF16)
        keys = k[:, pl.ds(col, 2 * HEAD_DIM)]
        values = v[:, pl.ds(col, 2 * HEAD_DIM)]
        dk_sum[...] = jnp.zeros_like(dk_sum)
        dv_sum[...] = jnp.zeros_like(dv_sum)
        head_rows = [pl.ds(pl.multiple_of(col + HEAD_DIM * j, HEAD_DIM), HEAD_DIM) for j in range(2)]
        for j in range(2):
            mine = lane // HEAD_DIM == j
            k_aug[j] = jnp.where(mine, keys, ones)
            v_aug[j] = jnp.where(mine, values, ones)
            grad = grads[head_rows[j], :]
            inner = jnp.sum(
                grad.astype(F32) * attended[head_rows[j], :].astype(F32), axis=0, keepdims=True
            )
            base, extra = HEAD_DIM * j, HEAD_DIM * (1 - j)
            q_aug[j, base : base + HEAD_DIM, :] = qt[head_rows[j], :]
            q_aug[j, extra : extra + HEAD_DIM, :] = extra_rows(-lse[pl.ds(pair * 2 + j, 1)][0])
            d_aug[j, base : base + HEAD_DIM, :] = grad
            d_aug[j, extra : extra + HEAD_DIM, :] = extra_rows(-inner)

        def body(start, low):
            stop = start + block
            inner = start - low
            for j in range(2):
                scores = dot(k_aug[j, low:stop, :], q_aug[j, :, start:stop])
                grad_probs = dot(v_aug[j, low:stop, :], d_aug[j, :, start:stop])
                probs = jnp.where(causal(block), jnp.exp(scores[inner:]), 0.0)
                if inner:
                    probs = jnp.concatenate([jnp.exp(scores[:inner]), probs], axis=0)
                grad_scores = (probs * grad_probs).astype(BF16)
                probs = probs.astype(BF16)
                rows = head_rows[j]
                dqt[rows, start:stop] = (
                    dot(kt[rows, low:stop], grad_scores) * HEAD_DIM ** (-0.5)
                ).astype(BF16)
                dv_sum[j, :, low:stop] += dot(grads[rows, start:stop], probs, NT)
                dk_sum[j, :, low:stop] += dot(qt[rows, start:stop], grad_scores, NT)

        query_blocks(tokens, block, two_docs, body)
        for j in range(2):
            dkt[head_rows[j], :] = dk_sum[j].astype(BF16)
            dvt[head_rows[j], :] = dv_sum[j]
        return 0

    lax.fori_loop(0, width // (2 * HEAD_DIM), pair_step, 0)


def attend_back(split, place, qt, k, kt, v, do_own, do_other, attended, lse, block=512):
    width, tokens = qt.shape
    vmem = pl.BlockSpec(memory_space=pltpu.VMEM)
    smem = pl.BlockSpec(memory_space=pltpu.SMEM)
    pair = 2 * HEAD_DIM
    return pl.pallas_call(
        functools.partial(attend_back_kernel, block),
        out_shape=(
            jax.ShapeDtypeStruct((width, tokens), BF16),
            jax.ShapeDtypeStruct((width, tokens), BF16),
            jax.ShapeDtypeStruct((width, tokens), F32),
        ),
        in_specs=[smem, smem] + [vmem] * 8,
        out_specs=(vmem, vmem, vmem),
        scratch_shapes=[
            pltpu.VMEM((width, tokens), BF16),
            pltpu.VMEM((2, pair, tokens), BF16),
            pltpu.VMEM((2, pair, tokens), BF16),
            pltpu.VMEM((2, tokens, pair), BF16),
            pltpu.VMEM((2, tokens, pair), BF16),
            pltpu.VMEM((2, HEAD_DIM, tokens), F32),
            pltpu.VMEM((2, HEAD_DIM, tokens), F32),
        ],
        compiler_params=pltpu.CompilerParams(vmem_limit_bytes=VMEM_LIMIT),
        name="attend_back",
    )(split, place, qt, k, kt, v, do_own, do_other, attended, lse)


def gelu_both(v):
    square = v * v
    tanh = jnp.tanh(v * (GELU_ROOT + (GELU_ROOT * GELU_CUBE) * square))
    half = 0.5 * v
    slope = 0.5 + 0.5 * tanh + half * (1.0 - tanh * tanh) * (
        GELU_ROOT + (3.0 * GELU_ROOT * GELU_CUBE) * square
    )
    return half + half * tanh, slope


def feed_kernel(
    steps, x, cot, att_own, att_other, wo_own, wo_other, bias_o, gain, bias,
    up_other, up_own, bu_other, bu_own, down_other, down_own, bias_d,
    out, grad_mid, grad_att, grad_up, grad_down, grad_wo, grad_bu, small,
    ln, ln_t, normed, inverse, middle, total, grad_ln,
):
    step = pl.program_id(0)
    heads = att_own.shape[0]

    @pl.when(step == 0)
    def _():
        branch = dot(att_own[...], wo_own[...], TN) + dot(att_other[...], wo_other[...], TN)
        mid = x[...].astype(F32) + (branch + bias_o[...].astype(F32))
        middle[...] = mid
        norm, inv = row_normalize(mid)
        normed[...] = norm
        inverse[...] = jnp.broadcast_to(inv, inverse.shape)
        low = (norm * gain[...].astype(F32) + bias[...].astype(F32)).astype(BF16)
        ln[...] = low
        ln_t[...] = low.T
        total[...] = jnp.zeros_like(total)
        grad_ln[...] = jnp.zeros_like(grad_ln)

    def chunk(up, bias_up, down):
        hidden = dot(ln[...], up[...]) + bias_up[...].astype(F32)
        act, slope = gelu_both(hidden)
        act = act.astype(BF16)
        grad_hidden = (dot(cot[...], down[...], NT) * slope).astype(BF16)
        total[...] += dot(act, down[...])
        grad_ln[...] += dot(grad_hidden, up[...], NT)
        grad_down[0] = dot(act, cot[...], TN).astype(BF16)
        grad_up[0] = dot(ln_t[...], grad_hidden).astype(BF16)
        grad_bu[0] = jnp.sum(grad_hidden.astype(F32), axis=0, keepdims=True)

    @pl.when(step < steps // 2)
    def _():
        chunk(up_other, bu_other, down_other)

    @pl.when(step >= steps // 2)
    def _():
        chunk(up_own, bu_own, down_own)

    @pl.when(step == steps - 1)
    def _():
        out[...] = (middle[...] + (total[...] + bias_d[...].astype(F32))).astype(BF16)
        grad = grad_ln[...]
        norm = normed[...]
        cot32 = cot[...].astype(F32)
        back = row_normalize_back(grad * gain[...].astype(F32), norm, inverse[:, :1])
        mid = cot32 + back
        grad_mid[...] = mid
        low = mid.astype(BF16)
        small[0:1, :] = jnp.sum(grad * norm, axis=0, keepdims=True)
        small[1:2, :] = jnp.sum(grad, axis=0, keepdims=True)
        small[2:3, :] = jnp.sum(low.astype(F32), axis=0, keepdims=True)
        small[3:4, :] = jnp.sum(cot32, axis=0, keepdims=True)
        grad_wo[:heads] = dot(att_own[...], low).astype(BF16)
        grad_wo[heads:] = dot(att_other[...], low).astype(BF16)
        grad_att[:heads] = dot(wo_own[...], low, NT).astype(BF16)
        grad_att[heads:] = dot(wo_other[...], low, NT).astype(BF16)


def feed(
    x, cot, att_own, att_other, wo_own, wo_other, bias_o, gain, bias,
    up_other, up_own, bu_other, bu_own, down_other, down_own, bias_d, chunk=512,
):
    rows, width = x.shape
    hidden = up_own.shape[1]
    steps = 2 * hidden // chunk
    half = steps // 2
    heads = att_own.shape[0]

    def first(j):
        return jnp.minimum(j, half - 1)

    def second(j):
        return jnp.maximum(j - half, 0)

    operands = (
        x, cot, att_own, att_other, wo_own, wo_other, bias_o, gain, bias,
        up_other, up_own, bu_other, bu_own, down_other, down_own, bias_d,
    )
    specs = [whole(a) for a in operands]
    specs[9] = pl.BlockSpec((width, chunk), lambda j: (0, first(j)))
    specs[10] = pl.BlockSpec((width, chunk), lambda j: (0, second(j)))
    specs[11] = pl.BlockSpec((1, chunk), lambda j: (0, first(j)))
    specs[12] = pl.BlockSpec((1, chunk), lambda j: (0, second(j)))
    specs[13] = pl.BlockSpec((chunk, width), lambda j: (first(j), 0))
    specs[14] = pl.BlockSpec((chunk, width), lambda j: (second(j), 0))
    results = [
        ((rows, width), BF16),
        ((rows, width), F32),
        ((2 * heads, rows), BF16),
        ((2, width, hidden), BF16),
        ((2, hidden, width), BF16),
        ((2 * heads, width), BF16),
        ((2, 1, hidden), F32),
        ((8, width), F32),
    ]
    out_specs = [whole_shape(s) for s, _ in results]
    out_specs[3] = pl.BlockSpec((1, width, chunk), lambda j: (j // half, 0, lax.rem(j, half)))
    out_specs[4] = pl.BlockSpec((1, chunk, width), lambda j: (j // half, lax.rem(j, half), 0))
    out_specs[6] = pl.BlockSpec((1, 1, chunk), lambda j: (j // half, 0, lax.rem(j, half)))
    return pl.pallas_call(
        functools.partial(feed_kernel, steps),
        grid=(steps,),
        in_specs=specs,
        out_specs=out_specs,
        out_shape=[jax.ShapeDtypeStruct(s, t) for s, t in results],
        scratch_shapes=[
            pltpu.VMEM((rows, width), BF16),
            pltpu.VMEM((width, rows), BF16),
            pltpu.VMEM((rows, width), F32),
            pltpu.VMEM((rows, 128), F32),
            pltpu.VMEM((rows, width), F32),
            pltpu.VMEM((rows, width), F32),
            pltpu.VMEM((rows, width), F32),
        ],
        compiler_params=pltpu.CompilerParams(vmem_limit_bytes=VMEM_LIMIT),
        name="feed",
    )(*operands)


def swap(array):
    return lax.ppermute(array, "tensor", [(0, 1), (1, 0)])


def on_device(
    input_rows, first_values, doc_split, gain_norm1, bias_norm1, w_query, bias_query, w_key,
    w_value, bias_value, w_out, bias_attn_out, gain_norm2, bias_norm2, w_up, bias_up, w_down,
    bias_down, cotangent,
):
    rows = input_rows.shape[0]
    heads = w_query.shape[1]
    fresh = w_value.shape[1]
    here = lax.axis_index("tensor")
    place = here.reshape(1).astype(jnp.int32)
    row = lambda a: a.reshape(1, -1)
    x_other = swap(input_rows)
    ln, qt, k, kt, v, vt = project(
        place, input_rows, x_other, first_values, row(gain_norm1), row(bias_norm1), w_query,
        row(bias_query), w_key, w_value, row(bias_value),
    )
    up_other, down_other, wo_other = swap(w_up), swap(w_down), swap(w_out)
    bu_other = swap(row(bias_up))
    attended, lse = attend(doc_split, qt, k, vt)
    mine = lambda a: lax.dynamic_slice_in_dim(a, here * rows, rows, 1)
    theirs = lambda a: lax.dynamic_slice_in_dim(a, (1 - here) * rows, rows, 1)
    att_other = swap(theirs(attended))
    output, grad_middle, grad_att, grad_up, grad_down, grad_wo, grad_bu, small = feed(
        input_rows, cotangent, mine(attended), att_other, w_out, wo_other, row(bias_attn_out),
        row(gain_norm2), row(bias_norm2), up_other, w_up, row(bu_other), row(bias_up), down_other,
        w_down, row(bias_down),
    )
    do_other = swap(grad_att[heads:])
    joined = lambda a: (a[1].astype(F32) + swap(a[0]).astype(F32)).astype(BF16)
    grad_up = joined(grad_up)
    grad_down = joined(grad_down)
    grad_wo = (grad_wo[:heads].astype(F32) + swap(grad_wo[heads:]).astype(F32)).astype(BF16)
    grad_bu = grad_bu[1, 0] + swap(grad_bu[0, 0])
    dqt, dkt, dvt = attend_back(
        doc_split, place, qt, k, kt, v, grad_att[:heads], do_other, attended, lse
    )
    grad_first = dvt[fresh:].T
    dft = dvt[:fresh].astype(BF16)
    stack = jnp.concatenate([dqt, dkt, dft], axis=0)
    weights = jnp.concatenate([w_query, w_key, w_value], axis=1)
    grad_qkv = dot(ln, stack, (((0,), (1,)), ((), ()))).astype(BF16)
    bias_sums = jnp.sum(stack.astype(F32), axis=1)
    terms_other = dot(theirs(stack), weights, (((0,), (1,)), ((), ()))).astype(BF16)
    terms = dot(mine(stack), weights, (((0,), (1,)), ((), ())))
    grad_ln = terms + swap(terms_other).astype(F32)
    normed, inverse = row_normalize(input_rows.astype(F32))
    grad_input = grad_middle + row_normalize_back(
        grad_ln * gain_norm1.astype(F32), normed, inverse
    )
    grad_up, grad_down, grad_wo, grad_qkv = lax.psum(
        (grad_up, grad_down, grad_wo, grad_qkv), "dp"
    )
    grad_bu, bias_sums = lax.psum((grad_bu, bias_sums), "dp")
    gain_one, shift_one, small = lax.psum(
        (jnp.sum(grad_ln * normed, axis=0), jnp.sum(grad_ln, axis=0), small[:4]), ("dp", "tensor")
    )
    grad_qkv = grad_qkv.astype(F32)
    return (
        output,
        grad_input,
        grad_first,
        gain_one,
        shift_one,
        grad_qkv[:, :heads],
        bias_sums[:heads],
        grad_qkv[:, heads : 2 * heads],
        grad_qkv[:, 2 * heads :],
        bias_sums[2 * heads :],
        grad_wo.astype(F32),
        small[2],
        small[0],
        small[1],
        grad_up.astype(F32),
        grad_bu,
        grad_down.astype(F32),
        small[3],
    )


def solution(mesh):
    rows = P(("dp", "tensor"), None)
    cols = P(None, "tensor")
    split = P("tensor")
    firsts = P("dp", "tensor")
    wide = P("tensor", None)
    return jax.shard_map(
        on_device,
        mesh=mesh,
        in_specs=(
            rows, firsts, P("dp"), P(), P(), cols, split, cols, cols, split, wide, P(), P(), P(),
            cols, split, wide, P(), rows,
        ),
        out_specs=(
            rows, rows, firsts, P(), P(), cols, split, cols, cols, split, wide, P(), P(), P(),
            cols, split, wide, P(),
        ),
        check_vma=False,
    )
```

time: 904 us -> 446 us (0.49)
  waiting for transfers between devices: 367 us -> 88.6 us
  matrix products: 176 us -> 15.4 us
  Pallas kernels: 0 us -> 117 us
  blocking collectives: 208 us -> 139 us
  other arithmetic: 78.7 us -> 20.9 us
  loops' own time: 13 us -> 0 us
    psum x1, waiting for transfers between devices: 262 us -> 85.8 us  [on_device(): lax.psum((grad_up, grad_down, grad_wo, grad_qkv), 'dp')]
    dot_general x44 -> x3, matrix products: 176 us -> 15.4 us  [dot(): return lax.dot_general(left, right, dims, preferred_element_type=F32)]
    pallas_call x0 -> x4, Pallas kernels: none -> 117 us  [the longest x1 58.5 us: feed(): pl.pallas_call(functools.partial(feed_kernel, steps), grid=(steps,), in_s...]
    psum x2, blocking collectives: 208 us -> 139 us  [the longest x1 101 us: on_device(): grad_bu, bias_sums = lax.psum((grad_bu, bias_sums), 'dp')]
    reduce_scatter x4 -> x0, waiting for transfers between devices: 64.6 us -> none  [the longest x1 47.6 us: on_device(): lax.psum_scatter(attn_terms, 'tensor', scatter_dimension=0, tiled=True)]
    all_gather x4 -> x0, waiting for transfers between devices: 38.9 us -> none  [the longest x1 13.7 us: on_device(): ln_one_all = lax.all_gather(ln_one_low, 'tensor', axis=0, tiled=True)]
    reduce_sum x13 -> x3, other arithmetic: 31 us -> 3.22 us  [the longest x1 2.35 us: on_device(): bias_sums = jnp.sum(stack.astype(F32), axis=1)]
    convert_element_type x16 -> x7, other arithmetic: 29.1 us -> 13.1 us  [the longest x2 5.67 us: on_device(): joined = lambda a: (a[1].astype(F32) + swap(a[0]).astype(F32)).astype(BF16)]
  transfers between devices with their start and end apart: 9 -> 13, of which waited for: 8 -> 5; matrix products, arithmetic and copies ran while one was open for 7% -> 11% of each run, Pallas kernels for 0% -> 13%
where the time goes in v1:
time: 446 us; the launch traced here: 438 us
  blocking collectives  139 us (31%)
  Pallas kernels  117 us (26%)
  waiting for transfers between devices  88.6 us (20%)
  local copies, waits for them, and re-layouts  37.6 us (8%)
  other arithmetic  20.9 us (5%)
  between operations  15.5 us (3%)
  matrix products  15.4 us (3%)
    psum x1, blocking collectives, on_device(): grad_bu, bias_sums = lax.psum((grad_bu, bias_sums), 'dp')  101 us
    psum x1, waiting for transfers between devices, on_device(): lax.psum((grad_up, grad_down, grad_wo, grad_qkv), 'dp')  85.8 us
    pallas_call x1, Pallas kernels, feed(): pl.pallas_call(functools.partial(feed_kernel, steps), grid=(steps,), in_s...  58.5 us
    psum x1, blocking collectives, on_device(): lax.psum((jnp.sum(grad_ln * normed, axis=0), jnp.sum(grad_ln, axis=0), sm...  37.7 us
    pallas_call x1, Pallas kernels, attend_back(): pl.pallas_call(functools.partial(attend_back_kernel, block), out_shape=(j...  32.5 us
    pallas_call x1, Pallas kernels, attend(): pl.pallas_call(functools.partial(attend_kernel, block), out_shape=(jax.Sh...  15.5 us
    dot_general x3, matrix products, dot(): return lax.dot_general(left, right, dims, preferred_element_type=F32)  15.4 us
    unnamed x68, local copies, waits for them, and re-layouts  11.4 us
  transfers between devices with their start and end apart: 13, of which 5 were waited for; matrix products, arithmetic and copies ran while one was open for 11% of the time, Pallas kernels for 13%

profile of v1, /device:TPU:0, one launch (start us, length us, event | category | flops | bytes accessed | tf_op | source)
XLA Modules:
  0.0 437.7 jit_solution(14563215621500187610)
XLA Ops:
  8.3 1.9 copy.38.wv
  10.1 2.2 copy.37.first
  12.4 1.3 reshape.93.gain
  13.6 1.3 reshape.94.bias
  14.9 1.2 reshape.95.bq
  16.1 1.2 reshape.96.bv
  18.0 10.8 %project.1 = (bf16[2048,768]{1,0:T(8,128)(2,1)}, bf16[384,2048]{1,0:T(8,128)(2,1)}, bf16[2048,384]{1,0:T(8,128)(2,1)}, bf16[384,2048]{1,0:T(8,128)(2,1)}, bf16[2...) custom-call(s32[1]{0:T(128)} %bitcast.place, bf16[1024,768]{1,0:T(8,128)(2,1)} %x.1, ...), custom_call_target="tpu_custom_call" | custom-call | tf_op jit(solution)/shard_map/project/pallas_call | solution.py:84
  28.9 15.5 %attend.1 = (bf16[384,2048]{1,0:T(8,128)(2,1)}, f32[6,1,2048]{2,1,0:T(1,128)}) custom-call(s32[1]{0:T(128)S(6)} %copy.46.split, bf16[384,2048]{1,0:T(8,128)(2,1)} %get-tuple-element.37.qt, bf16[2048,384]{1,0:T(8,128)(2,1)} %get-tuple-element.38.k, bf16[384,2048]{1,0:T(8,128)(2,1)} %get-tuple-element.39.vt), custom_call_target="tpu_custom_call" | custom-call | tf_op jit(solution)/shard_map/attend/pallas_call | solution.py:167
  44.3 2.4 constant_dynamic-slice_fusion
  47.5 0.6 reshape.101.bias_d
  48.1 0.6 reshape.97.bias_o
  48.7 0.6 reshape.98.gain
  49.2 0.6 reshape.99.bias
  49.9 0.8 copy-done.13
  51.0 1.1 copy-done.4
  52.1 58.5 %feed.1 = (bf16[1024,768]{1,0:T(8,128)(2,1)}, f32[1024,768]{1,0:T(8,128)}, bf16[768,1024]{1,0:T(8,128)(2,1)}, bf16[2,768,1536]{2,1,0:T(8,128)(2,1)}, bf16[2,1536...) custom-call(bf16[1024,768]{1,0:T(8,128)(2,1)} %x.1, ...), custom_call_target="tpu_custom_call" | custom-call | tf_op jit(solution)/shard_map/feed/pallas_call | solution.py:393
  110.7 3.4 slice_bitcast_fusion
  114.4 1.1 slice.77
  115.7 1.0 fusion.26
  117.1 1.5 slice_bitcast_fusion.1
  118.8 0.6 collective-permute-done.8
  119.4 1.0 add_convert_fusion
  120.6 0.9 copy-done.9
  121.4 32.5 %attend_back.1 = (bf16[384,2048]{1,0:T(8,128)(2,1)}, bf16[384,2048]{1,0:T(8,128)(2,1)}, f32[384,2048]{1,0:T(8,128)}) custom-call(s32[1]{0:T(128)S(6)} %copy.46.split, s32[1]{0:T(128)} %bitcast.place, bf16[384,2048]{1,0:T(8,128)(2,1)} %get-tuple-element.37.qt, bf16[2048,384]{1,0:T(8,128)(2,1)} %get-tuple-element.38.k, ...), custom_call_target="tpu_custom_call" | custom-call | tf_op jit(solution)/shard_map/attend_back/pallas_call | solution.py:257
  154.0 1.7 slice.110
  155.7 2.3 convert_reduce_fusion
  158.1 4.3 convolution_convert_fusion
  162.4 2.0 fusion
  164.4 3.7 fusion.1
  168.1 1.0 copy-done.6
  169.5 4.7 %fusion.19 = bf16[1024,768]{1,0:T(8,128)(2,1)} fusion(bf16[960,2048]{1,0:T(8,128)(2,1)} %copy-done.1, s32[]{:T(128)S(6)} %select_n.9, bf16[768,192]{1,0:T(8,128)(2,1)S(1)} %copy-done.6, bf16[768,384]{1,0:T(8,128)(2,1)S(1)} %copy-done.12, bf16[768,384]{1,0:T(8,128)(2,1)S(1)} %copy-done.11), kind=kOutput, calls=%fused_computation.27 | convolution fusion | flops 1515159552 | bytes 5013508 | tf_op jit(solution)/shard_map/dot_general | solution.py:23
  174.8 0.6 fusion.12
  175.7 1.9 collective-permute-done.10
  177.6 101.2 %all-reduce.1 = (f32[960]{0:T(1024)S(1)}, f32[1536]{0:T(1024)}) all-reduce(f32[960]{0:T(1024)S(1)} %get-tuple-element.93, f32[1536]{0:T(1024)S(1)} %add.63), channel_id=1, replica_groups=mesh['dp'=16,'tensor'=2] {'dp'}, use_global_device_ids=true, to_apply=%region_10.0 | all-reduce | flops 2496 | bytes 19968 | tf_op jit(solution)/shard_map/psum | solution.py:469
  278.8 0.6 slice.72
  279.9 2.7 slice_bitcast_fusion.2
  282.6 6.4 %fusion.11 = (f32[768]{0:T(1024)S(1)}, f32[1024]{0:T(1024)S(1)}, f32[1024]{0:T(1024)S(1)}, f32[768]{0:T(1024)S(1)}, f32[1024,768]{1,0:T(8,128)}) fusion(bf16[1024,768]{1,0:T(8,128)(2,1)S(1)} %copy-done, f32[1024]{0:T(1024)S(1)} %add_rsqrt_fusion, f32[1024]{0:T(1024)S(1)} %broadcast_multiply_fusion.2, f32[768]{0:T(1024)S(1)} %convert_element_type.67, ...), kind=kOutput, calls=%fused_computation.17 | convolution fusion | flops 1523806720 | bytes 9757700 | tf_op jit(solution)/shard_map/dot_general | solution.py:23
  289.0 37.7 %all-reduce = (f32[768]{0:T(1024)}, f32[768]{0:T(1024)}, f32[4,768]{1,0:T(4,128)S(1)}) all-reduce(f32[768]{0:T(1024)S(1)} %get-tuple-element.74, f32[768]{0:T(1024)S(1)} %get-tuple-element.77, f32[4,768]{1,0:T(4,128)S(1)} %slice.78), channel_id=1, replica_groups=mesh['dp'=16,'tensor'=2] {'dp','tensor'}, use_global_device_ids=true, to_apply=%region_5.0 | all-reduce | flops 4608 | bytes 36864 | tf_op jit(solution)/shard_map/psum | solution.py:470
  326.7 0.6 slice_reduce_fusion.2
  327.3 4.6 %fusion.10 = f32[1024,768]{1,0:T(8,128)} fusion(f32[1024,768]{1,0:T(8,128)} %get-tuple-element.42, bf16[1024,768]{1,0:T(8,128)(2,1)S(1)} %copy-done, f32[1024,768]{1,0:T(8,128)} %get-tuple-element.101, f32[1024]{0:T(1024)S(1)} %get-tuple-element.102, f32[1024]{0:T(1024)S(1)} %get-tuple-element.103, f32[768]{0:T(1024)S(1)} %convert_element_type.67, ...), kind=kLoop, calls=%fused_computation.16 | loop fusion | flops 7077888 | bytes 11029504 | tf_op jit(solution)/shard_map/add | solution.py:463
  331.9 85.8 %all-reduce.5.cloned.1.call-done = (bf16[768,960]{0,1:T(8,128)(2,1)}, bf16[384,768]{1,0:T(8,128)(2,1)}, bf16[768,1536]{1,0:T(8,128)(2,1)}, bf16[1536,768]{1,0:T(8,128)(2,1)}) async-done(((bf16[768,960]{0,1:T(8,128)(2,1)}, bf16[384,768]{1,0:T(8,128)(2,1)}, bf16[768,1536]{1,0:T(8,128)(2,1)}, bf16[1536,768]{1,0:T(8,128)(2,1)}), (bf16[768,960]{0,1:T(8,128)(2,1)}, bf16[384,768]{1,0:T(8,128)(2,1)}, ...) | async-done | bytes 6782992 | tf_op jit(solution)/shard_map/psum | solution.py:466
  417.8 1.6 fusion.27
  419.3 1.8 slice.92
  421.2 2.8 convert_element_type.79
  424.0 2.5 convert_element_type.84
  426.5 1.4 copy.40
  427.9 1.4 copy.41
  429.3 1.1 convert_element_type.74
  (97 shorter events, 5.3 us)
Async XLA Ops:
  7.2 410.6 %all-reduce.5.cloned.1.call-start = ((), (), s32[]{:S(2)}) async-start(), calls=%async_computation | async-start | bytes 13565952 | tf_op jit(solution)/shard_map/psum | solution.py:466
  7.2 10.8 %collective-permute-start = (bf16[1024,768]{1,0:T(8,128)(2,1)}, bf16[1024,768]{1,0:T(8,128)(2,1)}, u32[]{:S(2)}, u32[]{:S(2)}) collective-permute-start(bf16[1024,768]{1,0:T(8,128)(2,1)} %x.1), channel_id=1, source_target_pairs={{0,1},{1,0},{2,3},{3,2},{4,5},{5,4},{6,7},{7,6},{8,9},{9,8},{10,11... | collective-permute-start | bytes 4718600 | tf_op jit(solution)/shard_map/ppermute | solution.py:414
  7.8 42.2 %collective-permute-start.3 = (bf16[768,1536]{1,0:T(8,128)(2,1)}, bf16[768,1536]{1,0:T(8,128)(2,1)S(1)}, u32[]{:S(2)}, u32[]{:S(2)}) collective-permute-start(bf16[768,1536]{1,0:T(8,128)(2,1)} %up_own.1), channel_id=1, source_target_pairs={{0,1},{1,0},{2,3},{3,2},{4,5},{5,4},{6,7},{7,6},{8,9},{9,8},{10,11... | collective-permute-start | bytes 7077896 | tf_op jit(solution)/shard_map/ppermute | solution.py:414
  7.8 42.9 %collective-permute-start.5 = (bf16[1536,768]{1,0:T(8,128)(2,1)}, bf16[1536,768]{1,0:T(8,128)(2,1)}, u32[]{:S(2)}, u32[]{:S(2)}) collective-permute-start(bf16[1536,768]{1,0:T(8,128)(2,1)} %down_own.1), channel_id=1, source_target_pairs={{0,1},{1,0},{2,3},{3,2},{4,5},{5,4},{6,7},{7,6},{8,9},{9,8},{10,11... | collective-permute-start | bytes 7077896 | tf_op jit(solution)/shard_map/ppermute | solution.py:414
  28.8 18.5 %copy-start.20 = (bf16[1536]{0:T(1024)(128)(2,1)S(1)}, bf16[1536]{0:T(1024)(128)(2,1)}, u32[]{:S(2)}) copy-start(bf16[1536]{0:T(1024)(128)(2,1)} %param.34) | copy-start | bytes 9220
  28.8 18.7 %copy-start.21 = (bf16[768]{0:T(1024)(128)(2,1)S(1)}, bf16[768]{0:T(1024)(128)(2,1)}, u32[]{:S(2)}) copy-start(bf16[768]{0:T(1024)(128)(2,1)} %param.36) | copy-start | bytes 4612
  28.8 19.2 %copy-start.22 = (bf16[768]{0:T(1024)(128)(2,1)S(1)}, bf16[768]{0:T(1024)(128)(2,1)}, u32[]{:S(2)}) copy-start(bf16[768]{0:T(1024)(128)(2,1)} %param.30) | copy-start | bytes 4612
  28.8 19.8 %copy-start.23 = (bf16[768]{0:T(1024)(128)(2,1)S(1)}, bf16[768]{0:T(1024)(128)(2,1)}, u32[]{:S(2)}) copy-start(bf16[768]{0:T(1024)(128)(2,1)} %param.31) | copy-start | bytes 4612
  28.9 20.4 %copy-start.24 = (bf16[768]{0:T(1024)(128)(2,1)S(1)}, bf16[768]{0:T(1024)(128)(2,1)}, u32[]{:S(2)}) copy-start(bf16[768]{0:T(1024)(128)(2,1)} %param.32) | copy-start | bytes 4612
  44.3 2.5 copy-start.10
  46.8 3.1 collective-permute-start.1
  46.9 3.0 collective-permute-start.2
  47.3 3.4 copy-start.15
  47.3 2.6 collective-permute-start.4
  49.9 0.8 copy-start.18
  49.9 0.8 copy-start.13
  49.9 1.1 copy-start.8
  50.7 1.4 copy-start.4
  110.7 5.1 %copy-start.5 = (bf16[768,1024]{1,0:T(8,128)(2,1)S(1)}, bf16[768,1024]{1,0:T(8,128)(2,1)}, u32[]{:S(2)}) copy-start(bf16[768,1024]{1,0:T(8,128)(2,1)} %get-tuple-element.45) | copy-start | bytes 4718596
  110.7 6.4 %slice-start = ((s8[4718592]{0:T(1024)(128)(4,1)}), s8[4194304]{0:T(1024)(128)(4,1)S(1)}, s32[]{:S(2)}) async-start(s8[4718592]{0:T(1024)(128)(4,1)} %bitcast.15), calls=%async_computation.1 | async-start | bytes 8388608
  110.7 6.4 %slice-start.1 = ((s8[4718592]{0:T(1024)(128)(4,1)}), s8[524288]{0:T(1024)(128)(4,1)S(1)}, s32[]{:S(2)}) async-start(s8[4718592]{0:T(1024)(128)(4,1)} %bitcast.15), calls=%async_computation.2 | async-start | bytes 1048576
  114.1 48.3 %collective-permute-start.11 = (bf16[1536,768]{1,0:T(8,128)(2,1)}, bf16[1536,768]{1,0:T(8,128)(2,1)S(1)}, u32[]{:S(2)}, u32[]{:S(2)}) collective-permute-start(bf16[1536,768]{1,0:T(8,128)(2,1)} %slice_bitcast_fusion), channel_id=1, source_target_pairs={{0,1},{1,0},{2,3},{3,2},{4,5},{5,4},{6,7},{7,6},{8,9},{9,8},{10,11... | collective-permute-start | bytes 7077896 | tf_op jit(solution)/shard_map/ppermute | solution.py:414
  115.5 4.0 collective-permute-start.8
  116.7 2.7 copy-start.7
  116.8 3.8 collective-permute-start.6
  118.6 45.8 %collective-permute-start.9 = (bf16[768,1536]{1,0:T(8,128)(2,1)}, bf16[768,1536]{1,0:T(8,128)(2,1)}, u32[]{:S(2)}, u32[]{:S(2)}) collective-permute-start(bf16[768,1536]{1,0:T(8,128)(2,1)} %slice_bitcast_fusion.1), channel_id=1, source_target_pairs={{0,1},{1,0},{2,3},{3,2},{4,5},{5,4},{6,7},{7,6},{8,9},{9,8},{10,11... | collective-permute-start | bytes 7077896 | tf_op jit(solution)/shard_map/ppermute | solution.py:414
  120.6 0.9 copy-start.9
  154.0 4.1 copy-start.25
  155.7 6.7 %slice-start.4 = ((s8[4718592]{0:T(1024)(128)(4,1)}), s8[4194304]{0:T(1024)(128)(4,1)S(1)}, s32[]{:S(2)}) async-start(s8[4718592]{0:T(1024)(128)(4,1)} %bitcast.19), calls=%async_computation.5 | async-start | bytes 8388608
  155.7 8.7 %slice-start.2 = ((s8[4718592]{0:T(1024)(128)(4,1)}), s8[4194304]{0:T(1024)(128)(4,1)S(1)}, s32[]{:S(2)}) async-start(s8[4718592]{0:T(1024)(128)(4,1)} %bitcast.17), calls=%async_computation.3 | async-start | bytes 8388608
  158.0 4.3 copy-start.1
  158.1 4.3 slice-start.5
  158.1 6.3 %slice-start.3 = ((s8[4718592]{0:T(1024)(128)(4,1)}), s8[524288]{0:T(1024)(128)(4,1)S(1)}, s32[]{:S(2)}) async-start(s8[4718592]{0:T(1024)(128)(4,1)} %bitcast.17), calls=%async_computation.4 | async-start | bytes 1048576
  168.1 1.0 copy-start.6
  168.1 1.2 copy-start.11
  168.1 1.4 copy-start.12
  169.5 5.0 %copy-start = (bf16[1024,768]{1,0:T(8,128)(2,1)S(1)}, bf16[1024,768]{1,0:T(8,128)(2,1)}, u32[]{:S(2)}) copy-start(bf16[1024,768]{1,0:T(8,128)(2,1)} %x.1) | copy-start | bytes 4718596
  174.2 1.2 copy-start.16
  174.2 1.5 copy-start.17
  174.2 1.5 copy-start.19
  174.2 108.5 %collective-permute-start.7 = (bf16[1024,768]{1,0:T(8,128)(2,1)}, bf16[1024,768]{1,0:T(8,128)(2,1)}, u32[]{:S(2)}, u32[]{:S(2)}) collective-permute-start(bf16[1024,768]{1,0:T(8,128)(2,1)} %fusion.19), channel_id=1, source_target_pairs={{0,1},{1,0},{2,3},{3,2},{4,5},{5,4},{6,7},{7,6},{8,9},{9,8},{10,11... | collective-permute-start | bytes 4718600 | tf_op jit(solution)/shard_map/ppermute | solution.py:414
  175.4 2.2 collective-permute-start.10
  417.8 3.4 copy-start.3
  421.2 2.8 copy-start.2
  426.5 2.8 copy-start.14
Sparse Core Ops, SparseCore 0:
  168.2 249.4 all-reduce.4

commit v2 on v1

v2 whole, which is shorter than its diff:
```python
import functools

import jax
import jax.numpy as jnp
from jax import lax
from jax.experimental import pallas as pl
from jax.experimental.pallas import tpu as pltpu
from jax.sharding import PartitionSpec as P

HEAD_DIM = 64
NORM_EPS = 1e-05
GELU_ROOT = 0.7978845608028654
GELU_CUBE = 0.044715
NN = (((1,), (0,)), ((), ()))
NT = (((1,), (1,)), ((), ()))
TN = (((0,), (0,)), ((), ()))
F32 = jnp.float32
BF16 = jnp.bfloat16
VMEM_LIMIT = 60 << 20
MESH = pl.DeviceIdType.MESH


def dot(left, right, dims=NN):
    return lax.dot_general(left, right, dims, preferred_element_type=F32)


def whole(array):
    return pl.BlockSpec(array.shape, lambda *_, nd=array.ndim: (0,) * nd)


def whole_shape(shape):
    return pl.BlockSpec(shape, lambda *_, nd=len(shape): (0,) * nd)


def row_normalize(rows):
    centered = rows - jnp.mean(rows, axis=1, keepdims=True)
    inverse = lax.rsqrt(jnp.mean(centered * centered, axis=1, keepdims=True) + NORM_EPS)
    return centered * inverse, inverse


def row_normalize_back(scaled, normed, inverse):
    return inverse * (
        scaled
        - jnp.mean(scaled, axis=1, keepdims=True)
        - normed * jnp.mean(scaled * normed, axis=1, keepdims=True)
    )


AXES = ("x", "y", "z")
SIZE = {"x": 2, "y": 2, "z": 4}


class Place:
    def __init__(self, row_chips):
        index = lax.axis_index("dp")
        self.core = lax.axis_index("tensor")
        self.wide = row_chips
        self.index = index
        self.x = lax.rem(index, row_chips)
        self.y = lax.rem(index // row_chips, row_chips)
        self.z = index // (row_chips * row_chips)
        self.at = {"x": lax.rem(self.x, 2), "y": lax.rem(self.y, 2), "z": self.z}

    def peer(self, axis, step):
        size = SIZE[axis]
        spot = lax.rem(self.at[axis] + step, size)
        stride = {"x": 1, "y": self.wide, "z": self.wide * self.wide}[axis]
        return spot, (self.index + (spot - self.at[axis]) * stride, self.core)

    def twin(self):
        return (self.index, 1 - self.core)

    def others(self):
        return [self.twin()] + [self.peer(a, k)[1] for a in AXES for k in range(1, SIZE[a])]


def greet(place):
    barrier = pltpu.get_barrier_semaphore()
    devices = place.others()
    for device in devices:
        pl.semaphore_signal(barrier, inc=1, device_id=device, device_id_type=MESH)
    return lambda: pl.semaphore_wait(barrier, len(devices))


class Sum:
    def __init__(self, place, order, held, slots, result, sems):
        self.place, self.order, self.held = place, order, held
        self.slots, self.result, self.sems = slots, result, sems
        self.rows = (held if held is not None else result).shape[0]

    def region(self, depth):
        start, size = 0, self.rows
        for axis in self.order[:depth]:
            size //= SIZE[axis]
            start = start + self.place.at[axis] * size
        return start, size

    def span(self, depth):
        start, size = self.region(depth)
        return pl.ds(pl.multiple_of(start, 16) if depth else start, size)

    def first_sem(self, gather, stage):
        count = 0
        for axis in self.order[:stage]:
            count += SIZE[axis] - 1
        return count + (5 if gather else 0)

    def scatter_copies(self, stage):
        axis = self.order[stage]
        start, size = self.region(stage)
        piece = size // SIZE[axis]
        base = self.first_sem(False, stage)
        copies = []
        for step in range(1, SIZE[axis]):
            spot, device = self.place.peer(axis, step)
            copies.append(
                pltpu.make_async_remote_copy(
                    src_ref=self.held.at[pl.ds(pl.multiple_of(start + spot * piece, 16), piece), :],
                    dst_ref=self.slots[stage].at[step - 1],
                    send_sem=self.sems.at[0, base + step - 1],
                    recv_sem=self.sems.at[1, base + step - 1],
                    device_id=device,
                    device_id_type=MESH,
                )
            )
        return copies

    def scatter_end(self, stage):
        for copy in self.scatter_copies(stage):
            copy.wait()
        span = self.span(stage + 1)
        total = self.held[span, :].astype(F32)
        for step in range(SIZE[self.order[stage]] - 1):
            total = total + self.slots[stage][step].astype(F32)
        self.held[span, :] = total.astype(BF16)

    def gather_copies(self, stage, source):
        axis = self.order[stage]
        span = self.span(stage + 1)
        base = self.first_sem(True, stage)
        copies = []
        origin = self.result if source is None else source
        for step in range(1, SIZE[axis]):
            _, device = self.place.peer(axis, step)
            copies.append(
                pltpu.make_async_remote_copy(
                    src_ref=origin.at[span, :],
                    dst_ref=self.result.at[span, :],
                    send_sem=self.sems.at[0, base + step - 1],
                    recv_sem=self.sems.at[1, base + step - 1],
                    device_id=device,
                    device_id_type=MESH,
                )
            )
        if source is not None:
            copies.append(
                pltpu.make_async_copy(
                    source.at[span, :], self.result.at[span, :], self.sems.at[0, 10]
                )
            )
        return copies

    def run(self, action, source=None):
        verb, letter = action
        gather = letter in "cba"
        stage = "abc".index(letter) if gather else "ABC".index(letter)
        if gather:
            for copy in self.gather_copies(stage, source):
                copy.start() if verb == "s" else copy.wait()
        elif verb == "s":
            for copy in self.scatter_copies(stage):
                copy.start()
        else:
            self.scatter_end(stage)


def slot_shapes(order, rows, cols, stages="ABC"):
    shapes = []
    for letter, axis in zip("ABC", order):
        rows //= SIZE[axis]
        if letter in stages:
            shapes.append((SIZE[axis] - 1, rows, cols))
    return shapes


def as_slots(refs, stages="ABC"):
    refs = list(refs)
    return [refs.pop(0) if letter in stages else None for letter in "ABC"]


def project_kernel(
    x, first_t, gain, bias, wq, bq, wk, wv_t, bv, ln, qt, k, kt, v, vt,
    x_other, weights, s_ln, s_qt, s_k, s_kt, s_v, s_vt, pair_sems, out_sems,
):
    rows = x.shape[0]
    heads, fresh = wq.shape[1], wv_t.shape[0]
    core = lax.axis_index("tensor")
    twin = (lax.axis_index("dp"), 1 - core)
    barrier = pltpu.get_barrier_semaphore()
    pl.semaphore_signal(barrier, inc=1, device_id=twin, device_id_type=MESH)
    weights[:, :heads] = wq[...]
    weights[:, heads : 2 * heads] = wk[...]
    weights[:, 2 * heads :] = wv_t[...].T
    pl.semaphore_wait(barrier, 1)
    send = pltpu.make_async_remote_copy(
        src_ref=x, dst_ref=x_other, send_sem=pair_sems.at[0], recv_sem=pair_sems.at[1],
        device_id=twin, device_id_type=MESH,
    )
    send.start()
    gain_row = gain[...].astype(F32).reshape(1, -1)
    bias_row = bias[...].astype(F32).reshape(1, -1)
    bq_row = bq[...].astype(F32).reshape(1, -1)
    bv_row = bv[...].astype(F32).reshape(1, -1)
    copies = []
    for part, source in enumerate((x, x_other)):
        if part:
            send.wait_recv()
        spot = pl.multiple_of((core if part == 0 else 1 - core) * rows, rows)
        normed, _ = row_normalize(source[...].astype(F32))
        low = (normed * gain_row + bias_row).astype(BF16)
        s_ln[part] = low
        product = dot(low, weights[...])
        queries = (product[:, :heads] + bq_row).astype(BF16).astype(F32) * HEAD_DIM ** (-0.5)
        s_qt[part] = queries.astype(BF16).T
        keys = product[:, heads : 2 * heads].astype(BF16)
        s_k[part] = keys
        s_kt[part] = keys.T
        values = (product[:, 2 * heads :] + bv_row).astype(BF16)
        reused = first_t[:, pl.ds(spot, rows)]
        s_vt[part, :fresh] = values.T
        s_vt[part, fresh:] = reused
        s_v[part] = jnp.concatenate([values, reused.T], axis=1)
        targets = (
            (s_ln, ln.at[pl.ds(spot, rows), :]),
            (s_qt, qt.at[:, pl.ds(spot, rows)]),
            (s_k, k.at[pl.ds(spot, rows), :]),
            (s_kt, kt.at[:, pl.ds(spot, rows)]),
            (s_v, v.at[pl.ds(spot, rows), :]),
            (s_vt, vt.at[:, pl.ds(spot, rows)]),
        )
        for i, (held, target) in enumerate(targets):
            copy = pltpu.make_async_copy(held.at[part], target, out_sems.at[part, i])
            copy.start()
            copies.append(copy)
    send.wait_send()
    for copy in copies:
        copy.wait()


def project(x, first_t, gain, bias, wq, bq, wk, wv_t, bv):
    rows, width = x.shape
    heads = wq.shape[1]
    tall, flat = (rows, heads), (heads, rows)
    vmem = pl.BlockSpec(memory_space=pltpu.VMEM)
    shapes = ((2 * rows, width), (heads, 2 * rows), (2 * rows, heads)) + (
        (heads, 2 * rows), (2 * rows, heads), (heads, 2 * rows),
    )
    scratch = [(rows, width), (width, 2 * heads + wv_t.shape[0])]
    scratch += [(2,) + s for s in ((rows, width), flat, tall, flat, tall, flat)]
    return pl.pallas_call(
        project_kernel,
        out_shape=[jax.ShapeDtypeStruct(s, BF16) for s in shapes],
        in_specs=[vmem] * 9,
        out_specs=[pl.BlockSpec(memory_space=pl.ANY)] * 6,
        scratch_shapes=[pltpu.VMEM(s, BF16) for s in scratch]
        + [pltpu.SemaphoreType.DMA((2,)), pltpu.SemaphoreType.DMA((2, 6))],
        compiler_params=pltpu.CompilerParams(
            vmem_limit_bytes=VMEM_LIMIT, collective_id=1, has_side_effects=True
        ),
        name="project",
    )(x, first_t, gain, bias, wq, bq, wk, wv_t, bv)


def causal(size):
    keys = lax.broadcasted_iota(jnp.int32, (size, size), 0)
    return keys <= lax.broadcasted_iota(jnp.int32, (size, size), 1)


def query_blocks(tokens, block, two_docs, body):
    half = tokens // 2
    for start in range(0, tokens, block):
        if start < half:
            body(start, 0)
        else:

            @pl.when(two_docs)
            def _():
                body(start, half)

            @pl.when(jnp.logical_not(two_docs))
            def _():
                body(start, 0)


def attend_kernel(block, split, qt, k, vt, attended, lse, sums):
    width, tokens = qt.shape
    two_docs = split[0] < tokens
    ones = (lax.broadcasted_iota(jnp.int32, (16, tokens), 0) == 0).astype(BF16)
    sums[0, HEAD_DIM:, :] = ones
    sums[1, HEAD_DIM:, :] = ones

    def pair_step(pair, _):
        col = pl.multiple_of(pair * 2 * HEAD_DIM, 2 * HEAD_DIM)
        sums[0, :HEAD_DIM, :] = vt[pl.ds(col, HEAD_DIM), :]
        sums[1, :HEAD_DIM, :] = vt[pl.ds(col + HEAD_DIM, HEAD_DIM), :]
        owner = lax.broadcasted_iota(jnp.int32, (2 * HEAD_DIM, block), 0) // HEAD_DIM

        def body(start, low):
            stop = start + block
            inner = start - low
            queries = qt[pl.ds(col, 2 * HEAD_DIM), start:stop]
            keys = k[low:stop, pl.ds(col, 2 * HEAD_DIM)]
            scores = [
                dot(keys, jnp.where(owner == j, queries, jnp.zeros_like(queries))) for j in range(2)
            ]
            for j in range(2):
                edge = jnp.where(causal(block), scores[j][inner:], -1e30)
                top = jnp.max(edge, axis=0, keepdims=True)
                if inner:
                    near = scores[j][:inner]
                    top = jnp.maximum(top, jnp.max(near, axis=0, keepdims=True))
                    weights = jnp.concatenate(
                        [jnp.exp(near - top).astype(BF16), jnp.exp(edge - top).astype(BF16)], axis=0
                    )
                else:
                    weights = jnp.exp(edge - top).astype(BF16)
                total = dot(sums[j, :, low:stop], weights)
                denominator = total[HEAD_DIM : HEAD_DIM + 1]
                attended[pl.ds(col + HEAD_DIM * j, HEAD_DIM), start:stop] = (
                    total[:HEAD_DIM] * (1.0 / denominator)
                ).astype(BF16)
                lse[pl.ds(pair * 2 + j, 1), :, start:stop] = (top + jnp.log(denominator))[None]

        query_blocks(tokens, block, two_docs, body)
        return 0

    lax.fori_loop(0, width // (2 * HEAD_DIM), pair_step, 0)


def attend(split, qt, k, vt, block=512):
    width, tokens = qt.shape
    vmem = pl.BlockSpec(memory_space=pltpu.VMEM)
    return pl.pallas_call(
        functools.partial(attend_kernel, block),
        out_shape=(
            jax.ShapeDtypeStruct((width, tokens), BF16),
            jax.ShapeDtypeStruct((width // HEAD_DIM, 1, tokens), F32),
        ),
        in_specs=[pl.BlockSpec(memory_space=pltpu.SMEM), vmem, vmem, vmem],
        out_specs=(vmem, vmem),
        scratch_shapes=[pltpu.VMEM((2, HEAD_DIM + 16, tokens), BF16)],
        compiler_params=pltpu.CompilerParams(vmem_limit_bytes=VMEM_LIMIT),
        name="attend",
    )(split, qt, k, vt)


def gelu_both(v):
    square = v * v
    tanh = jnp.tanh(v * (GELU_ROOT + (GELU_ROOT * GELU_CUBE) * square))
    half = 0.5 * v
    slope = 0.5 + 0.5 * tanh + half * (1.0 - tanh * tanh) * (
        GELU_ROOT + (3.0 * GELU_ROOT * GELU_CUBE) * square
    )
    return half + half * tanh, slope


SUM_ROWS = 16
ROW_BU, ROW_BU_OTHER, ROW_BQ, ROW_BV = 6, 9, 12, 13


def feed_kernel(
    row_chips, x, cot, attended, wo_own, wo_other, bias_o, gain, bias,
    up_other, up_own, bu_other, bu_own, down_other, down_own, bias_d,
    out, grad_mid, grad_att, state, grad_wo, small,
    att_own, att_other, ln, normed, inverse, total, grad_ln, att_stage, stage, held,
    slots_a, slots_b, slots_c, move_sems, pair_sems, sum_sems,
):
    step = pl.program_id(0)
    place = Place(row_chips)
    core = place.core
    rows = x.shape[0]
    heads = att_own.shape[0]
    chunk = up_own.shape[1]
    index = step // 2
    own = pl.ds(pl.multiple_of(core * rows, rows), rows)
    theirs = pl.ds(pl.multiple_of((1 - core) * rows, rows), rows)

    def to_twin(source, target, i):
        return pltpu.make_async_remote_copy(
            src_ref=source, dst_ref=target, send_sem=pair_sems.at[0, i],
            recv_sem=pair_sems.at[1, i], device_id=place.twin(), device_id_type=MESH,
        )

    def stage_copy(i):
        return to_twin(stage.at[i], held.at[i], i)

    def part(i, j):
        return Sum(
            place, ("xyz", "yxz")[j], held.at[i, j],
            [slots_a.at[i, j], slots_b.at[i, j] if i < 2 else None, slots_c.at[j] if i < 1 else None],
            state.at[i, j], sum_sems.at[i, j],
        )

    def act(i, *actions):
        for action in actions:
            for j in range(2):
                part(i, j).run(action, held.at[i, j] if action[1] == "c" else None)

    @pl.when(step == 0)
    def _():
        ready = greet(place)
        local = pltpu.make_async_copy(attended.at[:, own], att_own, move_sems.at[0])
        local.start()
        ready()
        exchange = to_twin(attended.at[:, theirs], att_other, 3)
        exchange.start()
        total[...] = x[...].astype(F32) + bias_o[...].astype(F32).reshape(1, -1)
        grad_ln[...] = jnp.zeros_like(grad_ln)
        small[...] = jnp.zeros_like(small)
        local.wait()
        total[...] += dot(att_own[...], wo_own[...], TN)
        exchange.wait()
        mid = total[...] + dot(att_other[...], wo_other[...], TN)
        total[...] = mid + bias_d[...].astype(F32).reshape(1, -1)
        norm, inv = row_normalize(mid)
        normed[...] = norm
        inverse[...] = jnp.broadcast_to(inv, inverse.shape)
        ln[...] = (
            norm * gain[...].astype(F32).reshape(1, -1) + bias[...].astype(F32).reshape(1, -1)
        ).astype(BF16)

    def weight_grads(up, bias_up, down):
        hidden = dot(ln[...], up[...]) + bias_up[
            pl.ds(pl.multiple_of(index * chunk, chunk), chunk)
        ].astype(F32).reshape(1, -1)
        activated, slope = gelu_both(hidden)
        activated = activated.astype(BF16)
        grad_hidden = (dot(cot[...], down[...], NT) * slope).astype(BF16)
        grad_down = dot(activated, cot[...], TN)
        grad_up = dot(grad_hidden, ln[...], TN)
        sums = jnp.sum(grad_hidden.astype(F32), axis=0, keepdims=True)
        return activated, grad_hidden, grad_down, grad_up, sums

    def row_terms(activated, grad_hidden, up, down):
        total[...] += dot(activated, down[...])
        grad_ln[...] += dot(grad_hidden, up[...], NT)

    @pl.when(lax.rem(step, 2) == 0)
    def _():
        activated, grad_hidden, grad_down, grad_up, sums = weight_grads(
            up_other, bu_other, down_other
        )
        stage[index, 0] = grad_down.astype(BF16)
        stage[index, 1] = grad_up.astype(BF16)
        stage_copy(index).start()
        small[pl.ds(ROW_BU_OTHER + index, 1), :chunk] = sums
        row_terms(activated, grad_hidden, up_other, down_other)

        @pl.when(step == 2)
        def _():
            act(0, "fA", "sB")

        @pl.when(step == 4)
        def _():
            act(0, "fC", "sc")
            act(1, "fA", "sB")

    @pl.when(lax.rem(step, 2) == 1)
    def _():
        activated, grad_hidden, grad_down, grad_up, sums = weight_grads(up_own, bu_own, down_own)
        stage_copy(index).wait()
        held[index, 0] = (grad_down + held[index, 0].astype(F32)).astype(BF16)
        held[index, 1] = (grad_up + held[index, 1].astype(F32)).astype(BF16)
        small[pl.ds(ROW_BU + index, 1), :chunk] = sums

        @pl.when(step == 1)
        def _():
            act(0, "sA")

        @pl.when(step == 3)
        def _():
            act(0, "fB", "sC")
            act(1, "sA")

        @pl.when(step == 5)
        def _():
            act(1, "fB")
            act(2, "sA")

        row_terms(activated, grad_hidden, up_own, down_own)

    @pl.when(step == 5)
    def _():
        grad = grad_ln[...]
        norm = normed[...]
        cot32 = cot[...].astype(F32)
        scaled = grad * gain[...].astype(F32).reshape(1, -1)
        mid = cot32 + row_normalize_back(scaled, norm, inverse[:, :1])
        grad_mid[...] = mid
        low = mid.astype(BF16)
        att_stage[1] = dot(wo_other[...], low, NT).astype(BF16)
        exchange = to_twin(att_stage.at[1], grad_att.at[:, own], 4)
        exchange.start()
        att_stage[0] = dot(wo_own[...], low, NT).astype(BF16)
        local = pltpu.make_async_copy(att_stage.at[0], grad_att.at[:, own], move_sems.at[0])
        local.start()
        out[...] = total[...].astype(BF16)
        small[0:1, :] = jnp.sum(grad * norm, axis=0, keepdims=True)
        small[1:2, :] = jnp.sum(grad, axis=0, keepdims=True)
        small[2:3, :] = jnp.sum(low.astype(F32), axis=0, keepdims=True)
        small[3:4, :] = jnp.sum(cot32, axis=0, keepdims=True)
        grad_wo[:heads] = dot(att_own[...], low).astype(BF16)
        grad_wo[heads:] = dot(att_other[...], low).astype(BF16)
        act(0, "fc")
        act(2, "fA")
        moves = [local]
        for i, depth in ((1, 2), (2, 1)):
            for j in range(2):
                span = part(i, j).span(depth)
                move = pltpu.make_async_copy(
                    held.at[i, j, span, :], state.at[i, j, span, :], move_sems.at[1 + 2 * i + j]
                )
                move.start()
                moves.append(move)
        exchange.wait()
        for move in moves:
            move.wait()


def feed(
    row_chips, x, cot, attended, wo_own, wo_other, bias_o, gain, bias,
    up_other, up_own, bu_other, bu_own, down_other, down_own, bias_d,
):
    rows, width = x.shape
    hidden = up_own.shape[1]
    heads = wo_own.shape[0]
    chunk = hidden // 3
    once = pl.Buffered(1)
    fixed = lambda s: pl.BlockSpec(s, lambda j, nd=len(s): (0,) * nd, pipeline_mode=once)
    anywhere = pl.BlockSpec(memory_space=pl.ANY)
    up_spec = pl.BlockSpec((width, chunk), lambda j: (0, j // 2))
    down_spec = pl.BlockSpec((chunk, width), lambda j: (j // 2, 0))
    operands = (
        x, cot, attended, wo_own, wo_other, bias_o, gain, bias,
        up_other, up_own, bu_other, bu_own, down_other, down_own, bias_d,
    )
    specs = [fixed(a.shape) for a in operands]
    specs[2] = anywhere
    specs[8] = specs[9] = up_spec
    specs[12] = specs[13] = down_spec
    results = [
        ((rows, width), BF16),
        ((rows, width), F32),
        ((heads, 2 * rows), BF16),
        ((3, 2, chunk, width), BF16),
        ((2 * heads, width), BF16),
        ((SUM_ROWS, width), F32),
    ]
    out_specs = [fixed(s) for s, _ in results]
    out_specs[2] = out_specs[3] = anywhere
    part = slot_shapes("xyz", chunk, width)
    return pl.pallas_call(
        functools.partial(feed_kernel, row_chips),
        grid=(6,),
        in_specs=specs,
        out_specs=out_specs,
        out_shape=[jax.ShapeDtypeStruct(s, t) for s, t in results],
        scratch_shapes=[
            pltpu.VMEM((heads, rows), BF16),
            pltpu.VMEM((heads, rows), BF16),
            pltpu.VMEM((rows, width), BF16),
            pltpu.VMEM((rows, width), F32),
            pltpu.VMEM((rows, 128), F32),
            pltpu.VMEM((rows, width), F32),
            pltpu.VMEM((rows, width), F32),
            pltpu.VMEM((2, heads, rows), BF16),
            pltpu.VMEM((3, 2, chunk, width), BF16),
            pltpu.VMEM((3, 2, chunk, width), BF16),
            pltpu.VMEM((3, 2) + part[0], BF16),
            pltpu.VMEM((2, 2) + part[1], BF16),
            pltpu.VMEM((2,) + part[2], BF16),
            pltpu.SemaphoreType.DMA((7,)),
            pltpu.SemaphoreType.DMA((2, 5)),
            pltpu.SemaphoreType.DMA((3, 2, 2, 11)),
        ],
        compiler_params=pltpu.CompilerParams(
            vmem_limit_bytes=VMEM_LIMIT, collective_id=2, has_side_effects=True,
            dimension_semantics=("arbitrary",),
        ),
        name="feed",
    )(*operands)


def extra_rows(row, fourth):
    high = row.astype(BF16).astype(F32)
    middle = (row - high).astype(BF16).astype(F32)
    low = row - high - middle
    index = lax.broadcasted_iota(jnp.int32, (HEAD_DIM, row.shape[1]), 0)
    rest = jnp.where(index == 2, low, jnp.where(index == 3, fourth, 0.0))
    return jnp.where(index == 0, high, jnp.where(index == 1, middle, rest)).astype(BF16)


BACK_PLAN = {
    "start": ((0, "sb"), (2, "sB"), (1, "sC")),
    (0, 2): ((0, "fb"), (0, "sa"), (2, "fB")),
    (0, 3): ((1, "fC"), (1, "sc"), (2, "sC")),
    (1, 1): ((0, "fa"), (3, "sA")),
    (1, 2): ((1, "fc"), (1, "sb")),
    (1, 3): ((3, "fA"), (3, "sB"), (1, "fb"), (1, "sa")),
    (2, 1): ((2, "fC"), (2, "sc"), (3, "fB"), (3, "sC")),
    (2, 2): ((1, "fa"), (4, "sA")),
    (2, 3): ((2, "fc"), (2, "sb"), (4, "fA"), (4, "sB")),
    "e0": ((5, "sA"),),
    "e1": ((3, "fC"), (3, "sc"), (2, "fb"), (2, "sa"), (4, "fB"), (4, "sC")),
    "e2": ((5, "fA"), (5, "sB"), (3, "fc"), (3, "sb")),
    "e3": ((4, "fC"), (4, "sc"), (5, "fB"), (5, "sC"), (3, "fb"), (3, "sa")),
    "e4": ((2, "fa"), (4, "fc"), (4, "sb")),
    "e5": ((5, "fC"), (5, "sc"), (4, "fb"), (4, "sa")),
    "e6": ((3, "fa"), (5, "fc"), (5, "sb")),
    "e7": ((5, "fb"), (5, "sa")),
    "e8": ((4, "fa"), (5, "fa")),
}


def attend_back_kernel(
    row_chips, block, split, qt, k, kt, v, do, attended, lse, ln, x, gain, wq, wk, wv_t, grad_wo,
    small, state,
    back, dv_first, sums, red_down, red_up, red_wo, red_low, red_v, red_last,
    stack, q_aug, d_aug, k_aug, v_aug, dk_sum, dv_sum, weights, terms_send, terms_got,
    wo_got, held, held_wo, held_low, held_v, held_last, sums_got,
    one_c, two_b, two_c, wo_a, wo_b, wo_c, low_a, low_b, low_c, v_a, v_b, v_c,
    last_a, last_b, last_c, move_sems, pair_sems, tiny_sems, sum_sems,
):
    width, tokens = qt.shape
    half = tokens // 2
    fresh = wv_t.shape[0]
    place = Place(row_chips)
    core = place.core
    pair_width = 2 * HEAD_DIM
    own = pl.ds(pl.multiple_of(core * half, half), half)
    theirs = pl.ds(pl.multiple_of((1 - core) * half, half), half)
    orders = ("xyz", "yxz")

    def to_twin(source, target, i):
        return pltpu.make_async_remote_copy(
            src_ref=source, dst_ref=target, send_sem=pair_sems.at[0, i],
            recv_sem=pair_sems.at[1, i], device_id=place.twin(), device_id_type=MESH,
        )

    def part(i, j):
        sems = sum_sems.at[i, j]
        if i < 3:
            result = (red_down, red_up)[j].at[i]
            slots = [
                None,
                two_b.at[j] if i == 2 else None,
                (None, one_c, two_c)[i].at[j] if i else None,
            ]
            return Sum(place, orders[j], held.at[i - 1, j] if i else None, slots, result, sems)
        if i == 4:
            given = (held_low, [low_a, low_b, low_c], red_low)
            if j:
                given = (held_v, [v_a, v_b, v_c], red_v)
            return Sum(place, orders[j], given[0], given[1], given[2], sems)
        holder, slots, result = {
            3: (held_wo, [wo_a, wo_b, wo_c], red_wo),
            5: (held_last, [last_a, last_b, last_c], red_last),
        }[i]
        return Sum(place, orders[j], holder.at[j], [s.at[j] for s in slots], result.at[j], sems)

    def act(point):
        for i, action in BACK_PLAN.get(point, ()):
            for j in range(2):
                one = part(i, j)
                source = None
                if i == 0 and action[1] == "b":
                    source = state.at[0, j]
                elif action[1] == "c":
                    source = one.held
                one.run(action, source)

    loads = [
        pltpu.make_async_copy(
            state.at[i, j, part(i, j).span(depth), :],
            held.at[i - 1, j, part(i, j).span(depth), :],
            move_sems.at[2 * (i - 1) + j],
        )
        for i, depth in ((1, 2), (2, 1))
        for j in range(2)
    ]
    ready = greet(place)
    for load in loads:
        load.start()
    weights[:width] = wq[...].T
    weights[width : 2 * width] = wk[...].T
    weights[2 * width :] = wv_t[...]
    ready()
    wo_exchange = to_twin(grad_wo.at[width:, :], wo_got, 0)
    wo_exchange.start()
    for load in loads:
        load.wait()
    act("start")
    far = jnp.where(split[0] < tokens, -1e9, 0.0)
    token = lax.broadcasted_iota(jnp.int32, (1, tokens), 1)
    far_row = jnp.where(token >= half, far, 0.0)

    def weight_rows(rows):
        return dot(stack[rows, :], ln[...]).astype(BF16)

    def by_columns(target, start, values):
        cols = target.shape[2]
        for j in range(2):
            target[j, start : start + values.shape[0], :] = values[:, j * cols : (j + 1) * cols]

    def pair_step(pair, _):
        col = pl.multiple_of(pair * pair_width, pair_width)
        lane = lax.broadcasted_iota(jnp.int32, (tokens, pair_width), 1)
        key = lax.broadcasted_iota(jnp.int32, (tokens, pair_width), 0)
        within = lax.rem(lane, HEAD_DIM)
        ones = jnp.where((within < 3) | ((within == 3) & (key < half)), 1.0, 0.0).astype(BF16)
        keys = k[:, pl.ds(col, pair_width)]
        values = v[:, pl.ds(col, pair_width)]
        dk_sum[...] = jnp.zeros_like(dk_sum)
        dv_sum[...] = jnp.zeros_like(dv_sum)
        head_rows = [pl.ds(pl.multiple_of(col + HEAD_DIM * j, HEAD_DIM), HEAD_DIM) for j in range(2)]
        for j in range(2):
            mine = lane // HEAD_DIM == j
            k_aug[j] = jnp.where(mine, keys, ones)
            v_aug[j] = jnp.where(mine, values, ones)
            grad = do[head_rows[j], :]
            inner = jnp.sum(
                grad.astype(F32) * attended[head_rows[j], :].astype(F32), axis=0, keepdims=True
            )
            base, extra = HEAD_DIM * j, HEAD_DIM * (1 - j)
            q_aug[j, base : base + HEAD_DIM, :] = qt[head_rows[j], :]
            q_aug[j, extra : extra + HEAD_DIM, :] = extra_rows(
                -lse[pl.ds(pair * 2 + j, 1)][0], far_row
            )
            d_aug[j, base : base + HEAD_DIM, :] = grad
            d_aug[j, extra : extra + HEAD_DIM, :] = extra_rows(-inner, 0.0)

        for number in range(tokens // block):
            start = number * block
            stop = start + block
            for j in range(2):
                scores = dot(k_aug[j, :stop, :], q_aug[j, :, start:stop])
                grad_probs = dot(v_aug[j, :stop, :], d_aug[j, :, start:stop])
                probs = jnp.where(causal(block), jnp.exp(scores[start:]), 0.0)
                if start:
                    probs = jnp.concatenate([jnp.exp(scores[:start]), probs], axis=0)
                grad_scores = (probs * grad_probs).astype(BF16)
                probs = probs.astype(BF16)
                rows = head_rows[j]
                stack[rows, start:stop] = (
                    dot(kt[rows, :stop], grad_scores) * HEAD_DIM ** (-0.5)
                ).astype(BF16)
                dv_sum[j, :, :stop] += dot(do[rows, start:stop], probs, NT)
                dk_sum[j, :, :stop] += dot(qt[rows, start:stop], grad_scores, NT)
            for p in range(width // pair_width):
                if number < tokens // block - 1 and (p, number) in BACK_PLAN:
                    pl.when(pair == p)(functools.partial(act, (p, number)))

        for j in range(2):
            stack[pl.ds(pl.multiple_of(width + col + HEAD_DIM * j, HEAD_DIM), HEAD_DIM), :] = dk_sum[
                j
            ].astype(BF16)

        @pl.when(pair == 0)
        def _():
            stack[2 * width : 2 * width + HEAD_DIM, :] = dv_sum[0].astype(BF16)
            stack[2 * width + HEAD_DIM : 2 * width + 2 * HEAD_DIM, :] = dv_sum[1].astype(BF16)
            wo_exchange.wait()
            summed = (grad_wo[:width].astype(F32) + wo_got[...].astype(F32)).astype(BF16)
            by_columns(held_wo, 0, summed)
            for i in range(3):
                by_columns(
                    held_wo,
                    width + i * pair_width,
                    weight_rows(slice(i * width, i * width + pair_width)),
                )
            act((0, 3))

        @pl.when(pair == 1)
        def _():
            stack[2 * width + 2 * HEAD_DIM :, :] = dv_sum[0].astype(BF16)
            dv_first[:HEAD_DIM, :] = dv_sum[1]
            for i in range(2):
                held_low[i * pair_width : (i + 1) * pair_width] = weight_rows(
                    slice(i * width + pair_width, i * width + 2 * pair_width)
                )
            rest = weight_rows(slice(2 * width + 2 * HEAD_DIM, 2 * width + 3 * HEAD_DIM))
            cols = held_v.shape[1]
            held_v[...] = jnp.zeros_like(held_v)
            for j in range(2):
                held_v[HEAD_DIM * j : HEAD_DIM * (j + 1), :] = rest[:, j * cols : (j + 1) * cols]
            act((1, 3))

        @pl.when(pair == 2)
        def _():
            dv_first[HEAD_DIM : 2 * HEAD_DIM, :] = dv_sum[0]
            dv_first[2 * HEAD_DIM :, :] = dv_sum[1]
            for i in range(2):
                by_columns(
                    held_last,
                    i * pair_width,
                    weight_rows(slice(i * width + 2 * pair_width, i * width + 3 * pair_width)),
                )
            act((2, 3))

        return 0

    lax.fori_loop(0, width // pair_width, pair_step, 0)

    act("e0")
    terms_send[...] = dot(stack[:, theirs], weights[...], TN).astype(BF16)
    terms_exchange = to_twin(terms_send, terms_got, 1)
    terms_exchange.start()
    back[...] = dot(stack[:, own], weights[...], TN)
    act("e1")
    normed, inverse = row_normalize(x[...].astype(F32))
    terms_exchange.wait()
    grad = back[...] + terms_got[...].astype(F32)
    sums[...] = small[...]
    sums[4:5, :] = jnp.sum(grad * normed, axis=0, keepdims=True)
    sums[5:6, :] = jnp.sum(grad, axis=0, keepdims=True)
    biases = dot(jnp.ones((8, tokens), BF16), stack[...], NT)
    sums[ROW_BQ : ROW_BQ + 1, :width] = biases[:1, :width]
    sums[ROW_BV : ROW_BV + 1, :fresh] = biases[:1, 2 * width :]
    tiny = to_twin(sums, sums_got.at[0], 2)
    tiny.start()
    back[...] = row_normalize_back(grad * gain[...].astype(F32).reshape(1, -1), normed, inverse)
    tiny.wait()
    sums[:ROW_BU, :] = sums[:ROW_BU, :] + sums_got[0, :ROW_BU, :]
    sums[ROW_BU:ROW_BU_OTHER, :] = (
        sums[ROW_BU:ROW_BU_OTHER, :] + sums_got[0, ROW_BU_OTHER:ROW_BQ, :]
    )
    slot = 1
    points = iter(("e2", "e3", "e4"))
    for axis in AXES:
        copies = []
        for step in range(1, SIZE[axis]):
            _, device = place.peer(axis, step)
            copies.append(
                pltpu.make_async_remote_copy(
                    src_ref=sums, dst_ref=sums_got.at[slot], send_sem=tiny_sems.at[0, slot],
                    recv_sem=tiny_sems.at[1, slot], device_id=device, device_id_type=MESH,
                )
            )
            copies[-1].start()
            slot += 1
        act(next(points))
        for copy in copies:
            copy.wait()
        total = sums[...]
        for i in range(slot - len(copies), slot):
            total = total + sums_got[i]
        sums[...] = total
    for point in ("e5", "e6", "e7", "e8"):
        act(point)


def attend_back(
    row_chips, split, qt, k, kt, v, do, attended, lse, ln, x, gain, wq, wk, wv_t, grad_wo, small,
    state, block=512,
):
    width, tokens = qt.shape
    rows, model = x.shape
    fresh = wv_t.shape[0]
    pair = 2 * HEAD_DIM
    chunk = state.shape[2]
    low_rows = 2 * pair
    cols = model // 2
    vmem = pl.BlockSpec(memory_space=pltpu.VMEM)
    anywhere = pl.BlockSpec(memory_space=pl.ANY)
    results = [
        ((rows, model), F32, vmem),
        ((width - fresh, tokens), F32, vmem),
        ((SUM_ROWS, model), F32, vmem),
        ((3, chunk, model), BF16, anywhere),
        ((3, chunk, model), BF16, anywhere),
        ((2, 2 * width, cols), BF16, anywhere),
        ((low_rows, model), BF16, anywhere),
        ((low_rows, cols), BF16, anywhere),
        ((2, low_rows, cols), BF16, anywhere),
    ]
    part = slot_shapes("xyz", chunk, model)
    wo = slot_shapes("xyz", 2 * width, cols)
    low = slot_shapes("xyz", low_rows, model)
    thin = slot_shapes("xyz", low_rows, cols)
    two = lambda s: (2,) + s
    scratch = [
        ((2 * width + fresh, tokens), BF16),
        ((2, pair, tokens), BF16),
        ((2, pair, tokens), BF16),
        ((2, tokens, pair), BF16),
        ((2, tokens, pair), BF16),
        ((2, HEAD_DIM, tokens), F32),
        ((2, HEAD_DIM, tokens), F32),
        ((2 * width + fresh, model), BF16),
        ((rows, model), BF16),
        ((rows, model), BF16),
        ((width, model), BF16),
        ((2, 2, chunk, model), BF16),
        ((2, 2 * width, cols), BF16),
        ((low_rows, model), BF16),
        ((low_rows, cols), BF16),
        ((2, low_rows, cols), BF16),
        ((6, SUM_ROWS, model), F32),
        (two(part[2]), BF16),
        (two(part[1]), BF16),
        (two(part[2]), BF16),
    ]
    scratch += [(two(s), BF16) for s in wo]
    scratch += [(s, BF16) for s in low]
    scratch += [(s, BF16) for s in thin]
    scratch += [(two(s), BF16) for s in thin]
    return pl.pallas_call(
        functools.partial(attend_back_kernel, row_chips, block),
        out_shape=[jax.ShapeDtypeStruct(s, t) for s, t, _ in results],
        in_specs=[pl.BlockSpec(memory_space=pltpu.SMEM)] + [vmem] * 15 + [anywhere],
        out_specs=[spec for _, _, spec in results],
        scratch_shapes=[pltpu.VMEM(s, t) for s, t in scratch]
        + [
            pltpu.SemaphoreType.DMA((4,)),
            pltpu.SemaphoreType.DMA((2, 3)),
            pltpu.SemaphoreType.DMA((2, 6)),
            pltpu.SemaphoreType.DMA((6, 2, 2, 11)),
        ],
        compiler_params=pltpu.CompilerParams(
            vmem_limit_bytes=VMEM_LIMIT, collective_id=3, has_side_effects=True
        ),
        name="attend_back",
    )(split, qt, k, kt, v, do, attended, lse, ln, x, gain, wq, wk, wv_t, grad_wo, small, state)


def swap(array):
    return lax.ppermute(array, "tensor", [(0, 1), (1, 0)])


def across_blocks(array, row_chips):
    chips = 4 * row_chips * row_chips
    shift = 2
    while shift < row_chips:
        for stride in (shift, shift * row_chips):
            pairs = [(i, i ^ stride) for i in range(chips)]
            array = array + lax.ppermute(array, "dp", pairs)
        shift *= 2
    return array


def on_device(
    row_chips,
    input_rows, first_values, doc_split, gain_norm1, bias_norm1, w_query, bias_query, w_key,
    w_value, bias_value, w_out, bias_attn_out, gain_norm2, bias_norm2, w_up, bias_up, w_down,
    bias_down, cotangent,
):
    heads = w_query.shape[1]
    fresh = w_value.shape[1]
    hidden = w_up.shape[1]
    pair = 2 * HEAD_DIM
    wv_t = w_value.T
    ln, qt, k, kt, v, vt = project(
        input_rows, first_values.T, gain_norm1, bias_norm1, w_query, bias_query, w_key, wv_t,
        bias_value,
    )
    up, down, wo, bu, vt = lax.optimization_barrier((w_up, w_down, w_out, bias_up, vt))
    up_other, down_other, wo_other, bu_other = swap(up), swap(down), swap(wo), swap(bu)
    attended, lse = attend(doc_split, qt, k, vt)
    output, grad_middle, grad_att, state, grad_wo, small = feed(
        row_chips, input_rows, cotangent, attended, w_out, wo_other, bias_attn_out, gain_norm2,
        bias_norm2, up_other, w_up, bu_other, bias_up, down_other, w_down, bias_down,
    )
    back, dv_first, sums, red_down, red_up, red_wo, red_low, red_v, red_last = attend_back(
        row_chips, doc_split, qt, k, kt, v, grad_att, attended, lse, ln, input_rows, gain_norm1,
        w_query, w_key, wv_t, grad_wo, small, state,
    )
    red_down, red_up, red_wo, red_low, red_v, red_last, sums = [
        across_blocks(a, row_chips)
        for a in (red_down, red_up, red_wo, red_low, red_v, red_last, sums)
    ]
    red_wo = jnp.concatenate([red_wo[0], red_wo[1]], axis=1)
    red_last = jnp.concatenate([red_last[0], red_last[1]], axis=1)
    rest = jnp.concatenate([red_v[:HEAD_DIM], red_v[HEAD_DIM:pair]], axis=1)
    first = heads
    grad_q = jnp.concatenate([red_wo[first : first + pair], red_low[:pair], red_last[:pair]])
    grad_k = jnp.concatenate(
        [red_wo[first + pair : first + 2 * pair], red_low[pair:], red_last[pair:]]
    )
    grad_v = jnp.concatenate([red_wo[first + 2 * pair :], rest])
    grad_bu = sums[ROW_BU:ROW_BU_OTHER, : hidden // 3].reshape(-1)
    return (
        output,
        grad_middle + back,
        dv_first.T,
        sums[4],
        sums[5],
        grad_q.astype(F32).T,
        sums[ROW_BQ, :heads],
        grad_k.astype(F32).T,
        grad_v.astype(F32).T,
        sums[ROW_BV, :fresh],
        red_wo[:heads].astype(F32),
        sums[2],
        sums[0],
        sums[1],
        red_up.reshape(hidden, -1).astype(F32).T,
        grad_bu,
        red_down.reshape(hidden, -1).astype(F32),
        sums[3],
    )


def solution(mesh):
    row_chips = 1
    while 4 * row_chips * row_chips < mesh.shape["dp"]:
        row_chips += 1
    rows = P(("dp", "tensor"), None)
    cols = P(None, "tensor")
    split = P("tensor")
    firsts = P("dp", "tensor")
    wide = P("tensor", None)
    return jax.shard_map(
        functools.partial(on_device, row_chips),
        mesh=mesh,
        in_specs=(
            rows, firsts, P("dp"), P(), P(), cols, split, cols, cols, split, wide, P(), P(), P(),
            cols, split, wide, P(), rows,
        ),
        out_specs=(
            rows, rows, firsts, P(), P(), cols, split, cols, cols, split, wide, P(), P(), P(),
            cols, split, wide, P(),
        ),
        check_vma=False,
    )
```

time: 446 us -> 260 us (0.58)
  the two profiles are of different devices: /device:TPU:0 before, /device:TPU:24 now
where the time goes in v2:
time: 260 us; the launch traced here: 256 us
  Pallas kernels  216 us (83%)
  local copies, waits for them, and re-layouts  23 us (9%)
  other arithmetic  13.9 us (5%)
    pallas_call x1, Pallas kernels, attend_back(): pl.pallas_call(functools.partial(attend_back_kernel, row_chips, block), o...  117 us
    pallas_call x1, Pallas kernels, feed(): pl.pallas_call(functools.partial(feed_kernel, row_chips), grid=(6,), in_s...  73.5 us
    pallas_call x1, Pallas kernels, attend(): pl.pallas_call(functools.partial(attend_kernel, block), out_shape=(jax.Sh...  15.5 us
    pallas_call x1, Pallas kernels, project(): pl.pallas_call(project_kernel, out_shape=[jax.ShapeDtypeStruct(s, BF16) f...  9.9 us
    unnamed x24, local copies, waits for them, and re-layouts  7.46 us
    convert_element_type x1, other arithmetic, on_device(): red_down.reshape(hidden, -1).astype(F32)  6.79 us
    transpose x1, local copies, waits for them, and re-layouts, on_device(): red_up.reshape(hidden, -1).astype(F32)  6.04 us
  transfers between devices with their start and end apart: 4, of which 0 were waited for; matrix products, arithmetic and copies ran while one was open for 0% of the time, Pallas kernels for 6%

profile of v2, /device:TPU:24, one launch (start us, length us, event | category | flops | bytes accessed | tf_op | source)
XLA Modules:
  0.0 255.6 jit_solution(12848725200321295342)
XLA Ops:
  0.7 0.0 copy-start
  0.7 0.0 copy-start.3
  0.7 0.0 copy-start.8
  0.7 9.9 %project.1 = (bf16[2048,768]{1,0:T(8,128)(2,1)}, bf16[384,2048]{1,0:T(8,128)(2,1)}, bf16[2048,384]{1,0:T(8,128)(2,1)}, bf16[384,2048]{1,0:T(8,128)(2,1)}, bf16[2...) custom-call(bf16[1024,768]{1,0:T(8,128)(2,1)} %x.5, bf16[192,2048]{1,0:T(8,128)(2,1)} %bitcast.29, bf16[768]{0:T(1024)(128)(2,1)} %gain.5, ...), custom_call_target="tpu_custom_call" | custom-call | tf_op jit(solution)/shard_map/project/pallas_call | solution.py:260
  10.6 0.0 copy-done
  10.6 0.3 collective-permute-start.1
  10.9 0.3 collective-permute-start.3
  11.2 0.0 copy-done.3
  11.2 0.2 collective-permute-start
  11.4 0.0 copy-done.8
  11.4 0.3 collective-permute-start.2
  12.4 15.5 %attend.1 = (bf16[384,2048]{1,0:T(8,128)(2,1)}, f32[6,1,2048]{2,1,0:T(1,128)}) custom-call(s32[1]{0:T(128)S(6)} %copy.42.split, bf16[384,2048]{1,0:T(8,128)(2,1)} %get-tuple-element.46.qt, bf16[2048,384]{1,0:T(8,128)(2,1)} %get-tuple-element.47.k, bf16[384,2048]{1,0:T(8,128)(2,1)} %get-tuple-element.49.vt), custom_call_target="tpu_custom_call" | custom-call | tf_op jit(solution)/shard_map/attend/pallas_call | solution.py:343
  27.9 0.0 collective-permute-done.2.bu_other
  27.9 0.0 copy-start.9
  27.9 0.0 collective-permute-done.wo_other
  27.9 0.0 copy-start.4
  27.9 0.0 collective-permute-done.1.up_other
  27.9 0.0 collective-permute-done.3.down_other
  27.9 0.6 copy-done.9
  28.5 0.2 copy-done.4
  28.7 73.5 %feed.1 = (bf16[1024,768]{1,0:T(8,128)(2,1)}, f32[1024,768]{1,0:T(8,128)}, bf16[384,2048]{1,0:T(8,128)(2,1)}, bf16[3,2,512,768]{3,2,1,0:T(8,128)(2,1)}, bf16[768,768]{1,0:T(8,128)(2,1)}, /*index=5*/f32[16,768]{1,0:T(8,128)}) custom-call(bf16[1024,768]{1,0:T(8,128)(2,1)} %x.5, bf16[1024,768]{1,0:T(8,128)(2,1)} %cot.1, ...), custom_call_target="tpu_custom_call" | custom-call | tf_op jit(solution)/shard_map/feed/pallas_call | solution.py:562
  102.2 117.0 %attend_back.1 = (f32[1024,768]{1,0:T(8,128)}, f32[192,2048]{1,0:T(8,128)}, f32[16,768]{1,0:T(8,128)}, bf16[3,512,768]{2,1,0:T(8,128)(2,1)}, bf16[3,512,768]{2,1...) custom-call(s32[1]{0:T(128)S(6)} %copy.42.split, ...), custom_call_target="tpu_custom_call" | custom-call | tf_op jit(solution)/shard_map/attend_back/pallas_call | solution.py:917
  219.3 1.3 slice.85
  220.5 1.3 slice_reduce_fusion.6
  221.8 0.8 slice.90
  222.6 1.6 slice_reduce_fusion
  224.2 0.6 reshape.45
  224.8 1.5 fusion.17
  226.3 1.1 slice_bitcast_fusion.2
  227.3 0.0 copy-start.5
  227.4 1.4 slice_bitcast_fusion.1
  228.8 0.0 copy-done.5
  228.8 1.3 fusion.13
  230.1 1.4 copy.38
  231.5 1.4 copy.39
  232.9 6.8 %bitcast_convert_fusion = (f32[1536,768]{1,0:T(8,128)}, f32[1536,768]{1,0:T(8,128)}) fusion(bf16[3,512,768]{2,1,0:T(8,128)(2,1)} %get-tuple-element.73, bf16[3,512,768]{2,1,0:T(8,128)(2,1)} %get-tuple-element.72), kind=kLoop, calls=%fused_computation | loop fusion | flops 2359296 | bytes 14155776 | tf_op jit(solution)/shard_map/convert_element_type | solution.py:1008
  239.7 6.0 %copy.37 = f32[1536,768]{0,1:T(8,128)} copy(f32[1536,768]{1,0:T(8,128)} %get-tuple-element.110) | data formatting | bytes 9437184 | tf_op jit(solution)/shard_map/transpose | solution.py:1006
  245.7 0.0 copy-start.6
  245.7 0.0 copy-start.7
  245.7 4.9 %add.3 = f32[1024,768]{1,0:T(8,128)} add(f32[1024,768]{1,0:T(8,128)} %get-tuple-element.56, f32[1024,768]{1,0:T(8,128)} %get-tuple-element.65) | non-fusion elementwise | flops 786432 | bytes 9437184 | tf_op jit(solution)/shard_map/add | solution.py:993
  250.6 0.0 copy-start.1
  250.6 0.0 copy-done.6
  250.6 0.0 copy-done.7
  250.7 0.9 convert_bitcast_fusion.2
  251.5 0.8 copy-done.1
  252.3 1.1 copy.43
  253.4 0.8 copy-done.2
  254.2 1.1 copy.44
  (2 shorter events, 0.0 us)
Async XLA Ops:
  0.7 9.9 %copy-start = (bf16[768,1536]{1,0:T(8,128)(2,1)S(1)}, bf16[768,1536]{1,0:T(8,128)(2,1)}, u32[]{:S(2)}) copy-start(bf16[768,1536]{1,0:T(8,128)(2,1)} %up_own.1) | copy-start | bytes 7077892
  0.7 10.5 %copy-start.3 = (bf16[384,768]{1,0:T(8,128)(2,1)S(1)}, bf16[384,768]{1,0:T(8,128)(2,1)}, u32[]{:S(2)}) copy-start(bf16[384,768]{1,0:T(8,128)(2,1)} %wo_own.1) | copy-start | bytes 1769476
  0.7 10.8 %copy-start.8 = (bf16[1536]{0:T(1024)(128)(2,1)S(1)}, bf16[1536]{0:T(1024)(128)(2,1)}, u32[]{:S(2)}) copy-start(bf16[1536]{0:T(1024)(128)(2,1)} %bu_own.1) | copy-start | bytes 9220
  10.6 17.3 %collective-permute-start.1 = (bf16[768,1536]{1,0:T(8,128)(2,1)S(1)}, bf16[768,1536]{1,0:T(8,128)(2,1)}, u32[]{:S(2)}, u32[]{:S(2)}) collective-permute-start(bf16[768,1536]{1,0:T(8,128)(2,1)S(1)} %copy-done), channel_id=1, source_target_pairs={{0,1},{1,0},{2,3},{3,2},{4,5},{5,4},{6,7},{7,6},{8,9},{9,8},{10,11... | collective-permute-start | bytes 7077896 | tf_op jit(solution)/shard_map/ppermute | solution.py:937
  10.9 17.0 %collective-permute-start.3 = (bf16[1536,768]{1,0:T(8,128)(2,1)}, bf16[1536,768]{1,0:T(8,128)(2,1)}, u32[]{:S(2)}, u32[]{:S(2)}) collective-permute-start(bf16[1536,768]{1,0:T(8,128)(2,1)} %down_own.1), channel_id=1, source_target_pairs={{0,1},{1,0},{2,3},{3,2},{4,5},{5,4},{6,7},{7,6},{8,9},{9,8},{10,11... | collective-permute-start | bytes 7077896 | tf_op jit(solution)/shard_map/ppermute | solution.py:937
  11.2 16.7 %collective-permute-start = (bf16[384,768]{1,0:T(8,128)(2,1)S(1)}, bf16[384,768]{1,0:T(8,128)(2,1)S(1)}, u32[]{:S(2)}, u32[]{:S(2)}) collective-permute-start(bf16[384,768]{1,0:T(8,128)(2,1)S(1)} %copy-done.3), channel_id=1, source_target_pairs={{0,1},{1,0},{2,3},{3,2},{4,5},{5,4},{6,7},{7,6},{8,9},{9,8},{10,11... | collective-permute-start | bytes 1769480 | tf_op jit(solution)/shard_map/ppermute | solution.py:937
  11.4 16.4 %collective-permute-start.2 = (bf16[1536]{0:T(1024)(128)(2,1)S(1)}, bf16[1536]{0:T(1024)(128)(2,1)S(1)}, u32[]{:S(2)}, u32[]{:S(2)}) collective-permute-start(bf16[1536]{0:T(1024)(128)(2,1)S(1)} %copy-done.8), channel_id=1, source_target_pairs={{0,1},{1,0},{2,3},{3,2},{4,5},{5,4},{6,7},{7,6},{8,9},{9,8},{10,11... | collective-permute-start | bytes 9224 | tf_op jit(solution)/shard_map/ppermute | solution.py:937
  27.9 0.6 copy-start.9
  27.9 0.8 copy-start.4
  227.3 1.4 copy-start.5
  245.7 4.9 %copy-start.6 = (bf16[64,384]{1,0:T(8,128)(2,1)S(1)}, bf16[64,384]{1,0:T(8,128)(2,1)}, u32[]{:S(2)}) copy-start(bf16[64,384]{1,0:T(8,128)(2,1)} %get-tuple-element.107) | copy-start | bytes 147460
  245.7 4.9 %copy-start.7 = (bf16[64,384]{1,0:T(8,128)(2,1)S(1)}, bf16[64,384]{1,0:T(8,128)(2,1)}, u32[]{:S(2)}) copy-start(bf16[64,384]{1,0:T(8,128)(2,1)} %get-tuple-element.108) | copy-start | bytes 147460
  250.6 1.6 copy-start.1
  252.3 2.0 copy-start.2

commit v3 on v2

--- a/solution.py
+++ b/solution.py
@@ -174,18 +174,69 @@
             self.scatter_end(stage)
 
 
-def slot_shapes(order, rows, cols, stages="ABC"):
+def slot_shapes(order, rows, cols):
     shapes = []
-    for letter, axis in zip("ABC", order):
+    for axis in order:
         rows //= SIZE[axis]
-        if letter in stages:
-            shapes.append((SIZE[axis] - 1, rows, cols))
+        shapes.append((SIZE[axis] - 1, rows, cols))
     return shapes
 
 
-def as_slots(refs, stages="ABC"):
-    refs = list(refs)
-    return [refs.pop(0) if letter in stages else None for letter in "ABC"]
+ORDERS = ("xyz", "yxz")
+FEED_PLAN = {
+    "s1m": ((0, "sA"),),
+    "s3m": ((0, "fA"), (0, "sB"), (1, "sA"),),
+    "s4m": ((0, "fB"), (0, "sC"),),
+    "s5e": ((1, "fA"), (1, "sB"),),
+    "f_end": ((0, "fC"), (1, "fB"),),
+}
+BACK_PLAN = {
+    (0, 0): ((0, "sc"), (1, "sC"), (2, "sA"),),
+    (0, 3): ((0, "fc"), (2, "fA"), (0, "sb"), (2, "sB"), (3, "sA"),),
+    (1, 2): ((0, "fb"), (1, "fC"), (0, "sa"), (1, "sc"),),
+    (1, 3): ((2, "fB"), (2, "sC"), (4, "sA"),),
+    (2, 0): ((3, "fA"), (3, "sB"),),
+    (2, 1): ((1, "fc"), (1, "sb"),),
+    (2, 3): ((0, "fa"), (2, "fC"), (4, "fA"), (2, "sc"), (4, "sB"), (5, "sA"),),
+    "e2": ((3, "fB"), (3, "sC"),),
+    "e3": ((1, "fb"), (1, "sa"),),
+    "e4": ((4, "fB"), (4, "sC"),),
+    "e5": ((2, "fc"), (5, "fA"), (2, "sb"), (5, "sB"),),
+    "e7": ((3, "fC"), (3, "sc"),),
+    "w0": ((1, "fa"),),
+    "w1": ((4, "fC"), (4, "sc"),),
+    "w2": ((2, "fb"), (2, "sa"),),
+    "w3": ((5, "fB"), (5, "sC"),),
+    "w4": ((3, "fc"), (3, "sb"),),
+    "w5": ((4, "fc"), (4, "sb"),),
+    "w6": ((5, "fC"), (5, "sc"),),
+    "w7": ((2, "fa"),),
+    "w8": ((5, "fc"), (5, "sb"),),
+    "w9": ((3, "fb"), (3, "sa"),),
+    "w10": ((4, "fb"), (4, "sa"),),
+    "w11": ((5, "fb"), (5, "sa"),),
+    "w12": ((3, "fa"),),
+    "w13": ((4, "fa"),),
+    "w14": ((5, "fa"),),
+}
+
+
+def started(plan):
+    return [(i, action[1]) for actions in plan.values() for i, action in actions if action[0] == "s"]
+
+
+def progress(batch):
+    return sum(1 for i, _ in started(FEED_PLAN) if i == batch)
+
+
+def scatter_slots(plan, shapes):
+    slots = {}
+    for i, letter in started(plan):
+        if letter in "ABC":
+            for j, order in enumerate(ORDERS):
+                shape = slot_shapes(order, *shapes[i][j])["ABC".index(letter)]
+                slots[i, j, letter] = shape
+    return slots
 
 
 def project_kernel(
@@ -369,12 +420,14 @@
 
 
 def feed_kernel(
-    row_chips, x, cot, attended, wo_own, wo_other, bias_o, gain, bias,
+    row_chips, slot_keys, x, cot, attended, wo_own, wo_other, bias_o, gain, bias,
     up_other, up_own, bu_other, bu_own, down_other, down_own, bias_d,
-    out, grad_mid, grad_att, state, grad_wo, small,
-    att_own, att_other, ln, normed, inverse, total, grad_ln, att_stage, stage, held,
-    slots_a, slots_b, slots_c, move_sems, pair_sems, sum_sems,
+    out, grad_mid, grad_att, state_down, state_up, grad_wo, small,
+    att_own, att_other, ln, ln_t, normed, inverse, total, grad_ln, att_stage, stage_down, stage_up,
+    held_down, held_up, move_sems, pair_sems, sum_sems, *slot_refs,
 ):
+    state, stage, held = (state_down, state_up), (stage_down, stage_up), (held_down, held_up)
+    slots = dict(zip(slot_keys, slot_refs))
     step = pl.program_id(0)
     place = Place(row_chips)
     core = place.core
@@ -391,20 +444,25 @@
             recv_sem=pair_sems.at[1, i], device_id=place.twin(), device_id_type=MESH,
         )
 
-    def stage_copy(i):
-        return to_twin(stage.at[i], held.at[i], i)
+    def stage_copies(i):
+        return [to_twin(stage[j].at[i], held[j].at[i], 2 + 2 * i + j) for j in range(2)]
 
     def part(i, j):
         return Sum(
-            place, ("xyz", "yxz")[j], held.at[i, j],
-            [slots_a.at[i, j], slots_b.at[i, j] if i < 2 else None, slots_c.at[j] if i < 1 else None],
-            state.at[i, j], sum_sems.at[i, j],
+            place, ORDERS[j], held[j].at[i], [slots.get((i, j, letter)) for letter in "ABC"],
+            state[j].at[i], sum_sems.at[i, j],
         )
 
-    def act(i, *actions):
-        for action in actions:
+    def act(point):
+        for i, action in FEED_PLAN.get(point, ()):
             for j in range(2):
-                part(i, j).run(action, held.at[i, j] if action[1] == "c" else None)
+                part(i, j).run(action, held[j].at[i] if action[1] == "c" else None)
+
+    def act_at(name, odd):
+        for k in range(odd, 6, 2):
+            point = "s%d%s" % (k, name)
+            if point in FEED_PLAN:
+                pl.when(step == k)(functools.partial(act, point))
 
     @pl.when(step == 0)
     def _():
@@ -412,7 +470,7 @@
         local = pltpu.make_async_copy(attended.at[:, own], att_own, move_sems.at[0])
         local.start()
         ready()
-        exchange = to_twin(attended.at[:, theirs], att_other, 3)
+        exchange = to_twin(attended.at[:, theirs], att_other, 0)
         exchange.start()
         total[...] = x[...].astype(F32) + bias_o[...].astype(F32).reshape(1, -1)
         grad_ln[...] = jnp.zeros_like(grad_ln)
@@ -425,9 +483,11 @@
         norm, inv = row_normalize(mid)
         normed[...] = norm
         inverse[...] = jnp.broadcast_to(inv, inverse.shape)
-        ln[...] = (
+        low = (
             norm * gain[...].astype(F32).reshape(1, -1) + bias[...].astype(F32).reshape(1, -1)
         ).astype(BF16)
+        ln[...] = low
+        ln_t[...] = low.T
 
     def weight_grads(up, bias_up, down):
         hidden = dot(ln[...], up[...]) + bias_up[
@@ -437,7 +497,7 @@
         activated = activated.astype(BF16)
         grad_hidden = (dot(cot[...], down[...], NT) * slope).astype(BF16)
         grad_down = dot(activated, cot[...], TN)
-        grad_up = dot(grad_hidden, ln[...], TN)
+        grad_up = dot(ln_t[...], grad_hidden)
         sums = jnp.sum(grad_hidden.astype(F32), axis=0, keepdims=True)
         return activated, grad_hidden, grad_down, grad_up, sums
 
@@ -450,44 +510,27 @@
         activated, grad_hidden, grad_down, grad_up, sums = weight_grads(
             up_other, bu_other, down_other
         )
-        stage[index, 0] = grad_down.astype(BF16)
-        stage[index, 1] = grad_up.astype(BF16)
-        stage_copy(index).start()
+        stage_down[index] = grad_down.astype(BF16)
+        stage_up[index] = grad_up.astype(BF16)
+        for copy in stage_copies(index):
+            copy.start()
         small[pl.ds(ROW_BU_OTHER + index, 1), :chunk] = sums
+        act_at("m", 0)
         row_terms(activated, grad_hidden, up_other, down_other)
-
-        @pl.when(step == 2)
-        def _():
-            act(0, "fA", "sB")
-
-        @pl.when(step == 4)
-        def _():
-            act(0, "fC", "sc")
-            act(1, "fA", "sB")
+        act_at("e", 0)
 
     @pl.when(lax.rem(step, 2) == 1)
     def _():
         activated, grad_hidden, grad_down, grad_up, sums = weight_grads(up_own, bu_own, down_own)
-        stage_copy(index).wait()
-        held[index, 0] = (grad_down + held[index, 0].astype(F32)).astype(BF16)
-        held[index, 1] = (grad_up + held[index, 1].astype(F32)).astype(BF16)
+        for copy in stage_copies(index):
+            copy.wait()
+        held_down[index] = (grad_down + held_down[index].astype(F32)).astype(BF16)
+        held_up[index] = (grad_up + held_up[index].astype(F32)).astype(BF16)
         small[pl.ds(ROW_BU + index, 1), :chunk] = sums
 
-        @pl.when(step == 1)
-        def _():
-            act(0, "sA")
-
-        @pl.when(step == 3)
-        def _():
-            act(0, "fB", "sC")
-            act(1, "sA")
-
-        @pl.when(step == 5)
-        def _():
-            act(1, "fB")
-            act(2, "sA")
-
+        act_at("m", 1)
         row_terms(activated, grad_hidden, up_own, down_own)
+        act_at("e", 1)
 
     @pl.when(step == 5)
     def _():
@@ -499,7 +542,7 @@
         grad_mid[...] = mid
         low = mid.astype(BF16)
         att_stage[1] = dot(wo_other[...], low, NT).astype(BF16)
-        exchange = to_twin(att_stage.at[1], grad_att.at[:, own], 4)
+        exchange = to_twin(att_stage.at[1], grad_att.at[:, own], 1)
         exchange.start()
         att_stage[0] = dot(wo_own[...], low, NT).astype(BF16)
         local = pltpu.make_async_copy(att_stage.at[0], grad_att.at[:, own], move_sems.at[0])
@@ -511,14 +554,15 @@
         small[3:4, :] = jnp.sum(cot32, axis=0, keepdims=True)
         grad_wo[:heads] = dot(att_own[...], low).astype(BF16)
         grad_wo[heads:] = dot(att_other[...], low).astype(BF16)
-        act(0, "fc")
-        act(2, "fA")
+        act("f_end")
         moves = [local]
-        for i, depth in ((1, 2), (2, 1)):
+        for i in range(3):
+            if progress(i) > 3:
+                continue
             for j in range(2):
-                span = part(i, j).span(depth)
+                span = part(i, j).span(progress(i))
                 move = pltpu.make_async_copy(
-                    held.at[i, j, span, :], state.at[i, j, span, :], move_sems.at[1 + 2 * i + j]
+                    held[j].at[i, span, :], state[j].at[i, span, :], move_sems.at[1 + 2 * i + j]
                 )
                 move.start()
                 moves.append(move)
@@ -552,15 +596,16 @@
         ((rows, width), BF16),
         ((rows, width), F32),
         ((heads, 2 * rows), BF16),
-        ((3, 2, chunk, width), BF16),
+        ((3, chunk, width), BF16),
+        ((3, width, chunk), BF16),
         ((2 * heads, width), BF16),
         ((SUM_ROWS, width), F32),
     ]
     out_specs = [fixed(s) for s, _ in results]
-    out_specs[2] = out_specs[3] = anywhere
-    part = slot_shapes("xyz", chunk, width)
+    out_specs[2] = out_specs[3] = out_specs[4] = anywhere
+    slots = scatter_slots(FEED_PLAN, {i: ((chunk, width), (width, chunk)) for i in range(3)})
     return pl.pallas_call(
-        functools.partial(feed_kernel, row_chips),
+        functools.partial(feed_kernel, row_chips, list(slots)),
         grid=(6,),
         in_specs=specs,
         out_specs=out_specs,
@@ -569,20 +614,21 @@
             pltpu.VMEM((heads, rows), BF16),
             pltpu.VMEM((heads, rows), BF16),
             pltpu.VMEM((rows, width), BF16),
+            pltpu.VMEM((width, rows), BF16),
             pltpu.VMEM((rows, width), F32),
             pltpu.VMEM((rows, 128), F32),
             pltpu.VMEM((rows, width), F32),
             pltpu.VMEM((rows, width), F32),
             pltpu.VMEM((2, heads, rows), BF16),
-            pltpu.VMEM((3, 2, chunk, width), BF16),
-            pltpu.VMEM((3, 2, chunk, width), BF16),
-            pltpu.VMEM((3, 2) + part[0], BF16),
-            pltpu.VMEM((2, 2) + part[1], BF16),
-            pltpu.VMEM((2,) + part[2], BF16),
+            pltpu.VMEM((3, chunk, width), BF16),
+            pltpu.VMEM((3, width, chunk), BF16),
+            pltpu.VMEM((3, chunk, width), BF16),
+            pltpu.VMEM((3, width, chunk), BF16),
             pltpu.SemaphoreType.DMA((7,)),
-            pltpu.SemaphoreType.DMA((2, 5)),
+            pltpu.SemaphoreType.DMA((2, 8)),
             pltpu.SemaphoreType.DMA((3, 2, 2, 11)),
-        ],
+        ]
+        + [pltpu.VMEM(shape, BF16) for shape in slots.values()],
         compiler_params=pltpu.CompilerParams(
             vmem_limit_bytes=VMEM_LIMIT, collective_id=2, has_side_effects=True,
             dimension_semantics=("arbitrary",),
@@ -600,46 +646,25 @@
     return jnp.where(index == 0, high, jnp.where(index == 1, middle, rest)).astype(BF16)
 
 
-BACK_PLAN = {
-    "start": ((0, "sb"), (2, "sB"), (1, "sC")),
-    (0, 2): ((0, "fb"), (0, "sa"), (2, "fB")),
-    (0, 3): ((1, "fC"), (1, "sc"), (2, "sC")),
-    (1, 1): ((0, "fa"), (3, "sA")),
-    (1, 2): ((1, "fc"), (1, "sb")),
-    (1, 3): ((3, "fA"), (3, "sB"), (1, "fb"), (1, "sa")),
-    (2, 1): ((2, "fC"), (2, "sc"), (3, "fB"), (3, "sC")),
-    (2, 2): ((1, "fa"), (4, "sA")),
-    (2, 3): ((2, "fc"), (2, "sb"), (4, "fA"), (4, "sB")),
-    "e0": ((5, "sA"),),
-    "e1": ((3, "fC"), (3, "sc"), (2, "fb"), (2, "sa"), (4, "fB"), (4, "sC")),
-    "e2": ((5, "fA"), (5, "sB"), (3, "fc"), (3, "sb")),
-    "e3": ((4, "fC"), (4, "sc"), (5, "fB"), (5, "sC"), (3, "fb"), (3, "sa")),
-    "e4": ((2, "fa"), (4, "fc"), (4, "sb")),
-    "e5": ((5, "fC"), (5, "sc"), (4, "fb"), (4, "sa")),
-    "e6": ((3, "fa"), (5, "fc"), (5, "sb")),
-    "e7": ((5, "fb"), (5, "sa")),
-    "e8": ((4, "fa"), (5, "fa")),
-}
-
-
 def attend_back_kernel(
-    row_chips, block, split, qt, k, kt, v, do, attended, lse, ln, x, gain, wq, wk, wv_t, grad_wo,
-    small, state,
+    row_chips, block, slot_keys, split, gain, small, qt_far, k_far, kt_far, v_far, do_far, attended_far, lse_far,
+    ln_far, x_far, wq_far, wk_far, wv_far, grad_wo_far, state_down, state_up,
     back, dv_first, sums, red_down, red_up, red_wo, red_low, red_v, red_last,
     stack, q_aug, d_aug, k_aug, v_aug, dk_sum, dv_sum, weights, terms_send, terms_got,
-    wo_got, held, held_wo, held_low, held_v, held_last, sums_got,
-    one_c, two_b, two_c, wo_a, wo_b, wo_c, low_a, low_b, low_c, v_a, v_b, v_c,
-    last_a, last_b, last_c, move_sems, pair_sems, tiny_sems, sum_sems,
+    wo_got, held_down, held_up, held_wo, held_low, held_v, held_last, sums_got,
+    qt, k, kt, v, do, attended, lse, ln, x, grad_wo,
+    move_sems, load_sems, pair_sems, tiny_sems, sum_sems, *slot_refs,
 ):
+    state, held = (state_down, state_up), (held_down, held_up)
+    slots = dict(zip(slot_keys, slot_refs))
     width, tokens = qt.shape
     half = tokens // 2
-    fresh = wv_t.shape[0]
+    fresh, model = wv_far.shape
     place = Place(row_chips)
     core = place.core
     pair_width = 2 * HEAD_DIM
     own = pl.ds(pl.multiple_of(core * half, half), half)
     theirs = pl.ds(pl.multiple_of((1 - core) * half, half), half)
-    orders = ("xyz", "yxz")
 
     def to_twin(source, target, i):
         return pltpu.make_async_remote_copy(
@@ -648,58 +673,68 @@
         )
 
     def part(i, j):
-        sems = sum_sems.at[i, j]
+        chunk = state_down.shape[1]
         if i < 3:
-            result = (red_down, red_up)[j].at[i]
-            slots = [
-                None,
-                two_b.at[j] if i == 2 else None,
-                (None, one_c, two_c)[i].at[j] if i else None,
-            ]
-            return Sum(place, orders[j], held.at[i - 1, j] if i else None, slots, result, sems)
-        if i == 4:
-            given = (held_low, [low_a, low_b, low_c], red_low)
-            if j:
-                given = (held_v, [v_a, v_b, v_c], red_v)
-            return Sum(place, orders[j], given[0], given[1], given[2], sems)
-        holder, slots, result = {
-            3: (held_wo, [wo_a, wo_b, wo_c], red_wo),
-            5: (held_last, [last_a, last_b, last_c], red_last),
-        }[i]
-        return Sum(place, orders[j], holder.at[j], [s.at[j] for s in slots], result.at[j], sems)
+            holder = held[j].at[i]
+            result = red_up.at[:, i * chunk : (i + 1) * chunk] if j else red_down.at[i]
+        else:
+            holder, result = {
+                3: (held_wo.at[j], red_wo.at[j]),
+                4: ((held_low, red_low), (held_v, red_v))[j],
+                5: (held_last.at[j], red_last.at[j]),
+            }[i]
+        return Sum(
+            place, ORDERS[j], holder, [slots.get((i, j, letter)) for letter in "ABC"], result,
+            sum_sems.at[i, j],
+        )
 
     def act(point):
         for i, action in BACK_PLAN.get(point, ()):
             for j in range(2):
                 one = part(i, j)
                 source = None
-                if i == 0 and action[1] == "b":
-                    source = state.at[0, j]
-                elif action[1] == "c":
+                if action[1] == "c":
                     source = one.held
+                elif action[1] == "b" and i < 3 and progress(i) == 4:
+                    source = state[j].at[i]
                 one.run(action, source)
 
-    loads = [
-        pltpu.make_async_copy(
-            state.at[i, j, part(i, j).span(depth), :],
-            held.at[i - 1, j, part(i, j).span(depth), :],
-            move_sems.at[2 * (i - 1) + j],
-        )
-        for i, depth in ((1, 2), (2, 1))
-        for j in range(2)
-    ]
+    loads = []
+    for i in range(3):
+        if progress(i) < 4:
+            for j in range(2):
+                span = part(i, j).span(progress(i))
+                loads.append(
+                    pltpu.make_async_copy(
+                        state[j].at[i, span, :], held[j].at[i, span, :], move_sems.at[2 * i + j]
+                    )
+                )
     ready = greet(place)
     for load in loads:
         load.start()
-    weights[:width] = wq[...].T
-    weights[width : 2 * width] = wk[...].T
-    weights[2 * width :] = wv_t[...]
+    arriving = [
+        pltpu.make_async_copy(far, near, load_sems.at[i])
+        for i, (far, near) in enumerate(
+            (
+                (k_far, k), (qt_far, qt), (v_far, v), (do_far, do), (attended_far, attended),
+                (lse_far, lse), (kt_far, kt), (wq_far, terms_send.at[:model, :width]),
+                (wk_far, terms_send.at[:model, width:]), (wv_far, weights.at[2 * width :, :]), (ln_far, ln),
+                (grad_wo_far.at[:width, :], grad_wo), (x_far, x),
+            )
+        )
+    ]
+    for copy in arriving:
+        copy.start()
     ready()
-    wo_exchange = to_twin(grad_wo.at[width:, :], wo_got, 0)
+    wo_exchange = to_twin(grad_wo_far.at[width:, :], wo_got, 0)
     wo_exchange.start()
     for load in loads:
         load.wait()
     act("start")
+    for copy in arriving:
+        copy.wait()
+    weights[:width] = terms_send[:model, :width].T
+    weights[width : 2 * width] = terms_send[:model, width:].T
     far = jnp.where(split[0] < tokens, -1e9, 0.0)
     token = lax.broadcasted_iota(jnp.int32, (1, tokens), 1)
     far_row = jnp.where(token >= half, far, 0.0)
@@ -770,7 +805,7 @@
             stack[2 * width : 2 * width + HEAD_DIM, :] = dv_sum[0].astype(BF16)
             stack[2 * width + HEAD_DIM : 2 * width + 2 * HEAD_DIM, :] = dv_sum[1].astype(BF16)
             wo_exchange.wait()
-            summed = (grad_wo[:width].astype(F32) + wo_got[...].astype(F32)).astype(BF16)
+            summed = (grad_wo[...].astype(F32) + wo_got[...].astype(F32)).astype(BF16)
             by_columns(held_wo, 0, summed)
             for i in range(3):
                 by_columns(
@@ -815,8 +850,9 @@
     terms_send[...] = dot(stack[:, theirs], weights[...], TN).astype(BF16)
     terms_exchange = to_twin(terms_send, terms_got, 1)
     terms_exchange.start()
+    act("e1")
     back[...] = dot(stack[:, own], weights[...], TN)
-    act("e1")
+    act("e2")
     normed, inverse = row_normalize(x[...].astype(F32))
     terms_exchange.wait()
     grad = back[...] + terms_got[...].astype(F32)
@@ -828,6 +864,7 @@
     sums[ROW_BV : ROW_BV + 1, :fresh] = biases[:1, 2 * width :]
     tiny = to_twin(sums, sums_got.at[0], 2)
     tiny.start()
+    act("e3")
     back[...] = row_normalize_back(grad * gain[...].astype(F32).reshape(1, -1), normed, inverse)
     tiny.wait()
     sums[:ROW_BU, :] = sums[:ROW_BU, :] + sums_got[0, :ROW_BU, :]
@@ -835,7 +872,7 @@
         sums[ROW_BU:ROW_BU_OTHER, :] + sums_got[0, ROW_BU_OTHER:ROW_BQ, :]
     )
     slot = 1
-    points = iter(("e2", "e3", "e4"))
+    points = iter(("e4", "e5", "e6"))
     for axis in AXES:
         copies = []
         for step in range(1, SIZE[axis]):
@@ -855,19 +892,20 @@
         for i in range(slot - len(copies), slot):
             total = total + sums_got[i]
         sums[...] = total
-    for point in ("e5", "e6", "e7", "e8"):
-        act(point)
+    for point in BACK_PLAN:
+        if point == "e7" or point[0] == "w":
+            act(point)
 
 
 def attend_back(
-    row_chips, split, qt, k, kt, v, do, attended, lse, ln, x, gain, wq, wk, wv_t, grad_wo, small,
-    state, block=512,
+    row_chips, split, gain, small, qt, k, kt, v, do, attended, lse, ln, x, wq, wk, wv_t, grad_wo,
+    state_down, state_up, block=512,
 ):
     width, tokens = qt.shape
     rows, model = x.shape
     fresh = wv_t.shape[0]
     pair = 2 * HEAD_DIM
-    chunk = state.shape[2]
+    chunk = state_down.shape[1]
     low_rows = 2 * pair
     cols = model // 2
     vmem = pl.BlockSpec(memory_space=pltpu.VMEM)
@@ -877,17 +915,17 @@
         ((width - fresh, tokens), F32, vmem),
         ((SUM_ROWS, model), F32, vmem),
         ((3, chunk, model), BF16, anywhere),
-        ((3, chunk, model), BF16, anywhere),
+        ((model, 3 * chunk), BF16, anywhere),
         ((2, 2 * width, cols), BF16, anywhere),
         ((low_rows, model), BF16, anywhere),
         ((low_rows, cols), BF16, anywhere),
         ((2, low_rows, cols), BF16, anywhere),
     ]
-    part = slot_shapes("xyz", chunk, model)
-    wo = slot_shapes("xyz", 2 * width, cols)
-    low = slot_shapes("xyz", low_rows, model)
-    thin = slot_shapes("xyz", low_rows, cols)
-    two = lambda s: (2,) + s
+    shapes = {i: ((chunk, model), (model, chunk)) for i in range(3)}
+    shapes[3] = ((2 * width, cols),) * 2
+    shapes[4] = ((low_rows, model), (low_rows, cols))
+    shapes[5] = ((low_rows, cols),) * 2
+    slots = scatter_slots(BACK_PLAN, shapes)
     scratch = [
         ((2 * width + fresh, tokens), BF16),
         ((2, pair, tokens), BF16),
@@ -900,37 +938,109 @@
         ((rows, model), BF16),
         ((rows, model), BF16),
         ((width, model), BF16),
-        ((2, 2, chunk, model), BF16),
+        ((3, chunk, model), BF16),
+        ((3, model, chunk), BF16),
         ((2, 2 * width, cols), BF16),
         ((low_rows, model), BF16),
         ((low_rows, cols), BF16),
         ((2, low_rows, cols), BF16),
         ((6, SUM_ROWS, model), F32),
-        (two(part[2]), BF16),
-        (two(part[1]), BF16),
-        (two(part[2]), BF16),
     ]
-    scratch += [(two(s), BF16) for s in wo]
-    scratch += [(s, BF16) for s in low]
-    scratch += [(s, BF16) for s in thin]
-    scratch += [(two(s), BF16) for s in thin]
+    near = (qt, k, kt, v, do, attended, lse, ln, x)
+    scratch += [(a.shape, a.dtype) for a in near] + [((width, model), BF16)]
     return pl.pallas_call(
-        functools.partial(attend_back_kernel, row_chips, block),
+        functools.partial(attend_back_kernel, row_chips, block, list(slots)),
         out_shape=[jax.ShapeDtypeStruct(s, t) for s, t, _ in results],
-        in_specs=[pl.BlockSpec(memory_space=pltpu.SMEM)] + [vmem] * 15 + [anywhere],
+        in_specs=[pl.BlockSpec(memory_space=pltpu.SMEM), vmem, vmem] + [anywhere] * 15,
         out_specs=[spec for _, _, spec in results],
         scratch_shapes=[pltpu.VMEM(s, t) for s, t in scratch]
         + [
-            pltpu.SemaphoreType.DMA((4,)),
+            pltpu.SemaphoreType.DMA((6,)),
+            pltpu.SemaphoreType.DMA((13,)),
             pltpu.SemaphoreType.DMA((2, 3)),
             pltpu.SemaphoreType.DMA((2, 6)),
             pltpu.SemaphoreType.DMA((6, 2, 2, 11)),
-        ],
+        ]
+        + [pltpu.VMEM(shape, BF16) for shape in slots.values()],
         compiler_params=pltpu.CompilerParams(
             vmem_limit_bytes=VMEM_LIMIT, collective_id=3, has_side_effects=True
         ),
         name="attend_back",
-    )(split, qt, k, kt, v, do, attended, lse, ln, x, gain, wq, wk, wv_t, grad_wo, small, state)
+    )(
+        split, gain, small, qt, k, kt, v, do, attended, lse, ln, x, wq, wk, wv_t, grad_wo,
+        state_down, state_up,
+    )
+
+
+def finish_kernel(
+    mid, back, dv, sums, down, up, wo, low, thin, last,
+    grad_input, grad_first, grad_down, grad_up, grad_wo, grad_q, grad_k, grad_v, bu,
+    bias_q, bias_v, gain_two, shift_two, bias_o, bias_d, gain_one, shift_one,
+):
+    step = pl.program_id(0)
+    cols = wo.shape[2]
+    pair = 2 * HEAD_DIM
+    grad_input[...] = mid[...] + back[...].astype(F32)
+    grad_first[...] = dv[...]
+    grad_down[...] = down[0].astype(F32)
+    grad_up[...] = up[...].astype(F32)
+
+    @pl.when(step == 0)
+    def _():
+        heads = grad_wo.shape[0]
+        for j in range(2):
+            span = slice(j * cols, (j + 1) * cols)
+            grad_wo[:, span] = wo[j, :heads].astype(F32)
+            grad_v[:pair, span] = wo[j, heads + 2 * pair :].astype(F32)
+            grad_v[pair:, span] = thin[HEAD_DIM * j : HEAD_DIM * (j + 1)].astype(F32)
+            for i, target in enumerate((grad_q, grad_k)):
+                first = heads + i * pair
+                target[span, :pair] = wo[j, first : first + pair].astype(F32).T
+                target[span, 2 * pair :] = last[j, i * pair : (i + 1) * pair].astype(F32).T
+        for i, target in enumerate((grad_q, grad_k)):
+            target[:, pair : 2 * pair] = low[i * pair : (i + 1) * pair].astype(F32).T
+        chunk = bu.shape[0] // 3
+        for i in range(3):
+            bu[i * chunk : (i + 1) * chunk] = sums[ROW_BU + i, :chunk]
+        bias_q[...] = sums[ROW_BQ, : bias_q.shape[0]]
+        bias_v[...] = sums[ROW_BV, : bias_v.shape[0]]
+        for i, target in enumerate((gain_two, shift_two, bias_o, bias_d, gain_one, shift_one)):
+            target[...] = sums[i, :]
+
+
+def finish(mid, back, dv, sums, down, up, wo, low, thin, last):
+    rows, width = mid.shape
+    heads = wo.shape[1] // 2
+    fresh = heads // 2
+    hidden = up.shape[1]
+    steps = 6
+    chunk = down.shape[1]
+    half = chunk // 2
+    out_rows = 192
+    operands = (mid, back, dv, sums, down, up, wo, low, thin, last)
+    once = pl.Buffered(1)
+    fixed = lambda s: pl.BlockSpec(s, lambda i, nd=len(s): (0,) * nd, pipeline_mode=once)
+    by_rows = lambda n, c: pl.BlockSpec((n, c), lambda i: (i, 0))
+    specs = [fixed(a.shape) for a in operands]
+    specs[0] = specs[1] = by_rows(out_rows, width)
+    specs[2] = by_rows(dv.shape[0] // steps, dv.shape[1])
+    specs[4] = pl.BlockSpec((1, half, width), lambda i: (i // 2, lax.rem(i, 2), 0))
+    specs[5] = by_rows(width // steps, hidden)
+    shapes = [(rows, width), dv.shape, (hidden, width), (width, hidden), (heads, width)]
+    shapes += [(width, heads), (width, heads), (fresh, width)]
+    shapes += [(hidden,), (heads,), (fresh,)] + [(width,)] * 6
+    out_specs = [fixed(s) for s in shapes]
+    out_specs[0], out_specs[1] = specs[0], specs[2]
+    out_specs[2], out_specs[3] = by_rows(half, width), specs[5]
+    return pl.pallas_call(
+        finish_kernel,
+        grid=(steps,),
+        in_specs=specs,
+        out_specs=out_specs,
+        out_shape=[jax.ShapeDtypeStruct(s, F32) for s in shapes],
+        compiler_params=pltpu.CompilerParams(vmem_limit_bytes=VMEM_LIMIT),
+        name="finish",
+    )(*operands)
 
 
 def swap(array):
@@ -966,47 +1076,23 @@
     up, down, wo, bu, vt = lax.optimization_barrier((w_up, w_down, w_out, bias_up, vt))
     up_other, down_other, wo_other, bu_other = swap(up), swap(down), swap(wo), swap(bu)
     attended, lse = attend(doc_split, qt, k, vt)
-    output, grad_middle, grad_att, state, grad_wo, small = feed(
+    output, grad_middle, grad_att, state_down, state_up, grad_wo, small = feed(
         row_chips, input_rows, cotangent, attended, w_out, wo_other, bias_attn_out, gain_norm2,
         bias_norm2, up_other, w_up, bu_other, bias_up, down_other, w_down, bias_down,
     )
-    back, dv_first, sums, red_down, red_up, red_wo, red_low, red_v, red_last = attend_back(
-        row_chips, doc_split, qt, k, kt, v, grad_att, attended, lse, ln, input_rows, gain_norm1,
-        w_query, w_key, wv_t, grad_wo, small, state,
+    back, dv_first, *reduced = attend_back(
+        row_chips, doc_split, gain_norm1, small, qt, k, kt, v, grad_att, attended, lse, ln,
+        input_rows, w_query, w_key, wv_t, grad_wo, state_down, state_up,
     )
-    red_down, red_up, red_wo, red_low, red_v, red_last, sums = [
-        across_blocks(a, row_chips)
-        for a in (red_down, red_up, red_wo, red_low, red_v, red_last, sums)
-    ]
-    red_wo = jnp.concatenate([red_wo[0], red_wo[1]], axis=1)
-    red_last = jnp.concatenate([red_last[0], red_last[1]], axis=1)
-    rest = jnp.concatenate([red_v[:HEAD_DIM], red_v[HEAD_DIM:pair]], axis=1)
-    first = heads
-    grad_q = jnp.concatenate([red_wo[first : first + pair], red_low[:pair], red_last[:pair]])
-    grad_k = jnp.concatenate(
-        [red_wo[first + pair : first + 2 * pair], red_low[pair:], red_last[pair:]]
-    )
-    grad_v = jnp.concatenate([red_wo[first + 2 * pair :], rest])
-    grad_bu = sums[ROW_BU:ROW_BU_OTHER, : hidden // 3].reshape(-1)
+    reduced = [across_blocks(a, row_chips) for a in reduced]
+    (
+        grad_input, grad_first, grad_down, grad_up, grad_wo, grad_q, grad_k, grad_v, bias_grad_up,
+        bias_grad_q, bias_grad_v, gain_two, shift_two, bias_grad_o, bias_grad_d, gain_one, shift_one,
+    ) = finish(grad_middle, back, dv_first, *reduced)
     return (
-        output,
-        grad_middle + back,
-        dv_first.T,
-        sums[4],
-        sums[5],
-        grad_q.astype(F32).T,
-        sums[ROW_BQ, :heads],
-        grad_k.astype(F32).T,
-        grad_v.astype(F32).T,
-        sums[ROW_BV, :fresh],
-        red_wo[:heads].astype(F32),
-        sums[2],
-        sums[0],
-        sums[1],
-        red_up.reshape(hidden, -1).astype(F32).T,
-        grad_bu,
-        red_down.reshape(hidden, -1).astype(F32),
-        sums[3],
+        output, grad_input, grad_first.T, gain_one, shift_one, grad_q, bias_grad_q, grad_k, grad_v.T,
+        bias_grad_v, grad_wo, bias_grad_o, gain_two, shift_two, grad_up, bias_grad_up, grad_down,
+        bias_grad_d,
     )
 
 

time: 260 us -> 235 us (0.904)
  the two profiles are of different devices: /device:TPU:24 before, /device:TPU:0 now
where the time goes in v3:
time: 235 us; the launch traced here: 230 us
  Pallas kernels  226 us (96%)
    pallas_call x1, Pallas kernels, attend_back(): pl.pallas_call(functools.partial(attend_back_kernel, row_chips, block, li...  116 us
    pallas_call x1, Pallas kernels, feed(): pl.pallas_call(functools.partial(feed_kernel, row_chips, list(slots)), gr...  70.5 us
    pallas_call x1, Pallas kernels, attend(): pl.pallas_call(functools.partial(attend_kernel, block), out_shape=(jax.Sh...  15.5 us
    pallas_call x1, Pallas kernels, finish(): pl.pallas_call(finish_kernel, grid=(steps,), in_specs=specs, out_specs=ou...  13.6 us
    pallas_call x1, Pallas kernels, project(): pl.pallas_call(project_kernel, out_shape=[jax.ShapeDtypeStruct(s, BF16) f...  10.1 us
  transfers between devices with their start and end apart: 4, of which 0 were waited for; matrix products, arithmetic and copies ran while one was open for 0% of the time, Pallas kernels for 7%

profile of v3, /device:TPU:0, one launch (start us, length us, event | category | flops | bytes accessed | tf_op | source)
XLA Modules:
  0.0 230.3 jit_solution(12435245582755660461)
XLA Ops:
  0.7 0.0 copy-start
  0.7 0.0 copy-start.2
  0.7 0.0 copy-start.4
  0.7 10.1 %project.1 = (bf16[2048,768]{1,0:T(8,128)(2,1)}, bf16[384,2048]{1,0:T(8,128)(2,1)}, bf16[2048,384]{1,0:T(8,128)(2,1)}, bf16[384,2048]{1,0:T(8,128)(2,1)}, bf16[2...) custom-call(bf16[1024,768]{1,0:T(8,128)(2,1)} %x_far.1, bf16[192,2048]{1,0:T(8,128)(2,1)} %bitcast.6, bf16[768]{0:T(1024)(128)(2,1)} %gain.5, ...), custom_call_target="tpu_custom_call" | custom-call | tf_op jit(solution)/shard_map/project/pallas_call | solution.py:311
  10.8 0.0 copy-done
  10.8 0.4 collective-permute-start.1
  11.2 0.2 collective-permute-start.3
  11.4 0.0 copy-done.2
  11.4 0.3 collective-permute-start
  11.7 0.0 copy-done.4
  11.7 0.2 collective-permute-start.2
  12.5 15.5 %attend.1 = (bf16[384,2048]{1,0:T(8,128)(2,1)}, f32[6,1,2048]{2,1,0:T(1,128)}) custom-call(s32[1]{0:T(128)S(6)} %copy.38.split, bf16[384,2048]{1,0:T(8,128)(2,1)} %get-tuple-element.64.qt.qt_far, bf16[2048,384]{1,0:T(8,128)(2,1)} %get-tuple-element.65.k.k_far, bf16[384,2048]{1,0:T(8,128)(2,1)} %get-tuple-element.67.vt), custom_call_target="tpu_custom_call" | custom-call | tf_op jit(solution)/shard_map/attend/pallas_call | solution.py:394
  28.0 0.0 collective-permute-done.2.bu_other
  28.0 0.0 copy-start.5
  28.1 0.0 collective-permute-done.wo_other
  28.1 0.0 copy-start.3
  28.1 0.0 collective-permute-done.1.up_other
  28.1 0.0 collective-permute-done.3.down_other
  28.1 0.6 copy-done.5
  28.6 0.2 copy-done.3
  28.9 70.5 %feed.1 = (bf16[1024,768]{1,0:T(8,128)(2,1)}, f32[1024,768]{1,0:T(8,128)}, bf16[384,2048]{1,0:T(8,128)(2,1)}, bf16[3,512,768]{2,1,0:T(8,128)(2,1)}, bf16[3,768,5...) custom-call(bf16[1024,768]{1,0:T(8,128)(2,1)} %x_far.1, bf16[1024,768]{1,0:T(8,128)(2,1)} %cot.1, ...), custom_call_target="tpu_custom_call" | custom-call | tf_op jit(solution)/shard_map/feed/pallas_call | solution.py:607
  99.4 116.0 %attend_back.1 = (f32[1024,768]{1,0:T(8,128)}, f32[192,2048]{1,0:T(8,128)}, f32[16,768]{1,0:T(8,128)}, bf16[3,512,768]{2,1,0:T(8,128)(2,1)}, bf16[768,1536]{1,0:...) custom-call(s32[1]{0:T(128)S(6)} %copy.38.split, ...), custom_call_target="tpu_custom_call" | custom-call | tf_op jit(solution)/shard_map/attend_back/pallas_call | solution.py:951
  215.3 0.0 copy-start.1
  215.3 13.6 %finish.1 = (f32[1024,768]{1,0:T(8,128)}, f32[192,2048]{1,0:T(8,128)}, f32[1536,768]{1,0:T(8,128)}, f32[768,1536]{1,0:T(8,128)}, f32[384,768]{1,0:T(8,128)}, /*i...) custom-call(f32[1024,768]{1,0:T(8,128)} %get-tuple-element.74.mid, ...), custom_call_target="tpu_custom_call" | custom-call | tf_op jit(solution)/shard_map/finish/pallas_call | solution.py:1035
  228.9 0.0 copy-done.1
  229.0 1.1 copy.39
Async XLA Ops:
  0.7 10.1 %copy-start = (bf16[768,1536]{1,0:T(8,128)(2,1)S(1)}, bf16[768,1536]{1,0:T(8,128)(2,1)}, u32[]{:S(2)}) copy-start(bf16[768,1536]{1,0:T(8,128)(2,1)} %up_own.1) | copy-start | bytes 7077892
  0.7 10.7 %copy-start.2 = (bf16[384,768]{1,0:T(8,128)(2,1)S(1)}, bf16[384,768]{1,0:T(8,128)(2,1)}, u32[]{:S(2)}) copy-start(bf16[384,768]{1,0:T(8,128)(2,1)} %wo_own.1) | copy-start | bytes 1769476
  0.7 11.0 %copy-start.4 = (bf16[1536]{0:T(1024)(128)(2,1)S(1)}, bf16[1536]{0:T(1024)(128)(2,1)}, u32[]{:S(2)}) copy-start(bf16[1536]{0:T(1024)(128)(2,1)} %bu_own.1) | copy-start | bytes 9220
  10.8 17.3 %collective-permute-start.1 = (bf16[768,1536]{1,0:T(8,128)(2,1)S(1)}, bf16[768,1536]{1,0:T(8,128)(2,1)}, u32[]{:S(2)}, u32[]{:S(2)}) collective-permute-start(bf16[768,1536]{1,0:T(8,128)(2,1)S(1)} %copy-done), channel_id=1, source_target_pairs={{0,1},{1,0},{2,3},{3,2},{4,5},{5,4},{6,7},{7,6},{8,9},{9,8},{10,11... | collective-permute-start | bytes 7077896 | tf_op jit(solution)/shard_map/ppermute | solution.py:1047
  11.2 16.9 %collective-permute-start.3 = (bf16[1536,768]{1,0:T(8,128)(2,1)}, bf16[1536,768]{1,0:T(8,128)(2,1)}, u32[]{:S(2)}, u32[]{:S(2)}) collective-permute-start(bf16[1536,768]{1,0:T(8,128)(2,1)} %down_own.1), channel_id=1, source_target_pairs={{0,1},{1,0},{2,3},{3,2},{4,5},{5,4},{6,7},{7,6},{8,9},{9,8},{10,11... | collective-permute-start | bytes 7077896 | tf_op jit(solution)/shard_map/ppermute | solution.py:1047
  11.4 16.7 %collective-permute-start = (bf16[384,768]{1,0:T(8,128)(2,1)S(1)}, bf16[384,768]{1,0:T(8,128)(2,1)S(1)}, u32[]{:S(2)}, u32[]{:S(2)}) collective-permute-start(bf16[384,768]{1,0:T(8,128)(2,1)S(1)} %copy-done.2), channel_id=1, source_target_pairs={{0,1},{1,0},{2,3},{3,2},{4,5},{5,4},{6,7},{7,6},{8,9},{9,8},{10,11... | collective-permute-start | bytes 1769480 | tf_op jit(solution)/shard_map/ppermute | solution.py:1047
  11.7 16.4 %collective-permute-start.2 = (bf16[1536]{0:T(1024)(128)(2,1)S(1)}, bf16[1536]{0:T(1024)(128)(2,1)S(1)}, u32[]{:S(2)}, u32[]{:S(2)}) collective-permute-start(bf16[1536]{0:T(1024)(128)(2,1)S(1)} %copy-done.4), channel_id=1, source_target_pairs={{0,1},{1,0},{2,3},{3,2},{4,5},{5,4},{6,7},{7,6},{8,9},{9,8},{10,11... | collective-permute-start | bytes 9224 | tf_op jit(solution)/shard_map/ppermute | solution.py:1047
  28.0 0.6 copy-start.5
  28.1 0.8 copy-start.3
  215.3 13.6 %copy-start.1 = (bf16[1024,768]{1,0:T(8,128)(2,1)S(1)}, bf16[1024,768]{1,0:T(8,128)(2,1)}, u32[]{:S(2)}) copy-start(bf16[1024,768]{1,0:T(8,128)(2,1)} %get-tuple-element.128) | copy-start | bytes 4718596

commit v4 on v3

--- a/solution.py
+++ b/solution.py
@@ -191,33 +191,32 @@
     "f_end": ((0, "fC"), (1, "fB"),),
 }
 BACK_PLAN = {
-    (0, 0): ((0, "sc"), (1, "sC"), (2, "sA"),),
-    (0, 3): ((0, "fc"), (2, "fA"), (0, "sb"), (2, "sB"), (3, "sA"),),
-    (1, 2): ((0, "fb"), (1, "fC"), (0, "sa"), (1, "sc"),),
-    (1, 3): ((2, "fB"), (2, "sC"), (4, "sA"),),
-    (2, 0): ((3, "fA"), (3, "sB"),),
-    (2, 1): ((1, "fc"), (1, "sb"),),
-    (2, 3): ((0, "fa"), (2, "fC"), (4, "fA"), (2, "sc"), (4, "sB"), (5, "sA"),),
-    "e2": ((3, "fB"), (3, "sC"),),
-    "e3": ((1, "fb"), (1, "sa"),),
-    "e4": ((4, "fB"), (4, "sC"),),
-    "e5": ((2, "fc"), (5, "fA"), (2, "sb"), (5, "sB"),),
-    "e7": ((3, "fC"), (3, "sc"),),
-    "w0": ((1, "fa"),),
+    (0, 0): ((1, "sC"), (2, "sA"), (0, "sc"),),
+    (0, 7): ((1, "fC"), (2, "fA"), (2, "sB"), (3, "sA"), (1, "sc"),),
+    (1, 5): ((2, "fB"), (0, "fc"), (2, "sC"), (0, "sb"),),
+    (1, 7): ((3, "fA"), (3, "sB"), (4, "sA"),),
+    (2, 0): ((1, "fc"), (1, "sb"),),
+    (2, 2): ((0, "fb"), (0, "sa"),),
+    (2, 4): ((3, "fB"), (3, "sC"),),
+    (2, 6): ((2, "fC"), (4, "fA"), (4, "sB"), (2, "sc"),),
+    (2, 7): ((5, "sA"),),
+    "e1": ((1, "fb"), (3, "fC"), (1, "sa"), (3, "sc"),),
+    "e5": ((0, "fa"), (4, "fB"), (2, "fc"), (4, "sC"), (2, "sb"),),
+    "e6": ((5, "fA"), (5, "sB"),),
+    "w0": ((3, "fc"), (3, "sb"),),
     "w1": ((4, "fC"), (4, "sc"),),
-    "w2": ((2, "fb"), (2, "sa"),),
-    "w3": ((5, "fB"), (5, "sC"),),
-    "w4": ((3, "fc"), (3, "sb"),),
-    "w5": ((4, "fc"), (4, "sb"),),
+    "w2": ((1, "fa"),),
+    "w3": ((2, "fb"), (4, "fc"), (2, "sa"), (4, "sb"),),
+    "w4": ((5, "fB"), (5, "sC"),),
+    "w5": ((3, "fb"), (3, "sa"),),
     "w6": ((5, "fC"), (5, "sc"),),
-    "w7": ((2, "fa"),),
-    "w8": ((5, "fc"), (5, "sb"),),
-    "w9": ((3, "fb"), (3, "sa"),),
-    "w10": ((4, "fb"), (4, "sa"),),
+    "w7": ((5, "fc"), (5, "sb"),),
+    "w8": ((2, "fa"),),
+    "w9": ((4, "fb"), (4, "sa"),),
+    "w10": ((3, "fa"),),
     "w11": ((5, "fb"), (5, "sa"),),
-    "w12": ((3, "fa"),),
-    "w13": ((4, "fa"),),
-    "w14": ((5, "fa"),),
+    "w12": ((4, "fa"),),
+    "w13": ((5, "fa"),),
 }
 
 
@@ -240,7 +239,7 @@
 
 
 def project_kernel(
-    x, first_t, gain, bias, wq, bq, wk, wv_t, bv, ln, qt, k, kt, v, vt,
+    block, x, first_t, gain, bias, wq, bq, wk, wv_t, bv, ln, qt, k, kt, v, vt,
     x_other, weights, s_ln, s_qt, s_k, s_kt, s_v, s_vt, pair_sems, out_sems,
 ):
     rows = x.shape[0]
@@ -267,20 +266,22 @@
         if part:
             send.wait_recv()
         spot = pl.multiple_of((core if part == 0 else 1 - core) * rows, rows)
-        normed, _ = row_normalize(source[...].astype(F32))
-        low = (normed * gain_row + bias_row).astype(BF16)
-        s_ln[part] = low
-        product = dot(low, weights[...])
-        queries = (product[:, :heads] + bq_row).astype(BF16).astype(F32) * HEAD_DIM ** (-0.5)
-        s_qt[part] = queries.astype(BF16).T
-        keys = product[:, heads : 2 * heads].astype(BF16)
-        s_k[part] = keys
-        s_kt[part] = keys.T
-        values = (product[:, 2 * heads :] + bv_row).astype(BF16)
-        reused = first_t[:, pl.ds(spot, rows)]
-        s_vt[part, :fresh] = values.T
-        s_vt[part, fresh:] = reused
-        s_v[part] = jnp.concatenate([values, reused.T], axis=1)
+        for first in range(0, rows, block):
+            span = pl.ds(first, block)
+            normed, _ = row_normalize(source[span, :].astype(F32))
+            low = (normed * gain_row + bias_row).astype(BF16)
+            s_ln[part, span] = low
+            product = dot(low, weights[...])
+            queries = (product[:, :heads] + bq_row).astype(BF16).astype(F32) * HEAD_DIM ** (-0.5)
+            s_qt[part, :, span] = queries.astype(BF16).T
+            keys = product[:, heads : 2 * heads].astype(BF16)
+            s_k[part, span] = keys
+            s_kt[part, :, span] = keys.T
+            values = (product[:, 2 * heads :] + bv_row).astype(BF16)
+            reused = first_t[:, pl.ds(pl.multiple_of(spot + first, block), block)]
+            s_vt[part, :fresh, span] = values.T
+            s_vt[part, fresh:, span] = reused
+            s_v[part, span] = jnp.concatenate([values, reused.T], axis=1)
         targets = (
             (s_ln, ln.at[pl.ds(spot, rows), :]),
             (s_qt, qt.at[:, pl.ds(spot, rows)]),
@@ -298,7 +299,7 @@
         copy.wait()
 
 
-def project(x, first_t, gain, bias, wq, bq, wk, wv_t, bv):
+def project(x, first_t, gain, bias, wq, bq, wk, wv_t, bv, block=256):
     rows, width = x.shape
     heads = wq.shape[1]
     tall, flat = (rows, heads), (heads, rows)
@@ -309,7 +310,7 @@
     scratch = [(rows, width), (width, 2 * heads + wv_t.shape[0])]
     scratch += [(2,) + s for s in ((rows, width), flat, tall, flat, tall, flat)]
     return pl.pallas_call(
-        project_kernel,
+        functools.partial(project_kernel, block),
         out_shape=[jax.ShapeDtypeStruct(s, BF16) for s in shapes],
         in_specs=[vmem] * 9,
         out_specs=[pl.BlockSpec(memory_space=pl.ANY)] * 6,
@@ -327,79 +328,82 @@
     return keys <= lax.broadcasted_iota(jnp.int32, (size, size), 1)
 
 
-def query_blocks(tokens, block, two_docs, body):
+def attend_kernel(block, ahead, split, qt, k, vt, attended, lse, sums, k_aug, q_aug):
+    width, tokens = qt.shape
     half = tokens // 2
-    for start in range(0, tokens, block):
-        if start < half:
-            body(start, 0)
-        else:
-
-            @pl.when(two_docs)
-            def _():
-                body(start, half)
-
-            @pl.when(jnp.logical_not(two_docs))
-            def _():
-                body(start, 0)
-
-
-def attend_kernel(block, split, qt, k, vt, attended, lse, sums):
+    pair_width = 2 * HEAD_DIM
+    far = jnp.where(split[0] < tokens, -1e9, 0.0)
+    row = lax.broadcasted_iota(jnp.int32, (HEAD_DIM, tokens), 0)
+    token = lax.broadcasted_iota(jnp.int32, (HEAD_DIM, tokens), 1)
+    far_rows = jnp.where((row == 0) & (token >= half), far, 0.0).astype(BF16)
+    lane = lax.broadcasted_iota(jnp.int32, (tokens, pair_width), 1)
+    key = lax.broadcasted_iota(jnp.int32, (tokens, pair_width), 0)
+    first_half = jnp.where((lax.rem(lane, HEAD_DIM) == 0) & (key < half), 1.0, 0.0).astype(BF16)
+    ones = (lax.broadcasted_iota(jnp.int32, (16, tokens), 0) == 0).astype(BF16)
+    for j in range(2):
+        sums[j, HEAD_DIM:, :] = ones
+        extra = HEAD_DIM * (1 - j)
+        q_aug[j, extra : extra + HEAD_DIM, :] = far_rows
+
+    def pair_step(pair, _):
+        col = pl.multiple_of(pair * pair_width, pair_width)
+        head_rows = [pl.ds(pl.multiple_of(col + HEAD_DIM * j, HEAD_DIM), HEAD_DIM) for j in range(2)]
+        keys = k[:, pl.ds(col, pair_width)]
+        for j in range(2):
+            base = HEAD_DIM * j
+            sums[j, :HEAD_DIM, :] = vt[head_rows[j], :]
+            k_aug[j] = jnp.where(lane // HEAD_DIM == j, keys, first_half)
+            q_aug[j, base : base + HEAD_DIM, :] = qt[head_rows[j], :]
+
+        def products(number, j):
+            start, stop = number * block, (number + 1) * block
+            return dot(k_aug[j, :stop, :], q_aug[j, :, start:stop])
+
+        def average(number, j, scores):
+            start, stop = number * block, (number + 1) * block
+            edge = jnp.where(causal(block), scores[start:], -1e30)
+            top = jnp.max(edge, axis=0, keepdims=True)
+            if start:
+                near = scores[:start]
+                top = jnp.maximum(top, jnp.max(near, axis=0, keepdims=True))
+                weights = jnp.concatenate(
+                    [jnp.exp(near - top).astype(BF16), jnp.exp(edge - top).astype(BF16)], axis=0
+                )
+            else:
+                weights = jnp.exp(edge - top).astype(BF16)
+            total = dot(sums[j, :, :stop], weights)
+            denominator = total[HEAD_DIM : HEAD_DIM + 1]
+            attended[head_rows[j], start:stop] = (total[:HEAD_DIM] * (1.0 / denominator)).astype(BF16)
+            lse[pl.ds(pair * 2 + j, 1), :, start:stop] = (top + jnp.log(denominator))[None]
+
+        units = [(number, j) for number in range(tokens // block) for j in range(2)]
+        queue = [products(*unit) for unit in units[:ahead]]
+        for i, unit in enumerate(units):
+            if i + ahead < len(units):
+                queue.append(products(*units[i + ahead]))
+            average(*unit, queue.pop(0))
+        return 0
+
+    lax.fori_loop(0, width // pair_width, pair_step, 0)
+
+
+def attend(split, qt, k, vt, block=256, ahead=4):
     width, tokens = qt.shape
-    two_docs = split[0] < tokens
-    ones = (lax.broadcasted_iota(jnp.int32, (16, tokens), 0) == 0).astype(BF16)
-    sums[0, HEAD_DIM:, :] = ones
-    sums[1, HEAD_DIM:, :] = ones
-
-    def pair_step(pair, _):
-        col = pl.multiple_of(pair * 2 * HEAD_DIM, 2 * HEAD_DIM)
-        sums[0, :HEAD_DIM, :] = vt[pl.ds(col, HEAD_DIM), :]
-        sums[1, :HEAD_DIM, :] = vt[pl.ds(col + HEAD_DIM, HEAD_DIM), :]
-        owner = lax.broadcasted_iota(jnp.int32, (2 * HEAD_DIM, block), 0) // HEAD_DIM
-
-        def body(start, low):
-            stop = start + block
-            inner = start - low
-            queries = qt[pl.ds(col, 2 * HEAD_DIM), start:stop]
-            keys = k[low:stop, pl.ds(col, 2 * HEAD_DIM)]
-            scores = [
-                dot(keys, jnp.where(owner == j, queries, jnp.zeros_like(queries))) for j in range(2)
-            ]
-            for j in range(2):
-                edge = jnp.where(causal(block), scores[j][inner:], -1e30)
-                top = jnp.max(edge, axis=0, keepdims=True)
-                if inner:
-                    near = scores[j][:inner]
-                    top = jnp.maximum(top, jnp.max(near, axis=0, keepdims=True))
-                    weights = jnp.concatenate(
-                        [jnp.exp(near - top).astype(BF16), jnp.exp(edge - top).astype(BF16)], axis=0
-                    )
-                else:
-                    weights = jnp.exp(edge - top).astype(BF16)
-                total = dot(sums[j, :, low:stop], weights)
-                denominator = total[HEAD_DIM : HEAD_DIM + 1]
-                attended[pl.ds(col + HEAD_DIM * j, HEAD_DIM), start:stop] = (
-                    total[:HEAD_DIM] * (1.0 / denominator)
-                ).astype(BF16)
-                lse[pl.ds(pair * 2 + j, 1), :, start:stop] = (top + jnp.log(denominator))[None]
-
-        query_blocks(tokens, block, two_docs, body)
-        return 0
-
-    lax.fori_loop(0, width // (2 * HEAD_DIM), pair_step, 0)
-
-
-def attend(split, qt, k, vt, block=512):
-    width, tokens = qt.shape
+    pair_width = 2 * HEAD_DIM
     vmem = pl.BlockSpec(memory_space=pltpu.VMEM)
     return pl.pallas_call(
-        functools.partial(attend_kernel, block),
+        functools.partial(attend_kernel, block, ahead),
         out_shape=(
             jax.ShapeDtypeStruct((width, tokens), BF16),
             jax.ShapeDtypeStruct((width // HEAD_DIM, 1, tokens), F32),
         ),
         in_specs=[pl.BlockSpec(memory_space=pltpu.SMEM), vmem, vmem, vmem],
         out_specs=(vmem, vmem),
-        scratch_shapes=[pltpu.VMEM((2, HEAD_DIM + 16, tokens), BF16)],
+        scratch_shapes=[
+            pltpu.VMEM((2, HEAD_DIM + 16, tokens), BF16),
+            pltpu.VMEM((2, tokens, pair_width), BF16),
+            pltpu.VMEM((2, pair_width, tokens), BF16),
+        ],
         compiler_params=pltpu.CompilerParams(vmem_limit_bytes=VMEM_LIMIT),
         name="attend",
     )(split, qt, k, vt)
@@ -420,11 +424,12 @@
 
 
 def feed_kernel(
-    row_chips, slot_keys, x, cot, attended, wo_own, wo_other, bias_o, gain, bias,
+    row_chips, slot_keys, x_far, cot_far, attended, wo_own_far, wo_other_far, bias_o, gain, bias,
     up_other, up_own, bu_other, bu_own, down_other, down_own, bias_d,
     out, grad_mid, grad_att, state_down, state_up, grad_wo, small,
     att_own, att_other, ln, ln_t, normed, inverse, total, grad_ln, att_stage, stage_down, stage_up,
-    held_down, held_up, move_sems, pair_sems, sum_sems, *slot_refs,
+    held_down, held_up, x, cot, wo_own, wo_other, kept_act, kept_grad,
+    move_sems, load_sems, pair_sems, sum_sems, *slot_refs,
 ):
     state, stage, held = (state_down, state_up), (stage_down, stage_up), (held_down, held_up)
     slots = dict(zip(slot_keys, slot_refs))
@@ -467,16 +472,27 @@
     @pl.when(step == 0)
     def _():
         ready = greet(place)
-        local = pltpu.make_async_copy(attended.at[:, own], att_own, move_sems.at[0])
-        local.start()
+        loads = [
+            pltpu.make_async_copy(source, target, load_sems.at[i])
+            for i, (source, target) in enumerate(
+                (
+                    (attended.at[:, own], att_own), (wo_own_far, wo_own), (x_far, x),
+                    (wo_other_far, wo_other), (cot_far, cot),
+                )
+            )
+        ]
+        for load in loads:
+            load.start()
         ready()
         exchange = to_twin(attended.at[:, theirs], att_other, 0)
         exchange.start()
-        total[...] = x[...].astype(F32) + bias_o[...].astype(F32).reshape(1, -1)
         grad_ln[...] = jnp.zeros_like(grad_ln)
         small[...] = jnp.zeros_like(small)
-        local.wait()
-        total[...] += dot(att_own[...], wo_own[...], TN)
+        for load in loads:
+            load.wait()
+        total[...] = x[...].astype(F32) + (
+            dot(att_own[...], wo_own[...], TN) + bias_o[...].astype(F32).reshape(1, -1)
+        )
         exchange.wait()
         mid = total[...] + dot(att_other[...], wo_other[...], TN)
         total[...] = mid + bias_d[...].astype(F32).reshape(1, -1)
@@ -501,10 +517,6 @@
         sums = jnp.sum(grad_hidden.astype(F32), axis=0, keepdims=True)
         return activated, grad_hidden, grad_down, grad_up, sums
 
-    def row_terms(activated, grad_hidden, up, down):
-        total[...] += dot(activated, down[...])
-        grad_ln[...] += dot(grad_hidden, up[...], NT)
-
     @pl.when(lax.rem(step, 2) == 0)
     def _():
         activated, grad_hidden, grad_down, grad_up, sums = weight_grads(
@@ -515,9 +527,9 @@
         for copy in stage_copies(index):
             copy.start()
         small[pl.ds(ROW_BU_OTHER + index, 1), :chunk] = sums
+        kept_act[...] = activated
+        kept_grad[...] = grad_hidden
         act_at("m", 0)
-        row_terms(activated, grad_hidden, up_other, down_other)
-        act_at("e", 0)
 
     @pl.when(lax.rem(step, 2) == 1)
     def _():
@@ -529,7 +541,8 @@
         small[pl.ds(ROW_BU + index, 1), :chunk] = sums
 
         act_at("m", 1)
-        row_terms(activated, grad_hidden, up_own, down_own)
+        total[...] += dot(kept_act[...], down_other[...]) + dot(activated, down_own[...])
+        grad_ln[...] += dot(kept_grad[...], up_other[...], NT) + dot(grad_hidden, up_own[...], NT)
         act_at("e", 1)
 
     @pl.when(step == 5)
@@ -589,7 +602,8 @@
         up_other, up_own, bu_other, bu_own, down_other, down_own, bias_d,
     )
     specs = [fixed(a.shape) for a in operands]
-    specs[2] = anywhere
+    for i in range(5):
+        specs[i] = anywhere
     specs[8] = specs[9] = up_spec
     specs[12] = specs[13] = down_spec
     results = [
@@ -624,7 +638,14 @@
             pltpu.VMEM((3, width, chunk), BF16),
             pltpu.VMEM((3, chunk, width), BF16),
             pltpu.VMEM((3, width, chunk), BF16),
+            pltpu.VMEM((rows, width), BF16),
+            pltpu.VMEM((rows, width), BF16),
+            pltpu.VMEM((heads, width), BF16),
+            pltpu.VMEM((heads, width), BF16),
+            pltpu.VMEM((rows, chunk), BF16),
+            pltpu.VMEM((rows, chunk), BF16),
             pltpu.SemaphoreType.DMA((7,)),
+            pltpu.SemaphoreType.DMA((5,)),
             pltpu.SemaphoreType.DMA((2, 8)),
             pltpu.SemaphoreType.DMA((3, 2, 2, 11)),
         ]
@@ -652,7 +673,7 @@
     back, dv_first, sums, red_down, red_up, red_wo, red_low, red_v, red_last,
     stack, q_aug, d_aug, k_aug, v_aug, dk_sum, dv_sum, weights, terms_send, terms_got,
     wo_got, held_down, held_up, held_wo, held_low, held_v, held_last, sums_got,
-    qt, k, kt, v, do, attended, lse, ln, x, grad_wo,
+    qt, k, kt, v, do, attended, lse, ln, x,
     move_sems, load_sems, pair_sems, tiny_sems, sum_sems, *slot_refs,
 ):
     state, held = (state_down, state_up), (held_down, held_up)
@@ -719,7 +740,7 @@
                 (k_far, k), (qt_far, qt), (v_far, v), (do_far, do), (attended_far, attended),
                 (lse_far, lse), (kt_far, kt), (wq_far, terms_send.at[:model, :width]),
                 (wk_far, terms_send.at[:model, width:]), (wv_far, weights.at[2 * width :, :]), (ln_far, ln),
-                (grad_wo_far.at[:width, :], grad_wo), (x_far, x),
+                (x_far, x),
             )
         )
     ]
@@ -735,6 +756,9 @@
         copy.wait()
     weights[:width] = terms_send[:model, :width].T
     weights[width : 2 * width] = terms_send[:model, width:].T
+    grad_wo = terms_send.at[:width, :]
+    wo_load = pltpu.make_async_copy(grad_wo_far.at[:width, :], grad_wo, load_sems.at[12])
+    wo_load.start()
     far = jnp.where(split[0] < tokens, -1e9, 0.0)
     token = lax.broadcasted_iota(jnp.int32, (1, tokens), 1)
     far_row = jnp.where(token >= half, far, 0.0)
@@ -774,26 +798,38 @@
             d_aug[j, base : base + HEAD_DIM, :] = grad
             d_aug[j, extra : extra + HEAD_DIM, :] = extra_rows(-inner, 0.0)
 
-        for number in range(tokens // block):
-            start = number * block
-            stop = start + block
-            for j in range(2):
-                scores = dot(k_aug[j, :stop, :], q_aug[j, :, start:stop])
-                grad_probs = dot(v_aug[j, :stop, :], d_aug[j, :, start:stop])
-                probs = jnp.where(causal(block), jnp.exp(scores[start:]), 0.0)
-                if start:
-                    probs = jnp.concatenate([jnp.exp(scores[:start]), probs], axis=0)
-                grad_scores = (probs * grad_probs).astype(BF16)
-                probs = probs.astype(BF16)
-                rows = head_rows[j]
-                stack[rows, start:stop] = (
-                    dot(kt[rows, :stop], grad_scores) * HEAD_DIM ** (-0.5)
-                ).astype(BF16)
-                dv_sum[j, :, :stop] += dot(do[rows, start:stop], probs, NT)
-                dk_sum[j, :, :stop] += dot(qt[rows, start:stop], grad_scores, NT)
-            for p in range(width // pair_width):
-                if number < tokens // block - 1 and (p, number) in BACK_PLAN:
-                    pl.when(pair == p)(functools.partial(act, (p, number)))
+        def products(number, j):
+            start, stop = number * block, (number + 1) * block
+            return (
+                dot(k_aug[j, :stop, :], q_aug[j, :, start:stop]),
+                dot(v_aug[j, :stop, :], d_aug[j, :, start:stop]),
+            )
+
+        def gradients(number, j, scores, grad_probs):
+            start, stop = number * block, (number + 1) * block
+            probs = jnp.where(causal(block), jnp.exp(scores[start:]), 0.0)
+            if start:
+                probs = jnp.concatenate([jnp.exp(scores[:start]), probs], axis=0)
+            grad_scores = (probs * grad_probs).astype(BF16)
+            probs = probs.astype(BF16)
+            rows = head_rows[j]
+            stack[rows, start:stop] = (
+                dot(kt[rows, :stop], grad_scores) * HEAD_DIM ** (-0.5)
+            ).astype(BF16)
+            dv_sum[j, :, :stop] += dot(do[rows, start:stop], probs, NT)
+            dk_sum[j, :, :stop] += dot(qt[rows, start:stop], grad_scores, NT)
+
+        units = [(number, j) for number in range(tokens // block) for j in range(2)]
+        ahead = products(*units[0])
+        for i, unit in enumerate(units):
+            now = ahead
+            if i + 1 < len(units):
+                ahead = products(*units[i + 1])
+            gradients(*unit, *now)
+            if unit[1] and i + 1 < len(units):
+                for p in range(width // pair_width):
+                    if (p, unit[0]) in BACK_PLAN:
+                        pl.when(pair == p)(functools.partial(act, (p, unit[0])))
 
         for j in range(2):
             stack[pl.ds(pl.multiple_of(width + col + HEAD_DIM * j, HEAD_DIM), HEAD_DIM), :] = dk_sum[
@@ -805,6 +841,7 @@
             stack[2 * width : 2 * width + HEAD_DIM, :] = dv_sum[0].astype(BF16)
             stack[2 * width + HEAD_DIM : 2 * width + 2 * HEAD_DIM, :] = dv_sum[1].astype(BF16)
             wo_exchange.wait()
+            wo_load.wait()
             summed = (grad_wo[...].astype(F32) + wo_got[...].astype(F32)).astype(BF16)
             by_columns(held_wo, 0, summed)
             for i in range(3):
@@ -813,7 +850,7 @@
                     width + i * pair_width,
                     weight_rows(slice(i * width, i * width + pair_width)),
                 )
-            act((0, 3))
+            act((0, tokens // block - 1))
 
         @pl.when(pair == 1)
         def _():
@@ -828,7 +865,7 @@
             held_v[...] = jnp.zeros_like(held_v)
             for j in range(2):
                 held_v[HEAD_DIM * j : HEAD_DIM * (j + 1), :] = rest[:, j * cols : (j + 1) * cols]
-            act((1, 3))
+            act((1, tokens // block - 1))
 
         @pl.when(pair == 2)
         def _():
@@ -840,7 +877,7 @@
                     i * pair_width,
                     weight_rows(slice(i * width + 2 * pair_width, i * width + 3 * pair_width)),
                 )
-            act((2, 3))
+            act((2, tokens // block - 1))
 
         return 0
 
@@ -899,7 +936,7 @@
 
 def attend_back(
     row_chips, split, gain, small, qt, k, kt, v, do, attended, lse, ln, x, wq, wk, wv_t, grad_wo,
-    state_down, state_up, block=512,
+    state_down, state_up, block=256,
 ):
     width, tokens = qt.shape
     rows, model = x.shape
@@ -947,7 +984,7 @@
         ((6, SUM_ROWS, model), F32),
     ]
     near = (qt, k, kt, v, do, attended, lse, ln, x)
-    scratch += [(a.shape, a.dtype) for a in near] + [((width, model), BF16)]
+    scratch += [(a.shape, a.dtype) for a in near]
     return pl.pallas_call(
         functools.partial(attend_back_kernel, row_chips, block, list(slots)),
         out_shape=[jax.ShapeDtypeStruct(s, t) for s, t, _ in results],
@@ -973,32 +1010,27 @@
 
 
 def finish_kernel(
-    mid, back, dv, sums, down, up, wo, low, thin, last,
+    mid, back, dv, sums, down, up, wo, wo_low, low, thin, last,
     grad_input, grad_first, grad_down, grad_up, grad_wo, grad_q, grad_k, grad_v, bu,
     bias_q, bias_v, gain_two, shift_two, bias_o, bias_d, gain_one, shift_one,
 ):
-    step = pl.program_id(0)
     cols = wo.shape[2]
     pair = 2 * HEAD_DIM
-    grad_input[...] = mid[...] + back[...].astype(F32)
+    grad_input[...] = mid[...] + back[...]
     grad_first[...] = dv[...]
     grad_down[...] = down[0].astype(F32)
     grad_up[...] = up[...].astype(F32)
-
-    @pl.when(step == 0)
+    for j in range(2):
+        grad_wo[:, j * cols : (j + 1) * cols] = wo[j].astype(F32)
+    for i, target in enumerate((grad_q, grad_k)):
+        span = slice(i * pair, (i + 1) * pair)
+        for j, source in enumerate((wo_low[0, span], low[span], last[0, span])):
+            target[:, j * pair : (j + 1) * pair] = source.astype(F32).T
+    grad_v[:pair] = wo_low[0, 2 * pair :].astype(F32)
+    grad_v[pair:] = thin[...].astype(F32)
+
+    @pl.when(pl.program_id(0) == 0)
     def _():
-        heads = grad_wo.shape[0]
-        for j in range(2):
-            span = slice(j * cols, (j + 1) * cols)
-            grad_wo[:, span] = wo[j, :heads].astype(F32)
-            grad_v[:pair, span] = wo[j, heads + 2 * pair :].astype(F32)
-            grad_v[pair:, span] = thin[HEAD_DIM * j : HEAD_DIM * (j + 1)].astype(F32)
-            for i, target in enumerate((grad_q, grad_k)):
-                first = heads + i * pair
-                target[span, :pair] = wo[j, first : first + pair].astype(F32).T
-                target[span, 2 * pair :] = last[j, i * pair : (i + 1) * pair].astype(F32).T
-        for i, target in enumerate((grad_q, grad_k)):
-            target[:, pair : 2 * pair] = low[i * pair : (i + 1) * pair].astype(F32).T
         chunk = bu.shape[0] // 3
         for i in range(3):
             bu[i * chunk : (i + 1) * chunk] = sums[ROW_BU + i, :chunk]
@@ -1014,24 +1046,39 @@
     fresh = heads // 2
     hidden = up.shape[1]
     steps = 6
-    chunk = down.shape[1]
-    half = chunk // 2
+    half = down.shape[1] // 2
+    lanes = width // steps
     out_rows = 192
-    operands = (mid, back, dv, sums, down, up, wo, low, thin, last)
-    once = pl.Buffered(1)
-    fixed = lambda s: pl.BlockSpec(s, lambda i, nd=len(s): (0,) * nd, pipeline_mode=once)
+    operands = (mid, back, dv, sums, down, up, wo, wo, low, thin, last)
+    fixed = lambda s: pl.BlockSpec(s, lambda i, nd=len(s): (0,) * nd)
     by_rows = lambda n, c: pl.BlockSpec((n, c), lambda i: (i, 0))
-    specs = [fixed(a.shape) for a in operands]
-    specs[0] = specs[1] = by_rows(out_rows, width)
-    specs[2] = by_rows(dv.shape[0] // steps, dv.shape[1])
-    specs[4] = pl.BlockSpec((1, half, width), lambda i: (i // 2, lax.rem(i, 2), 0))
-    specs[5] = by_rows(width // steps, hidden)
+    by_lanes = lambda n: pl.BlockSpec((n, lanes), lambda i: (0, i))
+    by_halves = lambda n, k: pl.BlockSpec((1, n, lanes), lambda i: (i // 3, k, lax.rem(i, 3)))
+    moved = [
+        by_rows(out_rows, width),
+        by_rows(dv.shape[0] // steps, dv.shape[1]),
+        by_rows(half, width),
+        by_rows(width // steps, hidden),
+        by_rows(heads // steps, width),
+    ]
+    specs = [
+        moved[0],
+        moved[0],
+        moved[1],
+        fixed(sums.shape),
+        pl.BlockSpec((1, half, width), lambda i: (i // 2, lax.rem(i, 2), 0)),
+        moved[3],
+        pl.BlockSpec((2, heads // steps, wo.shape[2]), lambda i: (0, i, 0)),
+        by_halves(heads, 1),
+        by_lanes(low.shape[0]),
+        pl.BlockSpec((HEAD_DIM, lanes), lambda i: (i // 3, lax.rem(i, 3))),
+        by_halves(last.shape[1], 0),
+    ]
     shapes = [(rows, width), dv.shape, (hidden, width), (width, hidden), (heads, width)]
     shapes += [(width, heads), (width, heads), (fresh, width)]
     shapes += [(hidden,), (heads,), (fresh,)] + [(width,)] * 6
-    out_specs = [fixed(s) for s in shapes]
-    out_specs[0], out_specs[1] = specs[0], specs[2]
-    out_specs[2], out_specs[3] = by_rows(half, width), specs[5]
+    out_specs = moved + [by_rows(lanes, heads)] * 2 + [by_lanes(fresh)]
+    out_specs += [fixed(s) for s in shapes[8:]]
     return pl.pallas_call(
         finish_kernel,
         grid=(steps,),

time: 235 us -> 236 us (level); the launches traced: 230 us -> 234 us
  Pallas kernels: 226 us -> 230 us
    pallas_call x2, Pallas kernels: 25.6 us -> 30.1 us  [the longest x1 19.7 us: attend(): pl.pallas_call(functools.partial(attend_kernel, block, ahead), out_shape=...]
    pallas_call x1, Pallas kernels: 70.5 us -> 73.5 us  [feed(): pl.pallas_call(functools.partial(feed_kernel, row_chips, list(slots)), gr...]
    pallas_call x1, Pallas kernels: 116 us -> 113 us  [attend_back(): pl.pallas_call(functools.partial(attend_back_kernel, row_chips, block, li...]
  transfers between devices with their start and end apart: 4 -> 4, of which waited for: 0 -> 0; matrix products, arithmetic and copies ran while one was open for 0% -> 0% of each run, Pallas kernels for 7% -> 8%
where the time goes in v4:
time: 236 us; the launch traced here: 234 us
  Pallas kernels  230 us (97%)
    pallas_call x1, Pallas kernels, attend_back(): pl.pallas_call(functools.partial(attend_back_kernel, row_chips, block, li...  113 us
    pallas_call x1, Pallas kernels, feed(): pl.pallas_call(functools.partial(feed_kernel, row_chips, list(slots)), gr...  73.5 us
    pallas_call x1, Pallas kernels, attend(): pl.pallas_call(functools.partial(attend_kernel, block, ahead), out_shape=...  19.7 us
    pallas_call x1, Pallas kernels, finish(): pl.pallas_call(finish_kernel, grid=(steps,), in_specs=specs, out_specs=ou...  12.8 us
    pallas_call x1, Pallas kernels, project(): pl.pallas_call(functools.partial(project_kernel, block), out_shape=[jax.S...  10.5 us
  transfers between devices with their start and end apart: 4, of which 0 were waited for; matrix products, arithmetic and copies ran while one was open for 0% of the time, Pallas kernels for 8%

profile of v4, /device:TPU:0, one launch (start us, length us, event | category | flops | bytes accessed | tf_op | source)
XLA Modules:
  0.0 234.3 jit_solution(2457372277744254504)
XLA Ops:
  0.7 0.0 copy-start
  0.7 0.0 copy-start.2
  0.7 0.0 copy-start.4
  0.7 10.5 %project.1 = (bf16[2048,768]{1,0:T(8,128)(2,1)}, bf16[384,2048]{1,0:T(8,128)(2,1)}, bf16[2048,384]{1,0:T(8,128)(2,1)}, bf16[384,2048]{1,0:T(8,128)(2,1)}, bf16[2...) custom-call(bf16[1024,768]{1,0:T(8,128)(2,1)} %x_far.3, bf16[192,2048]{1,0:T(8,128)(2,1)} %bitcast.6, bf16[768]{0:T(1024)(128)(2,1)} %gain.5, ...), custom_call_target="tpu_custom_call" | custom-call | tf_op jit(solution)/shard_map/project/pallas_call | solution.py:312
  11.2 0.0 copy-done
  11.2 0.3 collective-permute-start.1
  11.5 0.2 collective-permute-start.3
  11.7 0.0 copy-done.2
  11.7 0.3 collective-permute-start
  12.0 0.0 copy-done.4
  12.0 0.2 collective-permute-start.2
  12.9 19.7 %attend.1 = (bf16[384,2048]{1,0:T(8,128)(2,1)}, f32[6,1,2048]{2,1,0:T(1,128)}) custom-call(s32[1]{0:T(128)S(6)} %copy.38.split, bf16[384,2048]{1,0:T(8,128)(2,1)} %get-tuple-element.64.qt.qt_far, bf16[2048,384]{1,0:T(8,128)(2,1)} %get-tuple-element.65.k.k_far, bf16[384,2048]{1,0:T(8,128)(2,1)} %get-tuple-element.67.vt), custom_call_target="tpu_custom_call" | custom-call | tf_op jit(solution)/shard_map/attend/pallas_call | solution.py:394
  32.6 0.0 collective-permute-done.2.bu_other
  32.6 0.0 copy-start.5
  32.6 0.0 collective-permute-done.wo_other_far
  32.6 0.0 copy-start.3
  32.6 0.0 collective-permute-done.1.up_other
  32.6 0.0 collective-permute-done.3.down_other
  32.6 0.6 copy-done.5
  33.2 0.2 copy-done.3
  33.4 73.5 %feed.1 = (bf16[1024,768]{1,0:T(8,128)(2,1)}, f32[1024,768]{1,0:T(8,128)}, bf16[384,2048]{1,0:T(8,128)(2,1)}, bf16[3,512,768]{2,1,0:T(8,128)(2,1)}, bf16[3,768,5...) custom-call(bf16[1024,768]{1,0:T(8,128)(2,1)} %x_far.3, bf16[1024,768]{1,0:T(8,128)(2,1)} %cot_far.1, ...), custom_call_target="tpu_custom_call" | custom-call | tf_op jit(solution)/shard_map/feed/pallas_call | solution.py:621
  106.9 113.3 %attend_back.1 = (f32[1024,768]{1,0:T(8,128)}, f32[192,2048]{1,0:T(8,128)}, f32[16,768]{1,0:T(8,128)}, bf16[3,512,768]{2,1,0:T(8,128)(2,1)}, bf16[768,1536]{1,0:...) custom-call(s32[1]{0:T(128)S(6)} %copy.38.split, ...), custom_call_target="tpu_custom_call" | custom-call | tf_op jit(solution)/shard_map/attend_back/pallas_call | solution.py:988
  220.2 0.0 copy-start.1
  220.2 12.8 %finish.1 = (f32[1024,768]{1,0:T(8,128)}, f32[192,2048]{1,0:T(8,128)}, f32[1536,768]{1,0:T(8,128)}, f32[768,1536]{1,0:T(8,128)}, f32[384,768]{1,0:T(8,128)}, /*i...) custom-call(f32[1024,768]{1,0:T(8,128)} %get-tuple-element.74.mid, ...), custom_call_target="tpu_custom_call" | custom-call | tf_op jit(solution)/shard_map/finish/pallas_call | solution.py:1082
  233.0 0.0 copy-done.1
  233.0 1.1 copy.39
Async XLA Ops:
  0.7 10.5 %copy-start = (bf16[768,1536]{1,0:T(8,128)(2,1)S(1)}, bf16[768,1536]{1,0:T(8,128)(2,1)}, u32[]{:S(2)}) copy-start(bf16[768,1536]{1,0:T(8,128)(2,1)} %up_own.1) | copy-start | bytes 7077892
  0.7 11.1 %copy-start.2 = (bf16[384,768]{1,0:T(8,128)(2,1)S(1)}, bf16[384,768]{1,0:T(8,128)(2,1)}, u32[]{:S(2)}) copy-start(bf16[384,768]{1,0:T(8,128)(2,1)} %wo_own_far.1) | copy-start | bytes 1769476
  0.7 11.3 %copy-start.4 = (bf16[1536]{0:T(1024)(128)(2,1)S(1)}, bf16[1536]{0:T(1024)(128)(2,1)}, u32[]{:S(2)}) copy-start(bf16[1536]{0:T(1024)(128)(2,1)} %bu_own.1) | copy-start | bytes 9220
  11.2 21.4 %collective-permute-start.1 = (bf16[768,1536]{1,0:T(8,128)(2,1)S(1)}, bf16[768,1536]{1,0:T(8,128)(2,1)}, u32[]{:S(2)}, u32[]{:S(2)}) collective-permute-start(bf16[768,1536]{1,0:T(8,128)(2,1)S(1)} %copy-done), channel_id=1, source_target_pairs={{0,1},{1,0},{2,3},{3,2},{4,5},{5,4},{6,7},{7,6},{8,9},{9,8},{10,11... | collective-permute-start | bytes 7077896 | tf_op jit(solution)/shard_map/ppermute | solution.py:1094
  11.5 21.1 %collective-permute-start.3 = (bf16[1536,768]{1,0:T(8,128)(2,1)}, bf16[1536,768]{1,0:T(8,128)(2,1)}, u32[]{:S(2)}, u32[]{:S(2)}) collective-permute-start(bf16[1536,768]{1,0:T(8,128)(2,1)} %down_own.1), channel_id=1, source_target_pairs={{0,1},{1,0},{2,3},{3,2},{4,5},{5,4},{6,7},{7,6},{8,9},{9,8},{10,11... | collective-permute-start | bytes 7077896 | tf_op jit(solution)/shard_map/ppermute | solution.py:1094
  11.7 20.8 %collective-permute-start = (bf16[384,768]{1,0:T(8,128)(2,1)S(1)}, bf16[384,768]{1,0:T(8,128)(2,1)S(1)}, u32[]{:S(2)}, u32[]{:S(2)}) collective-permute-start(bf16[384,768]{1,0:T(8,128)(2,1)S(1)} %copy-done.2), channel_id=1, source_target_pairs={{0,1},{1,0},{2,3},{3,2},{4,5},{5,4},{6,7},{7,6},{8,9},{9,8},{10,11... | collective-permute-start | bytes 1769480 | tf_op jit(solution)/shard_map/ppermute | solution.py:1094
  12.0 20.5 %collective-permute-start.2 = (bf16[1536]{0:T(1024)(128)(2,1)S(1)}, bf16[1536]{0:T(1024)(128)(2,1)S(1)}, u32[]{:S(2)}, u32[]{:S(2)}) collective-permute-start(bf16[1536]{0:T(1024)(128)(2,1)S(1)} %copy-done.4), channel_id=1, source_target_pairs={{0,1},{1,0},{2,3},{3,2},{4,5},{5,4},{6,7},{7,6},{8,9},{9,8},{10,11... | collective-permute-start | bytes 9224 | tf_op jit(solution)/shard_map/ppermute | solution.py:1094
  32.6 0.6 copy-start.5
  32.6 0.8 copy-start.3
  220.2 12.8 %copy-start.1 = (bf16[1024,768]{1,0:T(8,128)(2,1)S(1)}, bf16[1024,768]{1,0:T(8,128)(2,1)}, u32[]{:S(2)}) copy-start(bf16[1024,768]{1,0:T(8,128)(2,1)} %get-tuple-element.128) | copy-start | bytes 4718596

commit v5 on v4

--- a/solution.py
+++ b/solution.py
@@ -70,8 +70,20 @@
     def twin(self):
         return (self.index, 1 - self.core)
 
+    def across(self, step_x, step_y, other_core):
+        index = self.index
+        for axis, step, stride in (("x", step_x, 1), ("y", step_y, self.wide)):
+            index = index + (lax.rem(self.at[axis] + step, 2) - self.at[axis]) * stride
+        return (index, 1 - self.core if other_core else self.core)
+
+    def block(self):
+        places = [(0, 1), (1, 0), (1, 1)]
+        return [self.across(*p, False) for p in places] + [
+            self.across(*p, True) for p in [(0, 0)] + places
+        ]
+
     def others(self):
-        return [self.twin()] + [self.peer(a, k)[1] for a in AXES for k in range(1, SIZE[a])]
+        return self.block() + [self.peer("z", k)[1] for k in range(1, SIZE["z"])]
 
 
 def greet(place):
@@ -139,12 +151,12 @@
         span = self.span(stage + 1)
         base = self.first_sem(True, stage)
         copies = []
-        origin = self.result if source is None else source
+        origin = self.result.at[span, :] if source is None else source
         for step in range(1, SIZE[axis]):
             _, device = self.place.peer(axis, step)
             copies.append(
                 pltpu.make_async_remote_copy(
-                    src_ref=origin.at[span, :],
+                    src_ref=origin,
                     dst_ref=self.result.at[span, :],
                     send_sem=self.sems.at[0, base + step - 1],
                     recv_sem=self.sems.at[1, base + step - 1],
@@ -154,9 +166,7 @@
             )
         if source is not None:
             copies.append(
-                pltpu.make_async_copy(
-                    source.at[span, :], self.result.at[span, :], self.sems.at[0, 10]
-                )
+                pltpu.make_async_copy(source, self.result.at[span, :], self.sems.at[0, 10])
             )
         return copies
 
@@ -185,38 +195,40 @@
 ORDERS = ("xyz", "yxz")
 FEED_PLAN = {
     "s1m": ((0, "sA"),),
-    "s3m": ((0, "fA"), (0, "sB"), (1, "sA"),),
-    "s4m": ((0, "fB"), (0, "sC"),),
-    "s5e": ((1, "fA"), (1, "sB"),),
-    "f_end": ((0, "fC"), (1, "fB"),),
+    "s3q": ((0, "fA"), (0, "sB"),),
+    "s3m": ((1, "sA"),),
+    "s3e": ((0, "fB"), (0, "sC"),),
+    "s5q": ((1, "fA"), (1, "sB"),),
+    "s5m": ((0, "fC"), (0, "sc"), (2, "sA"),),
+    "s5e": ((1, "fB"),),
+    "f_end": ((0, "fc"), (2, "fA"),),
 }
 BACK_PLAN = {
-    (0, 0): ((1, "sC"), (2, "sA"), (0, "sc"),),
-    (0, 7): ((1, "fC"), (2, "fA"), (2, "sB"), (3, "sA"), (1, "sc"),),
-    (1, 5): ((2, "fB"), (0, "fc"), (2, "sC"), (0, "sb"),),
-    (1, 7): ((3, "fA"), (3, "sB"), (4, "sA"),),
-    (2, 0): ((1, "fc"), (1, "sb"),),
-    (2, 2): ((0, "fb"), (0, "sa"),),
-    (2, 4): ((3, "fB"), (3, "sC"),),
-    (2, 6): ((2, "fC"), (4, "fA"), (4, "sB"), (2, "sc"),),
-    (2, 7): ((5, "sA"),),
-    "e1": ((1, "fb"), (3, "fC"), (1, "sa"), (3, "sc"),),
-    "e5": ((0, "fa"), (4, "fB"), (2, "fc"), (4, "sC"), (2, "sb"),),
-    "e6": ((5, "fA"), (5, "sB"),),
-    "w0": ((3, "fc"), (3, "sb"),),
-    "w1": ((4, "fC"), (4, "sc"),),
-    "w2": ((1, "fa"),),
-    "w3": ((2, "fb"), (4, "fc"), (2, "sa"), (4, "sb"),),
-    "w4": ((5, "fB"), (5, "sC"),),
-    "w5": ((3, "fb"), (3, "sa"),),
-    "w6": ((5, "fC"), (5, "sc"),),
-    "w7": ((5, "fc"), (5, "sb"),),
-    "w8": ((2, "fa"),),
-    "w9": ((4, "fb"), (4, "sa"),),
-    "w10": ((3, "fa"),),
-    "w11": ((5, "fb"), (5, "sa"),),
-    "w12": ((4, "fa"),),
-    "w13": ((5, "fa"),),
+    "start": ((1, "sC"), (0, "sb"), (2, "sB"),),
+    (0, 2): ((0, "fb"), (0, "sa"),),
+    (0, 4): ((1, "fC"), (2, "fB"), (1, "sc"), (2, "sC"),),
+    (0, 7): ((0, "fa"), (3, "sA"),),
+    (1, 0): ((1, "fc"), (1, "sb"),),
+    (1, 5): ((3, "fA"), (2, "fC"), (2, "sc"), (3, "sB"),),
+    (1, 6): ((1, "fb"), (1, "sa"),),
+    (1, 7): ((3, "fB"), (3, "sC"), (4, "sA"),),
+    (2, 1): ((2, "fc"), (2, "sb"),),
+    (2, 4): ((1, "fa"),),
+    (2, 5): ((3, "fC"), (3, "sc"),),
+    (2, 6): ((4, "fA"), (4, "sB"),),
+    (2, 7): ((2, "fb"), (4, "fB"), (2, "sa"), (4, "sC"), (5, "sA"),),
+    "e0": ((3, "fc"), (3, "sb"),),
+    "e2": ((4, "fC"), (4, "sc"),),
+    "e3": ((2, "fa"),),
+    "e4": ((4, "fc"), (5, "fA"), (5, "sB"), (4, "sb"),),
+    "e5": ((3, "fb"), (3, "sa"),),
+    "e6": ((5, "fB"), (4, "fb"), (5, "sC"), (4, "sa"),),
+    "w0": ((5, "fC"), (5, "sc"),),
+    "w1": ((3, "fa"),),
+    "w2": ((5, "fc"), (5, "sb"),),
+    "w3": ((4, "fa"),),
+    "w4": ((5, "fb"), (5, "sa"),),
+    "w5": ((5, "fa"),),
 }
 
 
@@ -226,6 +238,10 @@
 
 def progress(batch):
     return sum(1 for i, _ in started(FEED_PLAN) if i == batch)
+
+
+def unfinished():
+    return [i for i in range(3) if progress(i) < 3]
 
 
 def scatter_slots(plan, shapes):
@@ -461,7 +477,8 @@
     def act(point):
         for i, action in FEED_PLAN.get(point, ()):
             for j in range(2):
-                part(i, j).run(action, held[j].at[i] if action[1] == "c" else None)
+                one = part(i, j)
+                one.run(action, one.held.at[one.span(3), :] if action[1] == "c" else None)
 
     def act_at(name, odd):
         for k in range(odd, 6, 2):
@@ -505,13 +522,14 @@
         ln[...] = low
         ln_t[...] = low.T
 
-    def weight_grads(up, bias_up, down):
+    def weight_grads(up, bias_up, down, odd):
         hidden = dot(ln[...], up[...]) + bias_up[
             pl.ds(pl.multiple_of(index * chunk, chunk), chunk)
         ].astype(F32).reshape(1, -1)
         activated, slope = gelu_both(hidden)
         activated = activated.astype(BF16)
         grad_hidden = (dot(cot[...], down[...], NT) * slope).astype(BF16)
+        act_at("q", odd)
         grad_down = dot(activated, cot[...], TN)
         grad_up = dot(ln_t[...], grad_hidden)
         sums = jnp.sum(grad_hidden.astype(F32), axis=0, keepdims=True)
@@ -520,7 +538,7 @@
     @pl.when(lax.rem(step, 2) == 0)
     def _():
         activated, grad_hidden, grad_down, grad_up, sums = weight_grads(
-            up_other, bu_other, down_other
+            up_other, bu_other, down_other, 0
         )
         stage_down[index] = grad_down.astype(BF16)
         stage_up[index] = grad_up.astype(BF16)
@@ -533,7 +551,7 @@
 
     @pl.when(lax.rem(step, 2) == 1)
     def _():
-        activated, grad_hidden, grad_down, grad_up, sums = weight_grads(up_own, bu_own, down_own)
+        activated, grad_hidden, grad_down, grad_up, sums = weight_grads(up_own, bu_own, down_own, 1)
         for copy in stage_copies(index):
             copy.wait()
         held_down[index] = (grad_down + held_down[index].astype(F32)).astype(BF16)
@@ -678,6 +696,9 @@
 ):
     state, held = (state_down, state_up), (held_down, held_up)
     slots = dict(zip(slot_keys, slot_refs))
+    live = unfinished()
+    done = [i for i in range(3) if i not in live]
+    packed = dict(zip([(i, j) for i in done for j in range(2)], slot_refs[len(slot_keys) :]))
     width, tokens = qt.shape
     half = tokens // 2
     fresh, model = wv_far.shape
@@ -696,7 +717,7 @@
     def part(i, j):
         chunk = state_down.shape[1]
         if i < 3:
-            holder = held[j].at[i]
+            holder = held[j].at[live.index(i)] if i in live else None
             result = red_up.at[:, i * chunk : (i + 1) * chunk] if j else red_down.at[i]
         else:
             holder, result = {
@@ -714,22 +735,18 @@
             for j in range(2):
                 one = part(i, j)
                 source = None
-                if action[1] == "c":
-                    source = one.held
-                elif action[1] == "b" and i < 3 and progress(i) == 4:
-                    source = state[j].at[i]
+                if action[1] == "cb"[progress(i) - 3] if i in done else action[1] == "c":
+                    source = packed[i, j] if i in done else one.held.at[one.span(3), :]
                 one.run(action, source)
 
     loads = []
     for i in range(3):
-        if progress(i) < 4:
-            for j in range(2):
-                span = part(i, j).span(progress(i))
-                loads.append(
-                    pltpu.make_async_copy(
-                        state[j].at[i, span, :], held[j].at[i, span, :], move_sems.at[2 * i + j]
-                    )
-                )
+        for j in range(2):
+            span = part(i, j).span(progress(i) if i in live else 6 - progress(i))
+            target = part(i, j).held.at[span, :] if i in live else packed[i, j]
+            loads.append(
+                pltpu.make_async_copy(state[j].at[i, span, :], target, move_sems.at[2 * i + j])
+            )
     ready = greet(place)
     for load in loads:
         load.start()
@@ -766,6 +783,9 @@
     def weight_rows(rows):
         return dot(stack[rows, :], ln[...]).astype(BF16)
 
+    def bias_sums(target, lanes, rows):
+        sums[target : target + 1, lanes] = dot(jnp.ones((8, tokens), BF16), stack[rows, :], NT)[:1]
+
     def by_columns(target, start, values):
         cols = target.shape[2]
         for j in range(2):
@@ -840,6 +860,9 @@
         def _():
             stack[2 * width : 2 * width + HEAD_DIM, :] = dv_sum[0].astype(BF16)
             stack[2 * width + HEAD_DIM : 2 * width + 2 * HEAD_DIM, :] = dv_sum[1].astype(BF16)
+            sums[...] = small[...]
+            bias_sums(ROW_BQ, slice(0, pair_width), slice(0, pair_width))
+            bias_sums(ROW_BV, slice(0, pair_width), slice(2 * width, 2 * width + pair_width))
             wo_exchange.wait()
             wo_load.wait()
             summed = (grad_wo[...].astype(F32) + wo_got[...].astype(F32)).astype(BF16)
@@ -856,6 +879,13 @@
         def _():
             stack[2 * width + 2 * HEAD_DIM :, :] = dv_sum[0].astype(BF16)
             dv_first[:HEAD_DIM, :] = dv_sum[1]
+            bias_sums(
+                ROW_BQ, slice(pair_width, 2 * pair_width), slice(pair_width, 2 * pair_width)
+            )
+            bias_sums(
+                ROW_BV, slice(pair_width, pair_width + HEAD_DIM),
+                slice(2 * width + pair_width, 2 * width + pair_width + HEAD_DIM),
+            )
             for i in range(2):
                 held_low[i * pair_width : (i + 1) * pair_width] = weight_rows(
                     slice(i * width + pair_width, i * width + 2 * pair_width)
@@ -871,6 +901,10 @@
         def _():
             dv_first[HEAD_DIM : 2 * HEAD_DIM, :] = dv_sum[0]
             dv_first[2 * HEAD_DIM :, :] = dv_sum[1]
+            bias_sums(
+                ROW_BQ, slice(2 * pair_width, 3 * pair_width),
+                slice(2 * pair_width, 3 * pair_width),
+            )
             for i in range(2):
                 by_columns(
                     held_last,
@@ -893,44 +927,44 @@
     normed, inverse = row_normalize(x[...].astype(F32))
     terms_exchange.wait()
     grad = back[...] + terms_got[...].astype(F32)
-    sums[...] = small[...]
     sums[4:5, :] = jnp.sum(grad * normed, axis=0, keepdims=True)
     sums[5:6, :] = jnp.sum(grad, axis=0, keepdims=True)
-    biases = dot(jnp.ones((8, tokens), BF16), stack[...], NT)
-    sums[ROW_BQ : ROW_BQ + 1, :width] = biases[:1, :width]
-    sums[ROW_BV : ROW_BV + 1, :fresh] = biases[:1, 2 * width :]
-    tiny = to_twin(sums, sums_got.at[0], 2)
-    tiny.start()
+
+    def spread(devices, first):
+        return [
+            pltpu.make_async_remote_copy(
+                src_ref=sums, dst_ref=sums_got.at[first + i], send_sem=tiny_sems.at[0, first + i],
+                recv_sem=tiny_sems.at[1, first + i], device_id=device, device_id_type=MESH,
+            )
+            for i, device in enumerate(devices)
+        ]
+
+    copies = spread(place.block(), 0)
+    for copy in copies:
+        copy.start()
     act("e3")
     back[...] = row_normalize_back(grad * gain[...].astype(F32).reshape(1, -1), normed, inverse)
-    tiny.wait()
-    sums[:ROW_BU, :] = sums[:ROW_BU, :] + sums_got[0, :ROW_BU, :]
-    sums[ROW_BU:ROW_BU_OTHER, :] = (
-        sums[ROW_BU:ROW_BU_OTHER, :] + sums_got[0, ROW_BU_OTHER:ROW_BQ, :]
-    )
-    slot = 1
-    points = iter(("e4", "e5", "e6"))
-    for axis in AXES:
-        copies = []
-        for step in range(1, SIZE[axis]):
-            _, device = place.peer(axis, step)
-            copies.append(
-                pltpu.make_async_remote_copy(
-                    src_ref=sums, dst_ref=sums_got.at[slot], send_sem=tiny_sems.at[0, slot],
-                    recv_sem=tiny_sems.at[1, slot], device_id=device, device_id_type=MESH,
-                )
-            )
-            copies[-1].start()
-            slot += 1
-        act(next(points))
-        for copy in copies:
-            copy.wait()
-        total = sums[...]
-        for i in range(slot - len(copies), slot):
-            total = total + sums_got[i]
-        sums[...] = total
+    act("e4")
+    for copy in copies:
+        copy.wait()
+    total = sums[...]
+    for i in range(3):
+        total = total + sums_got[i]
+    sums[...] = total
+    for i in range(3, 7):
+        sums[:ROW_BU, :] = sums[:ROW_BU, :] + sums_got[i, :ROW_BU, :]
+        sums[ROW_BU:ROW_BU_OTHER, :] = (
+            sums[ROW_BU:ROW_BU_OTHER, :] + sums_got[i, ROW_BU_OTHER:ROW_BQ, :]
+        )
+    copies = spread([place.peer("z", step)[1] for step in range(1, SIZE["z"])], 7)
+    for copy in copies:
+        copy.start()
+    act("e5")
+    for copy in copies:
+        copy.wait()
+    sums[...] = sums[...] + sums_got[7] + sums_got[8] + sums_got[9]
     for point in BACK_PLAN:
-        if point == "e7" or point[0] == "w":
+        if point == "e6" or point[0] == "w":
             act(point)
 
 
@@ -963,6 +997,7 @@
     shapes[4] = ((low_rows, model), (low_rows, cols))
     shapes[5] = ((low_rows, cols),) * 2
     slots = scatter_slots(BACK_PLAN, shapes)
+    live = unfinished()
     scratch = [
         ((2 * width + fresh, tokens), BF16),
         ((2, pair, tokens), BF16),
@@ -975,13 +1010,13 @@
         ((rows, model), BF16),
         ((rows, model), BF16),
         ((width, model), BF16),
-        ((3, chunk, model), BF16),
-        ((3, model, chunk), BF16),
+        ((max(len(live), 1), chunk, model), BF16),
+        ((max(len(live), 1), model, chunk), BF16),
         ((2, 2 * width, cols), BF16),
         ((low_rows, model), BF16),
         ((low_rows, cols), BF16),
         ((2, low_rows, cols), BF16),
-        ((6, SUM_ROWS, model), F32),
+        ((10, SUM_ROWS, model), F32),
     ]
     near = (qt, k, kt, v, do, attended, lse, ln, x)
     scratch += [(a.shape, a.dtype) for a in near]
@@ -995,10 +1030,16 @@
             pltpu.SemaphoreType.DMA((6,)),
             pltpu.SemaphoreType.DMA((13,)),
             pltpu.SemaphoreType.DMA((2, 3)),
-            pltpu.SemaphoreType.DMA((2, 6)),
+            pltpu.SemaphoreType.DMA((2, 10)),
             pltpu.SemaphoreType.DMA((6, 2, 2, 11)),
         ]
-        + [pltpu.VMEM(shape, BF16) for shape in slots.values()],
+        + [pltpu.VMEM(shape, BF16) for shape in slots.values()]
+        + [
+            pltpu.VMEM((shape[0] // (16 if progress(i) == 3 else 4), shape[1]), BF16)
+            for i in range(3)
+            if i not in live
+            for shape in shapes[i]
+        ],
         compiler_params=pltpu.CompilerParams(
             vmem_limit_bytes=VMEM_LIMIT, collective_id=3, has_side_effects=True
         ),

time: 236 us -> 229 us (0.970)
  Pallas kernels: 230 us -> 223 us
    pallas_call x1, Pallas kernels: 113 us -> 102 us  [attend_back(): pl.pallas_call(functools.partial(attend_back_kernel, row_chips, block, li...]
    pallas_call x1, Pallas kernels: 73.5 us -> 77.7 us  [feed(): pl.pallas_call(functools.partial(feed_kernel, row_chips, list(slots)), gr...]
  transfers between devices with their start and end apart: 4 -> 4, of which waited for: 0 -> 0; matrix products, arithmetic and copies ran while one was open for 0% -> 0% of each run, Pallas kernels for 8% -> 9%
where the time goes in v5:
time: 229 us; the launch traced here: 227 us
  Pallas kernels  223 us (97%)
    pallas_call x1, Pallas kernels, attend_back(): pl.pallas_call(functools.partial(attend_back_kernel, row_chips, block, li...  102 us
    pallas_call x1, Pallas kernels, feed(): pl.pallas_call(functools.partial(feed_kernel, row_chips, list(slots)), gr...  77.7 us
    pallas_call x1, Pallas kernels, attend(): pl.pallas_call(functools.partial(attend_kernel, block, ahead), out_shape=...  19.7 us
    pallas_call x1, Pallas kernels, finish(): pl.pallas_call(finish_kernel, grid=(steps,), in_specs=specs, out_specs=ou...  12.8 us
    pallas_call x1, Pallas kernels, project(): pl.pallas_call(functools.partial(project_kernel, block), out_shape=[jax.S...  10.5 us
  transfers between devices with their start and end apart: 4, of which 0 were waited for; matrix products, arithmetic and copies ran while one was open for 0% of the time, Pallas kernels for 9%

profile of v5, /device:TPU:0, one launch (start us, length us, event | category | flops | bytes accessed | tf_op | source)
XLA Modules:
  0.0 227.3 jit_solution(3351866061224092137)
XLA Ops:
  0.7 0.0 copy-start
  0.7 0.0 copy-start.2
  0.7 0.0 copy-start.4
  0.7 10.5 %project.1 = (bf16[2048,768]{1,0:T(8,128)(2,1)}, bf16[384,2048]{1,0:T(8,128)(2,1)}, bf16[2048,384]{1,0:T(8,128)(2,1)}, bf16[384,2048]{1,0:T(8,128)(2,1)}, bf16[2...) custom-call(bf16[1024,768]{1,0:T(8,128)(2,1)} %x_far.3, bf16[192,2048]{1,0:T(8,128)(2,1)} %bitcast.6, bf16[768]{0:T(1024)(128)(2,1)} %gain.5, ...), custom_call_target="tpu_custom_call" | custom-call | tf_op jit(solution)/shard_map/project/pallas_call | solution.py:328
  11.2 0.0 copy-done
  11.2 0.3 collective-permute-start.1
  11.5 0.2 collective-permute-start.3
  11.7 0.0 copy-done.2
  11.7 0.3 collective-permute-start
  12.0 0.0 copy-done.4
  12.0 0.2 collective-permute-start.2
  12.9 19.7 %attend.1 = (bf16[384,2048]{1,0:T(8,128)(2,1)}, f32[6,1,2048]{2,1,0:T(1,128)}) custom-call(s32[1]{0:T(128)S(6)} %copy.38.split, bf16[384,2048]{1,0:T(8,128)(2,1)} %get-tuple-element.64.qt.qt_far, bf16[2048,384]{1,0:T(8,128)(2,1)} %get-tuple-element.65.k.k_far, bf16[384,2048]{1,0:T(8,128)(2,1)} %get-tuple-element.67.vt), custom_call_target="tpu_custom_call" | custom-call | tf_op jit(solution)/shard_map/attend/pallas_call | solution.py:410
  32.6 0.0 collective-permute-done.2.bu_other
  32.6 0.0 copy-start.5
  32.6 0.0 collective-permute-done.wo_other_far
  32.6 0.0 copy-start.3
  32.6 0.0 collective-permute-done.1.up_other
  32.6 0.0 collective-permute-done.3.down_other
  32.6 0.6 copy-done.5
  33.2 0.2 copy-done.3
  33.4 77.7 %feed.1 = (bf16[1024,768]{1,0:T(8,128)(2,1)}, f32[1024,768]{1,0:T(8,128)}, bf16[384,2048]{1,0:T(8,128)(2,1)}, bf16[3,512,768]{2,1,0:T(8,128)(2,1)}, bf16[3,768,5...) custom-call(bf16[1024,768]{1,0:T(8,128)(2,1)} %x_far.3, bf16[1024,768]{1,0:T(8,128)(2,1)} %cot_far.1, ...), custom_call_target="tpu_custom_call" | custom-call | tf_op jit(solution)/shard_map/feed/pallas_call | solution.py:639
  111.1 102.0 %attend_back.1 = (f32[1024,768]{1,0:T(8,128)}, f32[192,2048]{1,0:T(8,128)}, f32[16,768]{1,0:T(8,128)}, bf16[3,512,768]{2,1,0:T(8,128)(2,1)}, bf16[768,1536]{1,0:...) custom-call(s32[1]{0:T(128)S(6)} %copy.38.split, ...), custom_call_target="tpu_custom_call" | custom-call | tf_op jit(solution)/shard_map/attend_back/pallas_call | solution.py:1023
  213.1 0.0 copy-start.1
  213.1 12.8 %finish.1 = (f32[1024,768]{1,0:T(8,128)}, f32[192,2048]{1,0:T(8,128)}, f32[1536,768]{1,0:T(8,128)}, f32[768,1536]{1,0:T(8,128)}, f32[384,768]{1,0:T(8,128)}, /*i...) custom-call(f32[1024,768]{1,0:T(8,128)} %get-tuple-element.74.mid, ...), custom_call_target="tpu_custom_call" | custom-call | tf_op jit(solution)/shard_map/finish/pallas_call | solution.py:1123
  225.9 0.0 copy-done.1
  225.9 1.1 copy.39
Async XLA Ops:
  0.7 10.5 %copy-start = (bf16[768,1536]{1,0:T(8,128)(2,1)S(1)}, bf16[768,1536]{1,0:T(8,128)(2,1)}, u32[]{:S(2)}) copy-start(bf16[768,1536]{1,0:T(8,128)(2,1)} %up_own.1) | copy-start | bytes 7077892
  0.7 11.1 %copy-start.2 = (bf16[384,768]{1,0:T(8,128)(2,1)S(1)}, bf16[384,768]{1,0:T(8,128)(2,1)}, u32[]{:S(2)}) copy-start(bf16[384,768]{1,0:T(8,128)(2,1)} %wo_own_far.1) | copy-start | bytes 1769476
  0.7 11.3 %copy-start.4 = (bf16[1536]{0:T(1024)(128)(2,1)S(1)}, bf16[1536]{0:T(1024)(128)(2,1)}, u32[]{:S(2)}) copy-start(bf16[1536]{0:T(1024)(128)(2,1)} %bu_own.1) | copy-start | bytes 9220
  11.2 21.4 %collective-permute-start.1 = (bf16[768,1536]{1,0:T(8,128)(2,1)S(1)}, bf16[768,1536]{1,0:T(8,128)(2,1)}, u32[]{:S(2)}, u32[]{:S(2)}) collective-permute-start(bf16[768,1536]{1,0:T(8,128)(2,1)S(1)} %copy-done), channel_id=1, source_target_pairs={{0,1},{1,0},{2,3},{3,2},{4,5},{5,4},{6,7},{7,6},{8,9},{9,8},{10,11... | collective-permute-start | bytes 7077896 | tf_op jit(solution)/shard_map/ppermute | solution.py:1135
  11.5 21.1 %collective-permute-start.3 = (bf16[1536,768]{1,0:T(8,128)(2,1)}, bf16[1536,768]{1,0:T(8,128)(2,1)}, u32[]{:S(2)}, u32[]{:S(2)}) collective-permute-start(bf16[1536,768]{1,0:T(8,128)(2,1)} %down_own.1), channel_id=1, source_target_pairs={{0,1},{1,0},{2,3},{3,2},{4,5},{5,4},{6,7},{7,6},{8,9},{9,8},{10,11... | collective-permute-start | bytes 7077896 | tf_op jit(solution)/shard_map/ppermute | solution.py:1135
  11.7 20.8 %collective-permute-start = (bf16[384,768]{1,0:T(8,128)(2,1)S(1)}, bf16[384,768]{1,0:T(8,128)(2,1)S(1)}, u32[]{:S(2)}, u32[]{:S(2)}) collective-permute-start(bf16[384,768]{1,0:T(8,128)(2,1)S(1)} %copy-done.2), channel_id=1, source_target_pairs={{0,1},{1,0},{2,3},{3,2},{4,5},{5,4},{6,7},{7,6},{8,9},{9,8},{10,11... | collective-permute-start | bytes 1769480 | tf_op jit(solution)/shard_map/ppermute | solution.py:1135
  12.0 20.5 %collective-permute-start.2 = (bf16[1536]{0:T(1024)(128)(2,1)S(1)}, bf16[1536]{0:T(1024)(128)(2,1)S(1)}, u32[]{:S(2)}, u32[]{:S(2)}) collective-permute-start(bf16[1536]{0:T(1024)(128)(2,1)S(1)} %copy-done.4), channel_id=1, source_target_pairs={{0,1},{1,0},{2,3},{3,2},{4,5},{5,4},{6,7},{7,6},{8,9},{9,8},{10,11... | collective-permute-start | bytes 9224 | tf_op jit(solution)/shard_map/ppermute | solution.py:1135
  32.6 0.6 copy-start.5
  32.6 0.8 copy-start.3
  213.1 12.8 %copy-start.1 = (bf16[1024,768]{1,0:T(8,128)(2,1)S(1)}, bf16[1024,768]{1,0:T(8,128)(2,1)}, u32[]{:S(2)}) copy-start(bf16[1024,768]{1,0:T(8,128)(2,1)} %get-tuple-element.128) | copy-start | bytes 4718596

commit v6 on v5

--- a/solution.py
+++ b/solution.py
@@ -204,31 +204,29 @@
     "f_end": ((0, "fc"), (2, "fA"),),
 }
 BACK_PLAN = {
-    "start": ((1, "sC"), (0, "sb"), (2, "sB"),),
-    (0, 2): ((0, "fb"), (0, "sa"),),
-    (0, 4): ((1, "fC"), (2, "fB"), (1, "sc"), (2, "sC"),),
+    "start": ((0, "sb"), (1, "sC"), (2, "sB"),),
+    (0, 3): ((0, "fb"), (0, "sa"),),
+    (0, 5): ((1, "fC"), (2, "fB"), (1, "sc"), (2, "sC"),),
     (0, 7): ((0, "fa"), (3, "sA"),),
     (1, 0): ((1, "fc"), (1, "sb"),),
-    (1, 5): ((3, "fA"), (2, "fC"), (2, "sc"), (3, "sB"),),
-    (1, 6): ((1, "fb"), (1, "sa"),),
-    (1, 7): ((3, "fB"), (3, "sC"), (4, "sA"),),
-    (2, 1): ((2, "fc"), (2, "sb"),),
-    (2, 4): ((1, "fa"),),
-    (2, 5): ((3, "fC"), (3, "sc"),),
-    (2, 6): ((4, "fA"), (4, "sB"),),
-    (2, 7): ((2, "fb"), (4, "fB"), (2, "sa"), (4, "sC"), (5, "sA"),),
-    "e0": ((3, "fc"), (3, "sb"),),
-    "e2": ((4, "fC"), (4, "sc"),),
-    "e3": ((2, "fa"),),
-    "e4": ((4, "fc"), (5, "fA"), (5, "sB"), (4, "sb"),),
-    "e5": ((3, "fb"), (3, "sa"),),
-    "e6": ((5, "fB"), (4, "fb"), (5, "sC"), (4, "sa"),),
-    "w0": ((5, "fC"), (5, "sc"),),
-    "w1": ((3, "fa"),),
-    "w2": ((5, "fc"), (5, "sb"),),
-    "w3": ((4, "fa"),),
-    "w4": ((5, "fb"), (5, "sa"),),
-    "w5": ((5, "fa"),),
+    (1, 4): ((3, "fA"), (3, "sB"),),
+    (1, 5): ((2, "fC"), (1, "fb"), (1, "sa"), (2, "sc"),),
+    (1, 6): ((3, "fB"), (3, "sC"),),
+    (1, 7): ((4, "sA"),),
+    (2, 0): ((2, "fc"), (2, "sb"),),
+    (2, 1): ((1, "fa"),),
+    (2, 4): ((4, "fA"), (3, "fC"), (3, "sc"), (4, "sB"),),
+    (2, 5): ((2, "fb"), (2, "sa"),),
+    (2, 6): ((4, "fB"), (4, "sC"),),
+    (2, 7): ((3, "fc"), (5, "sA"), (3, "sb"),),
+    "e0": ((4, "fC"), (4, "sc"),),
+    "e1": ((2, "fa"), (5, "fA"), (4, "fc"), (5, "sB"), (4, "sb"),),
+    "e2": ((3, "fb"), (5, "fB"), (3, "sa"), (5, "sC"),),
+    "e3": ((4, "fb"), (5, "fC"), (5, "sc"), (4, "sa"),),
+    "e5": ((5, "fc"), (3, "fa"), (5, "sb"),),
+    "e6": ((4, "fa"),),
+    "w0": ((5, "fb"), (5, "sa"),),
+    "w1": ((5, "fa"),),
 }
 
 
@@ -315,7 +313,7 @@
         copy.wait()
 
 
-def project(x, first_t, gain, bias, wq, bq, wk, wv_t, bv, block=256):
+def project(x, first_t, gain, bias, wq, bq, wk, wv_t, bv, block=1024):
     rows, width = x.shape
     heads = wq.shape[1]
     tall, flat = (rows, heads), (heads, rows)
@@ -750,18 +748,35 @@
     ready = greet(place)
     for load in loads:
         load.start()
+    pairs = width // pair_width
+
+    def pair_loads(pair):
+        lanes = pl.ds(pl.multiple_of(pair * pair_width, pair_width), pair_width)
+        heads = pl.ds(pair * 2, 2)
+        moves = [(far.at[:, lanes], near.at[:, lanes]) for far, near in ((k_far, k), (v_far, v))]
+        moves += [
+            (far.at[lanes, :], near.at[lanes, :])
+            for far, near in ((qt_far, qt), (kt_far, kt), (do_far, do), (attended_far, attended))
+        ]
+        moves.append((lse_far.at[heads], lse.at[heads]))
+        return [
+            pltpu.make_async_copy(far, near, load_sems.at[pair, i])
+            for i, (far, near) in enumerate(moves)
+        ]
+
     arriving = [
-        pltpu.make_async_copy(far, near, load_sems.at[i])
+        pltpu.make_async_copy(far, near, load_sems.at[pairs, i])
         for i, (far, near) in enumerate(
             (
-                (k_far, k), (qt_far, qt), (v_far, v), (do_far, do), (attended_far, attended),
-                (lse_far, lse), (kt_far, kt), (wq_far, terms_send.at[:model, :width]),
-                (wk_far, terms_send.at[:model, width:]), (wv_far, weights.at[2 * width :, :]), (ln_far, ln),
+                (grad_wo_far.at[:width, : model // 2], held_wo.at[0, :width, :]),
+                (grad_wo_far.at[:width, model // 2 :], held_wo.at[1, :width, :]),
+                (ln_far, ln), (wq_far, terms_send.at[:model, :width]),
+                (wk_far, terms_send.at[:model, width:]), (wv_far, weights.at[2 * width :, :]),
                 (x_far, x),
             )
         )
     ]
-    for copy in arriving:
+    for copy in pair_loads(0):
         copy.start()
     ready()
     wo_exchange = to_twin(grad_wo_far.at[width:, :], wo_got, 0)
@@ -769,13 +784,13 @@
     for load in loads:
         load.wait()
     act("start")
-    for copy in arriving:
-        copy.wait()
-    weights[:width] = terms_send[:model, :width].T
-    weights[width : 2 * width] = terms_send[:model, width:].T
-    grad_wo = terms_send.at[:width, :]
-    wo_load = pltpu.make_async_copy(grad_wo_far.at[:width, :], grad_wo, load_sems.at[12])
-    wo_load.start()
+    for copy in arriving[:3]:
+        copy.start()
+    for pair in range(1, pairs):
+        for copy in pair_loads(pair):
+            copy.start()
+    for copy in arriving[3:]:
+        copy.start()
     far = jnp.where(split[0] < tokens, -1e9, 0.0)
     token = lax.broadcasted_iota(jnp.int32, (1, tokens), 1)
     far_row = jnp.where(token >= half, far, 0.0)
@@ -792,6 +807,8 @@
             target[j, start : start + values.shape[0], :] = values[:, j * cols : (j + 1) * cols]
 
     def pair_step(pair, _):
+        for copy in pair_loads(pair):
+            copy.wait()
         col = pl.multiple_of(pair * pair_width, pair_width)
         lane = lax.broadcasted_iota(jnp.int32, (tokens, pair_width), 1)
         key = lax.broadcasted_iota(jnp.int32, (tokens, pair_width), 0)
@@ -860,13 +877,12 @@
         def _():
             stack[2 * width : 2 * width + HEAD_DIM, :] = dv_sum[0].astype(BF16)
             stack[2 * width + HEAD_DIM : 2 * width + 2 * HEAD_DIM, :] = dv_sum[1].astype(BF16)
-            sums[...] = small[...]
-            bias_sums(ROW_BQ, slice(0, pair_width), slice(0, pair_width))
-            bias_sums(ROW_BV, slice(0, pair_width), slice(2 * width, 2 * width + pair_width))
             wo_exchange.wait()
-            wo_load.wait()
-            summed = (grad_wo[...].astype(F32) + wo_got[...].astype(F32)).astype(BF16)
-            by_columns(held_wo, 0, summed)
+            for copy in arriving[:3]:
+                copy.wait()
+            for j in range(2):
+                got = wo_got[:, j * (model // 2) : (j + 1) * (model // 2)].astype(F32)
+                held_wo[j, :width, :] = (held_wo[j, :width, :].astype(F32) + got).astype(BF16)
             for i in range(3):
                 by_columns(
                     held_wo,
@@ -874,18 +890,14 @@
                     weight_rows(slice(i * width, i * width + pair_width)),
                 )
             act((0, tokens // block - 1))
+            sums[...] = small[...]
+            bias_sums(ROW_BQ, slice(0, pair_width), slice(0, pair_width))
+            bias_sums(ROW_BV, slice(0, pair_width), slice(2 * width, 2 * width + pair_width))
 
         @pl.when(pair == 1)
         def _():
             stack[2 * width + 2 * HEAD_DIM :, :] = dv_sum[0].astype(BF16)
             dv_first[:HEAD_DIM, :] = dv_sum[1]
-            bias_sums(
-                ROW_BQ, slice(pair_width, 2 * pair_width), slice(pair_width, 2 * pair_width)
-            )
-            bias_sums(
-                ROW_BV, slice(pair_width, pair_width + HEAD_DIM),
-                slice(2 * width + pair_width, 2 * width + pair_width + HEAD_DIM),
-            )
             for i in range(2):
                 held_low[i * pair_width : (i + 1) * pair_width] = weight_rows(
                     slice(i * width + pair_width, i * width + 2 * pair_width)
@@ -896,15 +908,18 @@
             for j in range(2):
                 held_v[HEAD_DIM * j : HEAD_DIM * (j + 1), :] = rest[:, j * cols : (j + 1) * cols]
             act((1, tokens // block - 1))
+            bias_sums(
+                ROW_BQ, slice(pair_width, 2 * pair_width), slice(pair_width, 2 * pair_width)
+            )
+            bias_sums(
+                ROW_BV, slice(pair_width, pair_width + HEAD_DIM),
+                slice(2 * width + pair_width, 2 * width + pair_width + HEAD_DIM),
+            )
 
         @pl.when(pair == 2)
         def _():
             dv_first[HEAD_DIM : 2 * HEAD_DIM, :] = dv_sum[0]
             dv_first[2 * HEAD_DIM :, :] = dv_sum[1]
-            bias_sums(
-                ROW_BQ, slice(2 * pair_width, 3 * pair_width),
-                slice(2 * pair_width, 3 * pair_width),
-            )
             for i in range(2):
                 by_columns(
                     held_last,
@@ -912,12 +927,20 @@
                     weight_rows(slice(i * width + 2 * pair_width, i * width + 3 * pair_width)),
                 )
             act((2, tokens // block - 1))
+            bias_sums(
+                ROW_BQ, slice(2 * pair_width, 3 * pair_width),
+                slice(2 * pair_width, 3 * pair_width),
+            )
 
         return 0
 
     lax.fori_loop(0, width // pair_width, pair_step, 0)
 
     act("e0")
+    for copy in arriving[3:]:
+        copy.wait()
+    weights[:width] = terms_send[:model, :width].T
+    weights[width : 2 * width] = terms_send[:model, width:].T
     terms_send[...] = dot(stack[:, theirs], weights[...], TN).astype(BF16)
     terms_exchange = to_twin(terms_send, terms_got, 1)
     terms_exchange.start()
@@ -1028,7 +1051,7 @@
         scratch_shapes=[pltpu.VMEM(s, t) for s, t in scratch]
         + [
             pltpu.SemaphoreType.DMA((6,)),
-            pltpu.SemaphoreType.DMA((13,)),
+            pltpu.SemaphoreType.DMA((4, 7)),
             pltpu.SemaphoreType.DMA((2, 3)),
             pltpu.SemaphoreType.DMA((2, 10)),
             pltpu.SemaphoreType.DMA((6, 2, 2, 11)),

time: 229 us -> 223 us (0.974)
  Pallas kernels: 223 us -> 217 us
    pallas_call x1, Pallas kernels: 102 us -> 96.6 us  [attend_back(): pl.pallas_call(functools.partial(attend_back_kernel, row_chips, block, li...]
where the time goes in v6:
time: 223 us; the launch traced here: 221 us
  Pallas kernels  217 us (97%)
    pallas_call x1, Pallas kernels, attend_back(): pl.pallas_call(functools.partial(attend_back_kernel, row_chips, block, li...  96.6 us
    pallas_call x1, Pallas kernels, feed(): pl.pallas_call(functools.partial(feed_kernel, row_chips, list(slots)), gr...  77.7 us
    pallas_call x1, Pallas kernels, attend(): pl.pallas_call(functools.partial(attend_kernel, block, ahead), out_shape=...  19.7 us
    pallas_call x1, Pallas kernels, finish(): pl.pallas_call(finish_kernel, grid=(steps,), in_specs=specs, out_specs=ou...  12.8 us
    pallas_call x1, Pallas kernels, project(): pl.pallas_call(functools.partial(project_kernel, block), out_shape=[jax.S...  10.1 us
  transfers between devices with their start and end apart: 4, of which 0 were waited for; matrix products, arithmetic and copies ran while one was open for 0% of the time, Pallas kernels for 9%

profile of v6, /device:TPU:0, one launch (start us, length us, event | category | flops | bytes accessed | tf_op | source)
XLA Modules:
  0.0 221.5 jit_solution(12955060069728757435)
XLA Ops:
  0.7 0.0 copy-start
  0.7 0.0 copy-start.2
  0.7 0.0 copy-start.4
  0.7 10.1 %project.1 = (bf16[2048,768]{1,0:T(8,128)(2,1)}, bf16[384,2048]{1,0:T(8,128)(2,1)}, bf16[2048,384]{1,0:T(8,128)(2,1)}, bf16[384,2048]{1,0:T(8,128)(2,1)}, bf16[2...) custom-call(bf16[1024,768]{1,0:T(8,128)(2,1)} %x_far.3, bf16[192,2048]{1,0:T(8,128)(2,1)} %bitcast.6, bf16[768]{0:T(1024)(128)(2,1)} %gain.5, ...), custom_call_target="tpu_custom_call" | custom-call | tf_op jit(solution)/shard_map/project/pallas_call | solution.py:326
  10.8 0.0 copy-done
  10.8 0.4 collective-permute-start.1
  11.2 0.2 collective-permute-start.3
  11.4 0.0 copy-done.2
  11.4 0.3 collective-permute-start
  11.7 0.0 copy-done.4
  11.7 0.2 collective-permute-start.2
  12.5 19.7 %attend.1 = (bf16[384,2048]{1,0:T(8,128)(2,1)}, f32[6,1,2048]{2,1,0:T(1,128)}) custom-call(s32[1]{0:T(128)S(6)} %copy.38.split, bf16[384,2048]{1,0:T(8,128)(2,1)} %get-tuple-element.64.qt.qt_far, bf16[2048,384]{1,0:T(8,128)(2,1)} %get-tuple-element.65.k.k_far, bf16[384,2048]{1,0:T(8,128)(2,1)} %get-tuple-element.67.vt), custom_call_target="tpu_custom_call" | custom-call | tf_op jit(solution)/shard_map/attend/pallas_call | solution.py:408
  32.2 0.0 collective-permute-done.2.bu_other
  32.2 0.0 copy-start.5
  32.2 0.0 collective-permute-done.wo_other_far
  32.2 0.0 copy-start.3
  32.2 0.0 collective-permute-done.1.up_other
  32.2 0.0 collective-permute-done.3.down_other
  32.2 0.6 copy-done.5
  32.8 0.2 copy-done.3
  33.0 77.7 %feed.1 = (bf16[1024,768]{1,0:T(8,128)(2,1)}, f32[1024,768]{1,0:T(8,128)}, bf16[384,2048]{1,0:T(8,128)(2,1)}, bf16[3,512,768]{2,1,0:T(8,128)(2,1)}, bf16[3,768,5...) custom-call(bf16[1024,768]{1,0:T(8,128)(2,1)} %x_far.3, bf16[1024,768]{1,0:T(8,128)(2,1)} %cot_far.1, ...), custom_call_target="tpu_custom_call" | custom-call | tf_op jit(solution)/shard_map/feed/pallas_call | solution.py:637
  110.7 96.6 %attend_back.1 = (f32[1024,768]{1,0:T(8,128)}, f32[192,2048]{1,0:T(8,128)}, f32[16,768]{1,0:T(8,128)}, bf16[3,512,768]{2,1,0:T(8,128)(2,1)}, bf16[768,1536]{1,0:...) custom-call(s32[1]{0:T(128)S(6)} %copy.38.split, ...), custom_call_target="tpu_custom_call" | custom-call | tf_op jit(solution)/shard_map/attend_back/pallas_call | solution.py:1046
  207.3 0.0 copy-start.1
  207.3 12.8 %finish.1 = (f32[1024,768]{1,0:T(8,128)}, f32[192,2048]{1,0:T(8,128)}, f32[1536,768]{1,0:T(8,128)}, f32[768,1536]{1,0:T(8,128)}, f32[384,768]{1,0:T(8,128)}, /*i...) custom-call(f32[1024,768]{1,0:T(8,128)} %get-tuple-element.74.mid, ...), custom_call_target="tpu_custom_call" | custom-call | tf_op jit(solution)/shard_map/finish/pallas_call | solution.py:1146
  220.1 0.0 copy-done.1
  220.1 1.1 copy.39
Async XLA Ops:
  0.7 10.1 %copy-start = (bf16[768,1536]{1,0:T(8,128)(2,1)S(1)}, bf16[768,1536]{1,0:T(8,128)(2,1)}, u32[]{:S(2)}) copy-start(bf16[768,1536]{1,0:T(8,128)(2,1)} %up_own.1) | copy-start | bytes 7077892
  0.7 10.7 %copy-start.2 = (bf16[384,768]{1,0:T(8,128)(2,1)S(1)}, bf16[384,768]{1,0:T(8,128)(2,1)}, u32[]{:S(2)}) copy-start(bf16[384,768]{1,0:T(8,128)(2,1)} %wo_own_far.1) | copy-start | bytes 1769476
  0.7 11.0 %copy-start.4 = (bf16[1536]{0:T(1024)(128)(2,1)S(1)}, bf16[1536]{0:T(1024)(128)(2,1)}, u32[]{:S(2)}) copy-start(bf16[1536]{0:T(1024)(128)(2,1)} %bu_own.1) | copy-start | bytes 9220
  10.8 21.4 %collective-permute-start.1 = (bf16[768,1536]{1,0:T(8,128)(2,1)S(1)}, bf16[768,1536]{1,0:T(8,128)(2,1)}, u32[]{:S(2)}, u32[]{:S(2)}) collective-permute-start(bf16[768,1536]{1,0:T(8,128)(2,1)S(1)} %copy-done), channel_id=1, source_target_pairs={{0,1},{1,0},{2,3},{3,2},{4,5},{5,4},{6,7},{7,6},{8,9},{9,8},{10,11... | collective-permute-start | bytes 7077896 | tf_op jit(solution)/shard_map/ppermute | solution.py:1158
  11.2 21.1 %collective-permute-start.3 = (bf16[1536,768]{1,0:T(8,128)(2,1)}, bf16[1536,768]{1,0:T(8,128)(2,1)}, u32[]{:S(2)}, u32[]{:S(2)}) collective-permute-start(bf16[1536,768]{1,0:T(8,128)(2,1)} %down_own.1), channel_id=1, source_target_pairs={{0,1},{1,0},{2,3},{3,2},{4,5},{5,4},{6,7},{7,6},{8,9},{9,8},{10,11... | collective-permute-start | bytes 7077896 | tf_op jit(solution)/shard_map/ppermute | solution.py:1158
  11.4 20.8 %collective-permute-start = (bf16[384,768]{1,0:T(8,128)(2,1)S(1)}, bf16[384,768]{1,0:T(8,128)(2,1)S(1)}, u32[]{:S(2)}, u32[]{:S(2)}) collective-permute-start(bf16[384,768]{1,0:T(8,128)(2,1)S(1)} %copy-done.2), channel_id=1, source_target_pairs={{0,1},{1,0},{2,3},{3,2},{4,5},{5,4},{6,7},{7,6},{8,9},{9,8},{10,11... | collective-permute-start | bytes 1769480 | tf_op jit(solution)/shard_map/ppermute | solution.py:1158
  11.7 20.5 %collective-permute-start.2 = (bf16[1536]{0:T(1024)(128)(2,1)S(1)}, bf16[1536]{0:T(1024)(128)(2,1)S(1)}, u32[]{:S(2)}, u32[]{:S(2)}) collective-permute-start(bf16[1536]{0:T(1024)(128)(2,1)S(1)} %copy-done.4), channel_id=1, source_target_pairs={{0,1},{1,0},{2,3},{3,2},{4,5},{5,4},{6,7},{7,6},{8,9},{9,8},{10,11... | collective-permute-start | bytes 9224 | tf_op jit(solution)/shard_map/ppermute | solution.py:1158
  32.2 0.6 copy-start.5
  32.2 0.8 copy-start.3
  207.3 12.8 %copy-start.1 = (bf16[1024,768]{1,0:T(8,128)(2,1)S(1)}, bf16[1024,768]{1,0:T(8,128)(2,1)}, u32[]{:S(2)}) copy-start(bf16[1024,768]{1,0:T(8,128)(2,1)} %get-tuple-element.128) | copy-start | bytes 4718596
